TPU v7x, 32 devices: a whole 2x2x4 slice. The times are simulated.
32 devices in a mesh: elem: 4 (over z), clus: 8 (over y, x, core).
Axes of the slice: x: 2, y: 2, z: 4, core: 2. Of those that a mesh axis runs over, the one named last changes fastest.
Arguments:
- nodal: float32 [512, 8192], P(None, ('elem', 'clus')), may hold values from -6 to 6
- metric: bfloat16 [3, 512, 8192], P(None, None, ('elem', 'clus')), may hold values from 0.25 to 2.5
- derivative: float32 [8, 8], replicated, may hold values from -2 to 2
- interp: float32 [2, 8, 8], replicated, may hold values from -2 to 2
- face_level: int32 [49152], P(('elem', 'clus')), may hold values from 0 to 4
- face_target: int32 [49152], P(('elem', 'clus')), may hold values from 0 to 895, as said below
- slot_mortar: int32 [12288], P(('elem', 'clus')), may hold values from 0 to 511
- vertex_ids: int32 [8, 8192], P(None, ('elem', 'clus')), may hold values from 0 to 1023, as said below
Outputs:
- applied: float32 [512, 8192], P(None, ('elem', 'clus'))
Inputs may be any that keep to these rules, and one draw needn't show every extreme that they name: `face_target`: No two faces of one device name the same slot, and on some device every slot is named. `vertex_ids`: the coarse vertices of the elements on elem index e lie in e * 256 to e * 256 + 2 * 256 - 1, taken modulo 1024.
All inputs are finite; a program needn't handle non-finite values.
Results may differ from a plain program's by a relative error of at most 0.0003.
Values sent between devices are 32-bit elements; how exact they have to be, the bound alone decides.
No kernel may reach another device: no remote copies, remote signals or barrier semaphores. Data moves between devices by JAX's collectives and lax.ppermute only.
A program may use at most 64 MiB of HBM per device.

v0:
```python
import jax
import jax.numpy as jnp
from jax import lax
from jax.sharding import PartitionSpec as P

POINTS = 8
CAP_E = 128
CAP_C = 16
M_DEV = 512
NV_DEV = 256


highest = lax.Precision.HIGHEST


def extended(array, sides, width):
    for axis, dim in sides:
        peers, length = (lax.axis_size(axis), array.shape[dim])
        up = [(i, (i + 1) % peers) for i in range(peers)]
        down = [(j, i) for i, j in up]
        last = lax.slice_in_dim(array, length - width, length, axis=dim)
        initial = lax.slice_in_dim(array, 0, width, axis=dim)
        before = lax.ppermute(last, axis, up)
        after = lax.ppermute(initial, axis, down)
        array = jnp.concatenate([before, array, after], axis=dim)
    return array


def face_traces(nodal_block, points):
    element_cube = nodal_block.reshape(points, points, points, -1)
    far_index = points - 1
    slab_list = [
        element_cube[0],
        element_cube[far_index],
        element_cube[:, 0],
        element_cube[:, far_index],
        element_cube[:, :, 0],
        element_cube[:, :, far_index],
    ]
    return jnp.concatenate(slab_list, axis=2)


def face_maps(interp, face_level, points):
    identity = jnp.eye(points, dtype=jnp.float32)[:, :, None]
    first_one = interp[0][:, :, None]
    second_one = interp[1][:, :, None]
    level_row = face_level[None, None, :]
    left_map = jnp.where(level_row == 0, identity, jnp.where(level_row <= 2, first_one, second_one))
    right_map = jnp.where(
        level_row == 0, identity, jnp.where(level_row % 2 == 1, first_one, second_one)
    )
    return (left_map, right_map)


def project_traces(traces, left_map, right_map):
    partial_rows = jnp.einsum("xaf,abf->xbf", left_map, traces, precision=highest)
    return jnp.einsum("ybf,xbf->xyf", right_map, partial_rows, precision=highest)


def back_project(values, left_map, right_map):
    partial_rows = jnp.einsum("xaf,xyf->ayf", left_map, values, precision=highest)
    return jnp.einsum("ybf,ayf->abf", right_map, partial_rows, precision=highest)


def stiffness_apply(nodal_block, metric_block, derivative, points):
    element_cube = nodal_block.reshape(points, points, points, -1)
    metric_cube = metric_block.astype(jnp.float32).reshape(3, points, points, points, -1)
    grad_first = jnp.einsum("ai,ijke->ajke", derivative, element_cube, precision=highest)
    grad_second = jnp.einsum("bj,ijke->ibke", derivative, element_cube, precision=highest)
    grad_third = jnp.einsum("ck,ijke->ijce", derivative, element_cube, precision=highest)
    result = jnp.einsum("ai,ajke->ijke", derivative, metric_cube[0] * grad_first, precision=highest)
    result = result + jnp.einsum(
        "bj,ibke->ijke", derivative, metric_cube[1] * grad_second, precision=highest
    )
    result = result + jnp.einsum(
        "ck,ijce->ijke", derivative, metric_cube[2] * grad_third, precision=highest
    )
    return result


def corner_values(nodal_block, points):
    element_cube = nodal_block.reshape(points, points, points, -1)
    far_index = points - 1
    return jnp.stack(
        [
            element_cube[
                corner // 4 * far_index, corner // 2 % 2 * far_index, corner % 2 * far_index
            ]
            for corner in range(8)
        ]
    )


def finish_block(result_cube, back_faces, corner_fix, points):
    far_index = points - 1
    count_elems = result_cube.shape[-1]
    face_parts = back_faces.reshape(points, points, 6, count_elems)
    result_cube = result_cube.at[0].add(face_parts[:, :, 0])
    result_cube = result_cube.at[far_index].add(face_parts[:, :, 1])
    result_cube = result_cube.at[:, 0].add(face_parts[:, :, 2])
    result_cube = result_cube.at[:, far_index].add(face_parts[:, :, 3])
    result_cube = result_cube.at[:, :, 0].add(face_parts[:, :, 4])
    result_cube = result_cube.at[:, :, far_index].add(face_parts[:, :, 5])
    for corner in range(8):
        result_cube = result_cube.at[
            corner // 4 * far_index, corner // 2 % 2 * far_index, corner % 2 * far_index
        ].add(corner_fix[corner])
    return result_cube.reshape(points**3, count_elems)


def curve_swap(pair):
    return extended(pair, (("elem", 0),), 1)


def group_swap(columns):
    return lax.all_to_all(columns, "clus", split_axis=1, concat_axis=1, tiled=True)


def coarse_correction(nodal, vertex_ids, points):
    corner_vals = corner_values(nodal, points).reshape(-1)
    total_vertices = NV_DEV * lax.axis_size("elem")
    window_ids = jnp.mod(vertex_ids - lax.axis_index("elem") * NV_DEV, total_vertices)
    flat_ids = window_ids.reshape(-1)
    totals = jnp.zeros((2 * NV_DEV,), jnp.float32).at[flat_ids].add(corner_vals)
    counts = (
        jnp.zeros((2 * NV_DEV,), jnp.float32)
        .at[flat_ids]
        .add(jnp.ones(flat_ids.shape, jnp.float32))
    )
    totals, counts = lax.psum((totals, counts), "clus")
    stacked = jnp.stack([totals.reshape(2, NV_DEV), counts.reshape(2, NV_DEV)], axis=1)
    widened = extended(stacked, (("elem", 0),), 1)
    window = jnp.concatenate([widened[0] + widened[1], widened[2] + widened[3]], axis=1)
    coarse = window[0] / (1.0 + window[1])
    return coarse[window_ids]


def on_device(nodal, metric, derivative, interp, face_level, face_target, slot_mortar, vertex_ids):
    points = POINTS
    width_sq = points * points
    group_size = lax.axis_size("clus")
    slot_count = 2 * CAP_E + group_size * CAP_C
    left_map, right_map = face_maps(interp, face_level, points)
    projected = project_traces(face_traces(nodal, points), left_map, right_map)
    outgoing = (
        jnp.zeros((width_sq, M_DEV + slot_count), jnp.float32)
        .at[:, face_target]
        .add(projected.reshape(width_sq, -1))
    )
    edge_pair = jnp.stack(
        [outgoing[:, M_DEV : M_DEV + CAP_E], outgoing[:, M_DEV + CAP_E : M_DEV + 2 * CAP_E]]
    )
    arrived_pair = curve_swap(edge_pair)
    arrived_group = group_swap(outgoing[:, M_DEV + 2 * CAP_E :])
    incoming = jnp.concatenate([arrived_pair[0], arrived_pair[3], arrived_group], axis=1)
    mortar = outgoing[:, :M_DEV].at[:, slot_mortar].add(incoming)
    answers = mortar[:, slot_mortar]
    answer_pair = curve_swap(jnp.stack([answers[:, :CAP_E], answers[:, CAP_E : 2 * CAP_E]]))
    answer_group = group_swap(answers[:, 2 * CAP_E :])
    returned = jnp.concatenate([mortar, answer_pair[0], answer_pair[3], answer_group], axis=1)
    picked = returned[:, face_target].reshape(points, points, -1)
    back_faces = back_project(picked, left_map, right_map)
    result_cube = stiffness_apply(nodal, metric, derivative, points)
    corner_fix = coarse_correction(nodal, vertex_ids, points)
    return finish_block(result_cube, back_faces, corner_fix, points)


def solution(mesh):
    in_specs = (
        P(None, ("elem", "clus")),
        P(None, None, ("elem", "clus")),
        P(),
        P(),
        P(("elem", "clus")),
        P(("elem", "clus")),
        P(("elem", "clus")),
        P(None, ("elem", "clus")),
    )
    out_specs = P(None, ("elem", "clus"))
    return jax.shard_map(
        on_device, mesh=mesh, in_specs=in_specs, out_specs=out_specs, check_vma=False
    )
```

profile of v0, /device:TPU:0, one launch (start us, length us, event | category | flops | bytes accessed | tf_op | source)
XLA Modules:
  0.0 208.4 jit_solution(5818145792768646223)
XLA Ops:
  1.7 1.3 fusion.76
  4.8 4.0 %copy.56 = f32[8,8,1536]{0,1,2:T(8,128)} copy(f32[8,8,1536]{2,1,0:T(8,128)S(1)} %bitcast_dynamic-update-slice_fusion) | data formatting | bytes 786432 | tf_op jit(solution)/shard_map/concatenate | solution.py:40
  8.9 20.6 %fusion.5 = f32[1536,8,8]{1,2,0:T(8,128)S(1)} fusion(f32[8,8,1536]{0,1,2:T(8,128)} %copy.56, f32[8,8]{0,1:T(8,128)S(1)} %copy.37, f32[8,8]{0,1:T(8,128)S(1)} %copy.36, f32[8,8]{0,1:T(8,128)S(1)} %fusion.64, pred[1536]{0:T(1024)(128)(4,1)S(1)} %get-tuple-element.212, pred[1536]{0:T(1024)(128)(4,1)S(1)} %get-tuple-element.213), kind=kOutput, calls=%fused_computation.14 | convolution fusion | flops 9633792 | bytes 790272 | tf_op jit(solution)/shard_map/xaf,abf->xbf/dot_general | solution.py:56
  29.5 18.5 %fusion.26 = f32[8,8,1536]{1,0,2:T(8,128)} fusion(f32[8,8]{0,1:T(8,128)S(1)} %copy.37, f32[8,8]{0,1:T(8,128)S(1)} %copy.36, f32[8,8]{0,1:T(8,128)S(1)} %fusion.64, pred[1536]{0:T(1024)(128)(4,1)S(1)} %get-tuple-element.214, pred[1536]{0:T(1024)(128)(4,1)S(1)} %get-tuple-element.213, f32[1536,8,8]{1,2,0:T(8,128)S(1)} %fusion.5), kind=kOutput, calls=%fused_computation.35 | convolution fusion | flops 9633792 | bytes 790272 | tf_op jit(solution)/shard_map/ybf,xbf->xyf/dot_general | solution.py:57
  48.0 4.4 %copy.39 = f32[8,8,1536]{2,1,0:T(8,128)S(1)} copy(f32[8,8,1536]{1,0,2:T(8,128)} %fusion.26) | data formatting | bytes 786432 | tf_op jit(solution)/shard_map/ybf,xbf->xyf/transpose | solution.py:57
  52.8 8.9 %scatter_custom_fusion = f32[64,896]{0,1:T(8,128)S(1)} fusion(s32[1536]{0:T(1024)S(1)} %compare_select_fusion.2, f32[1536,64]{1,0:T(8,128)S(1)} %copy.40, f32[]{:T(128)} %constant.457.clone.1), kind=kCustom, calls=%fused_computation.48 | custom fusion | flops 98304 | bytes 229380 | tf_op jit(solution)/shard_map/scatter-add | solution.py:148
  62.4 5.2 %all-to-all-start = ((f32[8,1,1024]{2,1,0:T(1,128)}), f32[8,1,1024]{2,1,0:T(1,128)S(1)}, u32[]{:S(2)}, u32[]{:S(2)}) async-start(f32[8,1,1024]{2,1,0:T(1,128)} %reshape.681), calls=%async_computation | async-start | bytes 65536 | tf_op jit(solution)/shard_map/all_to_all | solution.py:116
  67.6 1.6 collective-permute-start
  69.1 2.3 %collective-permute-start.1 = (f32[1,64,128]{1,2,0:T(8,128)S(1)}, f32[1,64,128]{1,2,0:T(8,128)S(1)}, u32[]{:S(2)}, u32[]{:S(2)}) collective-permute-start(f32[1,64,128]{1,2,0:T(8,128)S(1)} %get-tuple-element.192), channel_id=1, source_target_pairs={{8,0},{16,8},{24,16},{0,24},{9,1},{17,9},{25,17},{1,25},{10,2},{18... | collective-permute-start | bytes 98312 | tf_op jit(solution)/shard_map/ppermute | solution.py:24
  71.5 14.7 %scatter_custom_fusion.2 = f32[512]{0:T(512)S(1)} fusion(s32[2048]{0:T(1024)S(1)} %bitcast.206, f32[2048]{0:T(1024)S(1)} %bitcast.205, f32[]{:T(128)} %constant.457.clone.1), kind=kCustom, calls=%fused_computation.145 | custom fusion | flops 2048 | bytes 2052 | tf_op jit(solution)/shard_map/scatter-add | solution.py:124
  86.2 14.7 %scatter_custom_fusion.3 = f32[512]{0:T(512)S(1)} fusion(s32[2048]{0:T(1024)S(1)} %bitcast.207, f32[2048]{0:T(1024)S(1)} %broadcast.286, f32[]{:T(128)} %constant.457.clone.1), kind=kCustom, calls=%fused_computation.143 | custom fusion | flops 2048 | bytes 2052 | tf_op jit(solution)/shard_map/scatter-add | solution.py:128
  100.9 13.9 %all-reduce = (f32[2,1,256]{2,1,0:T(1,128)S(1)}, f32[2,1,256]{2,1,0:T(1,128)S(1)}) all-reduce(f32[2,1,256]{2,1,0:T(1,128)S(1)} %bitcast.203, f32[2,1,256]{2,1,0:T(1,128)S(1)} %bitcast.204), channel_id=1, replica_groups=mesh['elem'=4,'clus'=8] {'clus'}, use_global_device_ids=true, to_apply=%region_3.4 | all-reduce | flops 1024 | bytes 8192 | tf_op jit(solution)/shard_map/psum | solution.py:130
  114.8 1.8 collective-permute-start.5
  122.0 5.1 %collective-permute-done.4 = f32[1,2,256]{2,1,0:T(2,128)S(1)} collective-permute-done((f32[1,2,256]{2,1,0:T(2,128)S(1)}, f32[1,2,256]{2,1,0:T(2,128)S(1)}, u32[]{:S(2)}, u32[]{:S(2)}) %collective-permute-start.4) | collective-permute-done | bytes 2080 | tf_op jit(solution)/shard_map/ppermute | solution.py:23
  127.1 13.2 %gather_fusion.2 = f32[2048]{0:T(1024)S(1)} fusion(f32[512]{0:T(512)S(1)} %bitcast.176, s32[2048]{0:T(1024)S(1)} %broadcast_clamp_fusion), kind=kCustom, calls=%fused_computation.2 | custom fusion | bytes 24576 | tf_op jit(solution)/shard_map/gather | solution.py:135
  141.7 2.8 %scatter_custom_fusion.1 = f32[64,512]{0,1:T(8,128)S(1)} fusion(f32[64,512]{0,1:T(8,128)S(1)} %slice-done, s32[384]{0:T(512)S(1)} %compare_select_fusion.3, f32[64,128]{0,1:T(8,128)S(1)} %bitcast.193, f32[]{:T(128)} %constant.469, f32[64,128]{0,1:T(8,128)S(1)} %bitcast.199, f32[64,128]{0,1:T(8,128)S(1)} %bitcast.198), kind=kCustom, calls=%fused_computation.51 | custom fusion | flops 73728 | bytes 327684 | tf_op jit(solution)/shard_map/scatter-add | solution.py:156
  146.3 3.3 %all-to-all-start.1 = ((f32[8,1,1024]{2,1,0:T(1,128)}), f32[8,1,1024]{2,1,0:T(1,128)S(1)}, u32[]{:S(2)}, u32[]{:S(2)}) async-start(f32[8,1,1024]{2,1,0:T(1,128)} %reshape.683), calls=%async_computation.1 | async-start | bytes 65536 | tf_op jit(solution)/shard_map/all_to_all | solution.py:116
  149.7 3.8 %collective-permute-start.3 = (f32[1,64,128]{1,2,0:T(8,128)S(1)}, f32[1,64,128]{1,2,0:T(8,128)S(1)}, u32[]{:S(2)}, u32[]{:S(2)}) collective-permute-start(f32[1,64,128]{1,2,0:T(8,128)S(1)} %get-tuple-element.200), channel_id=1, source_target_pairs={{8,0},{16,8},{24,16},{0,24},{9,1},{17,9},{25,17},{1,25},{10,2},{18... | collective-permute-start | bytes 98312 | tf_op jit(solution)/shard_map/ppermute | solution.py:24
  155.2 1.2 collective-permute-done.2
  156.5 2.6 %gather_fusion.1 = f32[1536,64]{1,0:T(8,128)S(1)} fusion(f32[64,896]{0,1:T(8,128)S(1)} %pad_maximum_fusion, s32[2048]{0:T(1024)S(1)} %pad_clamp_fusion), kind=kCustom, calls=%fused_computation.1 | custom fusion | bytes 792576 | tf_op jit(solution)/shard_map/gather | solution.py:161
  159.3 4.0 %copy.58 = f32[8,8,1536]{0,1,2:T(8,128)} copy(f32[8,8,1536]{2,1,0:T(8,128)S(1)} %bitcast.190) | data formatting | bytes 786432 | tf_op jit(solution)/shard_map/reshape | solution.py:161
  163.3 18.7 %fusion.4 = f32[1536,8,8]{1,2,0:T(8,128)S(1)} fusion(f32[8,8,1536]{0,1,2:T(8,128)} %copy.58, f32[8,8]{0,1:T(8,128)S(1)} %copy.37, f32[8,8]{0,1:T(8,128)S(1)} %copy.36, f32[8,8]{0,1:T(8,128)S(1)} %fusion.64, pred[1536]{0:T(1024)(128)(4,1)S(1)} %get-tuple-element.212, pred[1536]{0:T(1024)(128)(4,1)S(1)} %get-tuple-element.213), kind=kOutput, calls=%fused_computation.13 | convolution fusion | flops 9633792 | bytes 790272 | tf_op jit(solution)/shard_map/xaf,xyf->ayf/dot_general | solution.py:61
  182.0 18.6 %fusion.29 = f32[8,8,1536]{0,1,2:T(8,128)} fusion(f32[8,8]{0,1:T(8,128)S(1)} %copy.37, f32[8,8]{0,1:T(8,128)S(1)} %copy.36, f32[8,8]{0,1:T(8,128)S(1)} %fusion.64, pred[1536]{0:T(1024)(128)(4,1)S(1)} %get-tuple-element.214, pred[1536]{0:T(1024)(128)(4,1)S(1)} %get-tuple-element.213, f32[1536,8,8]{1,2,0:T(8,128)S(1)} %fusion.4), kind=kOutput, calls=%fused_computation.36 | convolution fusion | flops 9633792 | bytes 790272 | tf_op jit(solution)/shard_map/ybf,ayf->abf/dot_general | solution.py:62
  200.6 4.4 %copy.42 = f32[8,8,1536]{2,1,0:T(8,128)S(1)} copy(f32[8,8,1536]{0,1,2:T(8,128)} %fusion.29) | data formatting | bytes 786432 | tf_op jit(solution)/shard_map/ybf,ayf->abf/transpose | solution.py:62
  (103 shorter events, 18.5 us)
Async XLA Ops:
  0.0 116.8 %copy-start = (f32[8,8]{1,0:T(8,128)S(1)}, f32[8,8]{1,0:T(8,128)}, u32[]{:S(2)}) copy-start(f32[8,8]{1,0:T(8,128)} %param.38) | copy-start | bytes 772
  0.0 8.7 %copy-start.5 = (s32[1536]{0:T(1024)S(1)}, s32[1536]{0:T(1024)}, u32[]{:S(2)}) copy-start(s32[1536]{0:T(1024)} %param.40) | copy-start | bytes 18436
  0.0 8.7 %copy-start.6 = (f32[2,8,8]{2,1,0:T(8,128)S(1)}, f32[2,8,8]{2,1,0:T(8,128)}, u32[]{:S(2)}) copy-start(f32[2,8,8]{2,1,0:T(8,128)} %param.39) | copy-start | bytes 1540
  48.0 4.8 %copy-start.7 = (s32[1536]{0:T(1024)S(1)}, s32[1536]{0:T(1024)}, u32[]{:S(2)}) copy-start(s32[1536]{0:T(1024)} %param.41) | copy-start | bytes 18436
  48.0 23.4 %copy-start.1 = (f32[512,256]{1,0:T(8,128)S(1)}, f32[512,256]{1,0:T(8,128)}, u32[]{:S(2)}) copy-start(f32[512,256]{1,0:T(8,128)} %param.36) | copy-start | bytes 1572868
  48.0 23.5 %copy-start.4 = (s32[8,256]{1,0:T(8,128)S(1)}, s32[8,256]{1,0:T(8,128)}, u32[]{:S(2)}) copy-start(s32[8,256]{1,0:T(8,128)} %param.43) | copy-start | bytes 24580
  48.0 68.6 %copy-start.8 = (s32[384]{0:T(512)S(1)}, s32[384]{0:T(512)}, u32[]{:S(2)}) copy-start(s32[384]{0:T(512)} %param.42) | copy-start | bytes 4612
  48.0 68.6 %copy-start.3 = (bf16[3,512,256]{2,1,0:T(8,128)(2,1)S(1)}, bf16[3,512,256]{2,1,0:T(8,128)(2,1)}, u32[]{:S(2)}) copy-start(bf16[3,512,256]{2,1,0:T(8,128)(2,1)} %param.37) | copy-start | bytes 2359300
  61.6 60.4 %copy-start.2 = (f32[64,896]{0,1:T(8,128)}, f32[64,896]{0,1:T(8,128)S(1)}, u32[]{:S(2)}) copy-start(f32[64,896]{0,1:T(8,128)S(1)} %scatter_custom_fusion) | copy-start | bytes 688132
  62.4 77.9 %all-to-all-start = ((f32[8,1,1024]{2,1,0:T(1,128)}), f32[8,1,1024]{2,1,0:T(1,128)S(1)}, u32[]{:S(2)}, u32[]{:S(2)}) async-start(f32[8,1,1024]{2,1,0:T(1,128)} %reshape.681), calls=%async_computation | async-start | bytes 65536 | tf_op jit(solution)/shard_map/all_to_all | solution.py:116
  67.6 74.1 %collective-permute-start = (f32[1,64,128]{1,2,0:T(8,128)S(1)}, f32[1,64,128]{1,2,0:T(8,128)S(1)}, u32[]{:S(2)}, u32[]{:S(2)}) collective-permute-start(f32[1,64,128]{1,2,0:T(8,128)S(1)} %get-tuple-element.190), channel_id=1, source_target_pairs={{0,8},{8,16},{16,24},{24,0},{1,9},{9,17},{17,25},{25,1},{2,10},{10... | collective-permute-start | bytes 98312 | tf_op jit(solution)/shard_map/ppermute | solution.py:23
  69.1 72.5 %collective-permute-start.1 = (f32[1,64,128]{1,2,0:T(8,128)S(1)}, f32[1,64,128]{1,2,0:T(8,128)S(1)}, u32[]{:S(2)}, u32[]{:S(2)}) collective-permute-start(f32[1,64,128]{1,2,0:T(8,128)S(1)} %get-tuple-element.192), channel_id=1, source_target_pairs={{8,0},{16,8},{24,16},{0,24},{9,1},{17,9},{25,17},{1,25},{10,2},{18... | collective-permute-start | bytes 98312 | tf_op jit(solution)/shard_map/ppermute | solution.py:24
  114.8 6.8 %collective-permute-start.5 = (f32[1,2,256]{2,1,0:T(2,128)S(1)}, f32[1,2,256]{2,1,0:T(2,128)S(1)}, u32[]{:S(2)}, u32[]{:S(2)}) collective-permute-start(f32[1,2,256]{2,1,0:T(2,128)S(1)} %pad_maximum_fusion.2), channel_id=1, source_target_pairs={{8,0},{16,8},{24,16},{0,24},{9,1},{17,9},{25,17},{1,25},{10,2},{18... | collective-permute-start | bytes 6152 | tf_op jit(solution)/shard_map/ppermute | solution.py:24
  121.7 5.4 %collective-permute-start.4 = (f32[1,2,256]{2,1,0:T(2,128)S(1)}, f32[1,2,256]{2,1,0:T(2,128)S(1)}, u32[]{:S(2)}, u32[]{:S(2)}) collective-permute-start(f32[1,2,256]{2,1,0:T(2,128)S(1)} %get-tuple-element.176), channel_id=1, source_target_pairs={{0,8},{8,16},{16,24},{24,0},{1,9},{9,17},{17,25},{25,1},{2,10},{10... | collective-permute-start | bytes 6152 | tf_op jit(solution)/shard_map/ppermute | solution.py:23
  122.0 19.7 %slice-start = ((f32[64,896]{0,1:T(8,128)}), f32[64,512]{0,1:T(8,128)S(1)}, s32[]{:S(2)}) async-start(f32[64,896]{0,1:T(8,128)} %copy-done.2), calls=%async_computation.2 | async-start | bytes 524288 | tf_op jit(solution)/shard_map/slice | solution.py:156
  146.3 8.1 %all-to-all-start.1 = ((f32[8,1,1024]{2,1,0:T(1,128)}), f32[8,1,1024]{2,1,0:T(1,128)S(1)}, u32[]{:S(2)}, u32[]{:S(2)}) async-start(f32[8,1,1024]{2,1,0:T(1,128)} %reshape.683), calls=%async_computation.1 | async-start | bytes 65536 | tf_op jit(solution)/shard_map/all_to_all | solution.py:116
  149.7 6.8 %collective-permute-start.2 = (f32[1,64,128]{1,2,0:T(8,128)S(1)}, f32[1,64,128]{1,2,0:T(8,128)S(1)}, u32[]{:S(2)}, u32[]{:S(2)}) collective-permute-start(f32[1,64,128]{1,2,0:T(8,128)S(1)} %get-tuple-element.199), channel_id=1, source_target_pairs={{0,8},{8,16},{16,24},{24,0},{1,9},{9,17},{17,25},{25,1},{2,10},{10... | collective-permute-start | bytes 98312 | tf_op jit(solution)/shard_map/ppermute | solution.py:23
  149.7 6.7 %collective-permute-start.3 = (f32[1,64,128]{1,2,0:T(8,128)S(1)}, f32[1,64,128]{1,2,0:T(8,128)S(1)}, u32[]{:S(2)}, u32[]{:S(2)}) collective-permute-start(f32[1,64,128]{1,2,0:T(8,128)S(1)} %get-tuple-element.200), channel_id=1, source_target_pairs={{8,0},{16,8},{24,16},{0,24},{9,1},{17,9},{25,17},{1,25},{10,2},{18... | collective-permute-start | bytes 98312 | tf_op jit(solution)/shard_map/ppermute | solution.py:24
where the time goes:
time: 209 us; the launch traced here: 208 us
  matrix products  81.1 us (39%)
  local copies, waits for them, and re-layouts  44.5 us (21%)
  other arithmetic  42.8 us (20%)
  starting transfers between devices  18.3 us (9%)
  blocking collectives  13.9 us (7%)
  waiting for transfers between devices  7.17 us (3%)
    dot_general x1, matrix products, project_traces(): jnp.einsum('xaf,abf->xbf', left_map, traces, precision=highest)  20.6 us
    dot_general x1, matrix products, back_project(): jnp.einsum('xaf,xyf->ayf', left_map, values, precision=highest)  18.7 us
    dot_general x1, matrix products, back_project(): jnp.einsum('ybf,ayf->abf', right_map, partial_rows, precision=highest)  18.6 us
    dot_general x1, matrix products, project_traces(): jnp.einsum('ybf,xbf->xyf', right_map, partial_rows, precision=highest)  18.5 us
    scatter-add x1, other arithmetic, coarse_correction(): totals = jnp.zeros((2 * NV_DEV,), jnp.float32).at[flat_ids].add(corner_vals)  14.7 us
    scatter-add x1, other arithmetic, coarse_correction(): counts = jnp.zeros((2 * NV_DEV,), jnp.float32).at[flat_ids].add(jnp.ones(...  14.7 us
    psum x1, blocking collectives, coarse_correction(): totals, counts = lax.psum((totals, counts), 'clus')  13.9 us
    gather x1, local copies, waits for them, and re-layouts, coarse_correction(): return coarse[window_ids]  13.2 us
  transfers between devices with their start and end apart: 8, of which 3 were waited for; matrix products, arithmetic and copies ran while one was open for 24% of the time, Pallas kernels for 0%

commit v1 on v0

v1 whole, which is shorter than its diff:
```python
import functools

import jax
import jax.numpy as jnp
from jax import lax
from jax.experimental import pallas as pl
from jax.experimental.pallas import tpu as pltpu
from jax.sharding import PartitionSpec as P

POINTS = 8
SQ = POINTS * POINTS
CAP_E = 128
CAP_C = 16
M_DEV = 512
NV_DEV = 256
HALF = 64
LANES = 128
MIB = 1 << 20

f32 = jnp.float32
bf16 = jnp.bfloat16
highest = lax.Precision.HIGHEST


def split(x):
    hi = x.astype(bf16)
    lo = (x - hi.astype(f32)).astype(bf16)
    return hi, lo


def stack3(x, axis=0):
    hi, lo = split(x)
    return jnp.concatenate([hi, lo, hi], axis=axis)


def stack2(x):
    hi, lo = split(x)
    return jnp.concatenate([hi, lo], axis=0)


def mm(a, b):
    return lax.dot_general(a, b, (((1,), (0,)), ((), ())), preferred_element_type=f32)


def mm_nt(a, b):
    return lax.dot_general(a, b, (((1,), (1,)), ((), ())), preferred_element_type=f32)


def iota(shape, dim):
    return lax.broadcasted_iota(jnp.int32, shape, dim)


def expand(matrix, copies):
    width = SQ * copies
    lane = iota((POINTS, width), 1) % SQ
    row = iota((POINTS, width), 0)
    to_first = (lane // POINTS == row).astype(f32)
    to_second = (lane % POINTS == row).astype(f32)
    first = jnp.dot(matrix, to_first, precision=highest, preferred_element_type=f32)
    second = jnp.dot(matrix, to_second, precision=highest, preferred_element_type=f32)
    first = jnp.broadcast_to(first[:, None, :], (POINTS, POINTS, width)).reshape(SQ, width)
    second = jnp.concatenate([second] * POINTS, axis=0)
    return first, second


def hi_hi_lo(matrix):
    hi = matrix.astype(bf16).astype(f32)
    lane = iota(matrix.shape, 1)
    return jnp.where(lane < 2 * SQ, hi, matrix - hi).astype(bf16)


def kron_four(low, high):
    low_first, low_second = expand(low, 3)
    high_first, high_second = expand(high, 3)
    maps = [
        low_first * low_second,
        low_first * high_second,
        high_first * low_second,
        high_first * high_second,
    ]
    return hi_hi_lo(jnp.concatenate(maps, axis=0))


def load_rows(ref, rows):
    return jnp.concatenate([ref[h, rows, :] for h in range(ref.shape[0])], axis=1)


def load_comb(ref, j):
    return jnp.concatenate([load_rows(ref, pl.ds(a * SQ + j * 8, 8)) for a in range(8)], axis=0)


def store_rows(ref, rows, value):
    for h in range(ref.shape[0]):
        ref[h, rows, :] = value[:, h * LANES : (h + 1) * LANES]


def add_rows(ref, rows, value):
    for h in range(ref.shape[0]):
        ref[h, rows, :] += value[:, h * LANES : (h + 1) * LANES]


def lane_copies(hbm, blocks, sems, outward):
    copies = []
    for h in range(blocks.shape[0]):
        outer = hbm.at[:, pl.ds(h * LANES, LANES)]
        ends = (blocks.at[h], outer) if outward else (outer, blocks.at[h])
        copies.append(pltpu.make_async_copy(*ends, sems.at[h]))
    return copies


def pick_level(plain, mapped, level):
    out = plain
    for number in range(1, 5):
        out = jnp.where(level == number, mapped[(number - 1) * SQ : number * SQ], out)
    return out


def one_hot_rows(ids, first, count):
    return (iota((count, ids.shape[1]), 0) + first == ids).astype(f32).astype(bf16)


def window_ids(vertex_ids, elem_index, total):
    shifted = vertex_ids - elem_index * NV_DEV
    return jnp.where(shifted < 0, shifted + total, shifted)


def corner_row(corner):
    last = POINTS - 1
    return corner // 4 * last * SQ + corner // 2 % 2 * last * POINTS + corner % 2 * last


def send_kernel(
    total_vertices,
    elem_ref,
    nodal_hbm,
    metric_hbm,
    level_ref,
    target_ref,
    interp_ref,
    vertex_ref,
    down_ref,
    up_ref,
    group_ref,
    nodal_ref,
    metric_ref,
    traces_ref,
    remote_ref,
    slot_level_ref,
    maps_ref,
    low_ids_ref,
    sems,
):
    nodal_copies = lane_copies(nodal_hbm, nodal_ref, sems, False)
    metric_copy = pltpu.make_async_copy(metric_hbm, metric_ref, sems.at[len(nodal_copies)])
    for copy in nodal_copies:
        copy.start()
    metric_copy.start()
    slots = remote_ref.shape[0]
    elems = nodal_hbm.shape[1]
    level = level_ref[...]
    remote_ref[...] = one_hot_rows(target_ref[...], M_DEV, slots)
    maps = kron_four(interp_ref[0], interp_ref[1])
    maps_ref[...] = maps
    window = window_ids(vertex_ref[...], elem_ref[0], total_vertices)
    high_id = window // HALF
    low_id = window % HALF
    zeros = jnp.zeros((HALF, elems), bf16)
    low_hot = []
    for corner in range(8):
        hot = one_hot_rows(low_id[corner : corner + 1], 0, HALF)
        low_hot.append(jnp.concatenate([zeros, hot], axis=0))
    low_hot = jnp.concatenate(low_hot, axis=1)
    low_ids_ref[...] = low_hot

    for copy in nodal_copies:
        copy.wait()
    faces = [
        load_rows(nodal_ref, pl.ds(0, SQ)),
        load_rows(nodal_ref, pl.ds(7 * SQ, SQ)),
        load_comb(nodal_ref, 0),
        load_comb(nodal_ref, 7),
        load_rows(nodal_ref, pl.ds(0, SQ, stride=8)),
        load_rows(nodal_ref, pl.ds(7, SQ, stride=8)),
    ]
    trace = jnp.concatenate(faces, axis=1)
    hi, lo = split(trace)
    traces_ref[0:SQ, :] = hi
    traces_ref[SQ : 2 * SQ, :] = lo
    traces_ref[2 * SQ :, :] = jnp.broadcast_to(level, (16, level.shape[1])).astype(f32).astype(bf16)

    picked = mm_nt(traces_ref[...], remote_ref[...])
    plain = picked[0:SQ] + picked[SQ : 2 * SQ]
    slot_level = picked[2 * SQ : 2 * SQ + 8]
    slot_level_ref[...] = slot_level
    mapped = mm(maps, stack3(plain))
    sent = pick_level(plain, mapped, slot_level[0:1])
    down_ref[...] = sent[:, 0:CAP_E]
    up_ref[...] = sent[:, CAP_E : 2 * CAP_E]

    row = iota((16, elems), 0)
    row_high = row % 4 + 4 * (row // 8)
    is_count = row // 4 % 2 == 1
    weighted = []
    for corner in range(8):
        value = load_rows(nodal_ref, pl.ds(corner_row(corner), 1))
        value_hi = value.astype(bf16).astype(f32)
        value_lo = value - value_hi
        mine = high_id[corner : corner + 1] == row_high
        first = jnp.where(mine, jnp.where(is_count, 1.0, value_hi), 0.0)
        second = jnp.where(mine & ~is_count, value_lo, 0.0)
        weighted.append(jnp.concatenate([first, second], axis=0).astype(bf16))
    sums = mm_nt(jnp.concatenate(weighted, axis=1), low_hot)
    sums = sums[0:16] + sums[16:32]
    group = sent[:, 2 * CAP_E :]
    group = jnp.concatenate([group, jnp.zeros_like(group)], axis=0).T
    group_ref[...] = group + jnp.concatenate([sums] * (group.shape[0] // 16), axis=0)
    metric_copy.wait()


def local_kernel(
    traces_ref,
    maps_ref,
    level_ref,
    target_ref,
    slot_mortar_ref,
    nodal_ref,
    metric_ref,
    derivative_ref,
    mortar_ref,
    answers_ref,
    equal_ref,
    local_ref,
    slot_hot_ref,
    stiff_ref,
    by_row,
    by_col,
):
    hi = traces_ref[0:SQ, :]
    lo = traces_ref[SQ : 2 * SQ, :]
    plain = hi.astype(f32) + lo.astype(f32)
    mapped = mm(maps_ref[...], jnp.concatenate([hi, lo, hi], axis=0))
    projected = pick_level(plain, mapped, level_ref[...])
    local_ref[...] = one_hot_rows(target_ref[...], 0, M_DEV)
    mortar = mm_nt(stack2(projected), local_ref[...])
    mortar = mortar[0:SQ] + mortar[SQ:]
    mortar_ref[...] = mortar
    slot_row = slot_mortar_ref[...]
    slots = slot_row.shape[1]
    slot_hot_t = one_hot_rows(slot_row, 0, M_DEV)
    answers = mm(stack2(mortar), slot_hot_t)
    answers_ref[...] = answers[0:SQ] + answers[SQ:]
    slot_col = jnp.broadcast_to(slot_row, (128, slots)).T[:, 0:1]
    equal_ref[...] = (slot_col == slot_row).astype(f32).astype(bf16)
    slot_hot_ref[...] = (slot_col == iota((slots, M_DEV), 1)).astype(f32).astype(bf16)
    stiffness(nodal_ref, metric_ref, derivative_ref, stiff_ref, by_row, by_col)


def stiffness(nodal_ref, metric_ref, derivative_ref, stiff_ref, by_row, by_col):
    derivative = derivative_ref[...]
    row = iota((SQ, 3 * SQ), 0)
    lane = iota((SQ, 3 * SQ), 1) % SQ

    def pair(matrix):
        first, second = expand(matrix, 3)
        outer = jnp.where(row % 8 == lane % 8, first, 0.0)
        inner = jnp.where(row // 8 == lane // 8, second, 0.0)
        return hi_hi_lo(outer), hi_hi_lo(inner)

    outer, inner = pair(derivative)
    outer_t, inner_t = pair(derivative.T)
    both = jnp.concatenate([outer, inner], axis=0)
    for i in range(8):
        slab = load_rows(nodal_ref, pl.ds(i * SQ, SQ))
        grad = mm(outer, stack3(slab))
        weighted = grad * metric_ref[1, i * SQ : (i + 1) * SQ, :].astype(f32)
        stiff_ref[i * SQ : (i + 1) * SQ, :] = mm(outer_t, stack3(weighted))
        by_row[i * SQ : (i + 1) * SQ, :] = metric_ref[0, i * SQ : (i + 1) * SQ, :].astype(f32)
        by_col[i * SQ : (i + 1) * SQ, :] = metric_ref[2, i * SQ : (i + 1) * SQ, :].astype(f32)

    def comb(ref, j):
        return jnp.concatenate([ref[i * SQ + j * 8 : i * SQ + j * 8 + 8, :] for i in range(8)], axis=0)

    for j in range(8):
        grad = mm(both, stack3(load_comb(nodal_ref, j)))
        out = mm(outer_t, stack3(grad[0:SQ] * comb(by_row, j)))
        out = out + mm(inner_t, stack3(grad[SQ:] * comb(by_col, j)))
        for i in range(8):
            stiff_ref[i * SQ + j * 8 : i * SQ + j * 8 + 8, :] += out[i * 8 : i * 8 + 8]


def answer_kernel(
    from_up_ref,
    from_down_ref,
    group_ref,
    equal_ref,
    local_answers_ref,
    down_ref,
    up_ref,
    group_out_ref,
    incoming_ref,
    sums_ref,
):
    group_in = group_ref[...]
    incoming = jnp.concatenate([from_up_ref[...], from_down_ref[...], group_in.T[0:SQ]], axis=1)
    incoming_ref[...] = incoming
    added = mm(stack2(incoming), equal_ref[...])
    answers = local_answers_ref[...] + added[0:SQ] + added[SQ:]
    sums = group_in[0:16]
    for block in range(1, group_in.shape[0] // 16):
        sums = sums + group_in[block * 16 : block * 16 + 16]
    sums_ref[...] = sums
    down_ref[0:SQ, :] = answers[:, 0:CAP_E]
    up_ref[0:SQ, :] = answers[:, CAP_E : 2 * CAP_E]
    down_ref[SQ:, :] = sums[0:8]
    up_ref[SQ:, :] = sums[8:16]
    group = answers[:, 2 * CAP_E :]
    group_out_ref[...] = jnp.concatenate([group, jnp.zeros_like(group)], axis=0).T


def gather_kernel(
    mortar_ref,
    incoming_ref,
    slot_hot_ref,
    local_ref,
    level_ref,
    interp_ref,
    stiff_ref,
    result_ref,
    maps_ref,
):
    added = mm(stack2(incoming_ref[...]), slot_hot_ref[...])
    mortar = mortar_ref[...] + added[0:SQ] + added[SQ:]
    picked = mm(stack2(mortar), local_ref[...])
    picked = picked[0:SQ] + picked[SQ:]
    maps = kron_four(interp_ref[0].T, interp_ref[1].T)
    maps_ref[...] = maps
    back = pick_level(picked, mm(maps, stack3(picked)), level_ref[...])
    store_rows(result_ref, slice(None), stiff_ref[...])
    add_faces(result_ref, back)


def add_faces(ref, back):
    elems = ref.shape[0] * LANES
    parts = [back[:, f * elems : (f + 1) * elems] for f in range(6)]
    add_rows(ref, pl.ds(0, SQ), parts[0])
    add_rows(ref, pl.ds(7 * SQ, SQ), parts[1])
    for a in range(8):
        add_rows(ref, pl.ds(a * SQ, 8), parts[2][a * 8 : a * 8 + 8])
        add_rows(ref, pl.ds(a * SQ + 56, 8), parts[3][a * 8 : a * 8 + 8])
    add_rows(ref, pl.ds(0, SQ, stride=8), parts[4])
    add_rows(ref, pl.ds(7, SQ, stride=8), parts[5])


def final_kernel(
    total_vertices,
    elem_ref,
    from_up_ref,
    from_down_ref,
    group_ref,
    slot_level_ref,
    maps_ref,
    remote_ref,
    sums_ref,
    vertex_ref,
    low_ids_ref,
    result_ref,
    out_hbm,
    out_ref,
    sems,
):
    arrived = jnp.concatenate(
        [from_up_ref[0:SQ, :], from_down_ref[0:SQ, :], group_ref[...].T[0:SQ]], axis=1
    )
    slot_back = pick_level(arrived, mm(maps_ref[...], stack3(arrived)), slot_level_ref[0:1, :])
    back = mm(stack2(slot_back), remote_ref[...])
    back = back[0:SQ] + back[SQ:]

    first = sums_ref[0:8, :] + from_up_ref[SQ:, :]
    second = sums_ref[8:16, :] + from_down_ref[SQ:, :]
    totals = jnp.concatenate([first[0:4], second[0:4]], axis=0)
    counts = jnp.concatenate([first[4:8], second[4:8]], axis=0)
    coarse = jnp.where(iota(totals.shape, 1) < HALF, 0.0, totals / (1.0 + counts))
    coarse_hi = coarse.astype(bf16).astype(f32)
    table = jnp.concatenate([coarse_hi, coarse - coarse_hi], axis=0).astype(bf16)
    found = mm(table, low_ids_ref[...])
    found = found[0:8] + found[8:16]
    high_id = window_ids(vertex_ref[...], elem_ref[0], total_vertices) // HALF

    out_ref[...] = result_ref[...]
    add_faces(out_ref, back)
    elems = out_hbm.shape[1]
    row = iota((8, elems), 0)
    for corner in range(8):
        mine = row == high_id[corner : corner + 1]
        fix = jnp.where(mine, found[:, corner * elems : (corner + 1) * elems], 0.0)
        at = corner_row(corner)
        add_rows(out_ref, pl.ds(at, 1), jnp.sum(fix, axis=0, keepdims=True))
    copies = lane_copies(out_hbm, out_ref, sems, True)
    for copy in copies:
        copy.start()
    for copy in copies:
        copy.wait()


VMEM = pl.BlockSpec(memory_space=pltpu.VMEM)
SMEM = pl.BlockSpec(memory_space=pltpu.SMEM)
HBM = pl.BlockSpec(memory_space=pltpu.HBM)


def params(mib):
    return pltpu.CompilerParams(vmem_limit_bytes=mib * MIB)


def cost(us):
    return pl.CostEstimate(flops=int(us * 5e8), bytes_accessed=int(us * 2e6), transcendentals=0)


def neighbours(axis):
    peers = lax.axis_size(axis)
    up = [(i, (i + 1) % peers) for i in range(peers)]
    return up, [(j, i) for i, j in up]


def exchange(down, up, group):
    up_pairs, down_pairs = neighbours("elem")
    group = lax.all_to_all(group, "clus", split_axis=0, concat_axis=0, tiled=True)
    return lax.ppermute(up, "elem", up_pairs), lax.ppermute(down, "elem", down_pairs), group


def on_device(nodal, metric, derivative, interp, face_level, face_target, slot_mortar, vertex_ids):
    elems = nodal.shape[1]
    faces = face_level.shape[0]
    slots = slot_mortar.shape[0]
    total_vertices = NV_DEV * lax.axis_size("elem")
    elem_index = lax.axis_index("elem").astype(jnp.int32).reshape(1)
    level = face_level.reshape(1, faces)
    target = face_target.reshape(1, faces)
    slot_row = slot_mortar.reshape(1, slots)
    blocked = (elems // LANES, nodal.shape[0], LANES)
    group_slots = slots - 2 * CAP_E

    down, up, group, nodal_in, metric_in, traces, remote, slot_level, maps, low_ids = pl.pallas_call(
        functools.partial(send_kernel, total_vertices),
        in_specs=[SMEM, HBM, HBM] + [VMEM] * 4,
        out_specs=[VMEM] * 10,
        out_shape=[
            pltpu.VMEM((SQ, CAP_E), f32),
            pltpu.VMEM((SQ, CAP_E), f32),
            pltpu.VMEM((group_slots, 128), f32),
            pltpu.VMEM(blocked, f32),
            pltpu.VMEM(metric.shape, bf16),
            pltpu.VMEM((2 * SQ + 16, faces), bf16),
            pltpu.VMEM((slots, faces), bf16),
            pltpu.VMEM((8, slots), f32),
            pltpu.VMEM((4 * SQ, 3 * SQ), bf16),
            pltpu.VMEM((2 * HALF, 8 * elems), bf16),
        ],
        scratch_shapes=[pltpu.SemaphoreType.DMA((blocked[0] + 1,))],
        compiler_params=params(16),
        name="send",
    )(elem_index, nodal, metric, level, target, interp, vertex_ids)

    from_up, from_down, group_in = exchange(down, up, group)

    mortar, local_answers, equal, local, slot_hot, stiff = pl.pallas_call(
        local_kernel,
        in_specs=[VMEM] * 8,
        out_specs=[VMEM] * 6,
        out_shape=[
            pltpu.VMEM((SQ, M_DEV), f32),
            pltpu.VMEM((SQ, slots), f32),
            pltpu.VMEM((slots, slots), bf16),
            pltpu.VMEM((M_DEV, faces), bf16),
            pltpu.VMEM((slots, M_DEV), bf16),
            pltpu.VMEM(nodal.shape, f32),
        ],
        scratch_shapes=[pltpu.VMEM(nodal.shape, f32), pltpu.VMEM(nodal.shape, f32)],
        compiler_params=params(16),
        cost_estimate=cost(3),
        name="local",
    )(traces, maps, level, target, slot_row, nodal_in, metric_in, derivative)

    down, up, group, incoming, sums = pl.pallas_call(
        answer_kernel,
        in_specs=[VMEM] * 5,
        out_specs=[VMEM] * 5,
        out_shape=[
            pltpu.VMEM((SQ + 8, CAP_E), f32),
            pltpu.VMEM((SQ + 8, CAP_E), f32),
            pltpu.VMEM((group_slots, 128), f32),
            pltpu.VMEM((SQ, slots), f32),
            pltpu.VMEM((16, 128), f32),
        ],
        compiler_params=params(16),
        name="answer",
    )(from_up, from_down, group_in, equal, local_answers)

    from_up, from_down, group_in = exchange(down, up, group)

    result, back_maps = pl.pallas_call(
        gather_kernel,
        in_specs=[VMEM] * 7,
        out_specs=[VMEM] * 2,
        out_shape=[pltpu.VMEM(blocked, f32), pltpu.VMEM((4 * SQ, 3 * SQ), bf16)],
        compiler_params=params(16),
        cost_estimate=cost(2),
        name="gather",
    )(mortar, incoming, slot_hot, local, level, interp, stiff)

    return pl.pallas_call(
        functools.partial(final_kernel, total_vertices),
        in_specs=[SMEM] + [VMEM] * 10,
        out_specs=HBM,
        out_shape=jax.ShapeDtypeStruct(nodal.shape, f32),
        scratch_shapes=[pltpu.VMEM(blocked, f32), pltpu.SemaphoreType.DMA((blocked[0],))],
        compiler_params=params(16),
        name="final",
    )(
        elem_index,
        from_up,
        from_down,
        group_in,
        slot_level,
        back_maps,
        remote,
        sums,
        vertex_ids,
        low_ids,
        result,
    )


def solution(mesh):
    in_specs = (
        P(None, ("elem", "clus")),
        P(None, None, ("elem", "clus")),
        P(),
        P(),
        P(("elem", "clus")),
        P(("elem", "clus")),
        P(("elem", "clus")),
        P(None, ("elem", "clus")),
    )
    out_specs = P(None, ("elem", "clus"))
    return jax.shard_map(
        on_device, mesh=mesh, in_specs=in_specs, out_specs=out_specs, check_vma=False
    )
```

time: 209 us -> 42.4 us (0.20)
  matrix products: 81.1 us -> 0 us
  other arithmetic: 42.8 us -> 0 us
  local copies, waits for them, and re-layouts: 44.5 us -> 16.2 us
  blocking collectives: 13.9 us -> 0 us
  Pallas kernels: 0 us -> 8.29 us
  waiting for transfers between devices: 7.17 us -> 0.02 us
    dot_general x10 -> x0, matrix products: 81.1 us -> none  [the longest x1 20.6 us: project_traces(): jnp.einsum('xaf,abf->xbf', left_map, traces, precision=highest)]
    scatter-add x8 -> x0, other arithmetic: 41.1 us -> none  [the longest x1 14.7 us: coarse_correction(): totals = jnp.zeros((2 * NV_DEV,), jnp.float32).at[flat_ids].add(corner_vals)]
    gather x4 -> x0, local copies, waits for them, and re-layouts: 17.2 us -> none  [the longest x1 13.2 us: coarse_correction(): return coarse[window_ids]]
    psum x1 -> x0, blocking collectives: 13.9 us -> none  [coarse_correction(): totals, counts = lax.psum((totals, counts), 'clus')]
    unnamed x30 -> x34, local copies, waits for them, and re-layouts: 5.09 us -> 14.1 us
    transpose x2 -> x0, local copies, waits for them, and re-layouts: 8.84 us -> none  [the longest x1 4.44 us: project_traces(): jnp.einsum('ybf,xbf->xyf', right_map, partial_rows, precision=highest)]
    pallas_call x0 -> x5, Pallas kernels: none -> 8.29 us  [the longest x1 2.7 us: on_device(): pl.pallas_call(local_kernel, in_specs=[VMEM] * 8, out_specs=[VMEM] * 6, o...]
    ppermute x6 -> x4, waiting for transfers between devices: 6.28 us -> 0.01 us  [the longest x2 0.01 us: exchange(): lax.ppermute(up, 'elem', up_pairs)]
  transfers between devices with their start and end apart: 8 -> 6, of which waited for: 3 -> 0; matrix products, arithmetic and copies ran while one was open for 24% -> 2% of each run, Pallas kernels for 0% -> 9%
where the time goes in v1:
time: 42.4 us; the launch traced here: 41.6 us
  starting transfers between devices  17 us (40%)
  local copies, waits for them, and re-layouts  16.2 us (38%)
  Pallas kernels  8.29 us (20%)
    unnamed x34, local copies, waits for them, and re-layouts  14.1 us
    all_to_all x2, starting transfers between devices, exchange(): lax.all_to_all(group, 'clus', split_axis=0, concat_axis=0, tiled=True)  9.37 us
    ppermute x2, starting transfers between devices, exchange(): lax.ppermute(down, 'elem', down_pairs)  6.06 us
    pallas_call x1, Pallas kernels, on_device(): pl.pallas_call(local_kernel, in_specs=[VMEM] * 8, out_specs=[VMEM] * 6, o...  2.7 us
    pallas_call x1, Pallas kernels, on_device(): pl.pallas_call(functools.partial(send_kernel, total_vertices), in_specs=[...  2.16 us
    ppermute x2, starting transfers between devices, exchange(): lax.ppermute(up, 'elem', up_pairs)  1.58 us
    pallas_call x1, Pallas kernels, on_device(): pl.pallas_call(functools.partial(final_kernel, total_vertices), in_specs=...  1.45 us
    pallas_call x1, Pallas kernels, on_device(): pl.pallas_call(gather_kernel, in_specs=[VMEM] * 7, out_specs=[VMEM] * 2,...  0.99 us
  transfers between devices with their start and end apart: 6, of which 0 were waited for; matrix products, arithmetic and copies ran while one was open for 2% of the time, Pallas kernels for 9%

profile of v1, /device:TPU:0, one launch (start us, length us, event | category | flops | bytes accessed | tf_op | source)
XLA Modules:
  0.0 41.6 jit_solution(14572176654806934174)
XLA Ops:
  0.0 0.7 %reshape.17.level_ref = s32[1,1536]{1,0:T(1,128)S(1)} reshape(s32[1536]{0:T(1024)} %param.12) | data formatting | bytes 12288 | tf_op jit(solution)/shard_map/reshape | solution.py:436
  0.7 0.7 %reshape.18.target_ref = s32[1,1536]{1,0:T(1,128)S(1)} reshape(s32[1536]{0:T(1024)} %param.13) | data formatting | bytes 12288 | tf_op jit(solution)/shard_map/reshape | solution.py:437
  1.4 1.1 %copy-done = bf16[3,512,256]{2,1,0:T(8,128)(2,1)S(1)} copy-done((bf16[3,512,256]{2,1,0:T(8,128)(2,1)S(1)}, bf16[3,512,256]{2,1,0:T(8,128)(2,1)}, u32[]{:S(2)}) %copy-start) | copy-done | bytes 786456
  2.5 1.0 %copy-done.1 = f32[512,256]{1,0:T(8,128)S(1)} copy-done((f32[512,256]{1,0:T(8,128)S(1)}, f32[512,256]{1,0:T(8,128)}, u32[]{:S(2)}) %copy-start.1) | copy-done | bytes 524312
  5.0 2.2 %send.1 = (f32[64,128]{1,0:T(8,128)S(1)}, f32[64,128]{1,0:T(8,128)S(1)}, f32[128,128]{1,0:T(8,128)}, f32[2,512,128]{2,1,0:T(8,128)S(1)}, bf16[3,512,256]{2,1,0:T...) custom-call(s32[1]{0:T(128)} %bitcast.elem_ref, ...), custom_call_target="tpu_custom_call" | custom-call | tf_op jit(solution)/shard_map/send/pallas_call | solution.py:442
  7.2 0.8 %copy-done.6 = f32[2,512,128]{2,1,0:T(8,128)} copy-done((f32[2,512,128]{2,1,0:T(8,128)}, f32[2,512,128]{2,1,0:T(8,128)S(1)}, u32[]{:S(2)}) %copy-start.6) | copy-done | bytes 524312
  7.9 0.8 %copy-done.8 = bf16[144,1536]{1,0:T(8,128)(2,1)} copy-done((bf16[144,1536]{1,0:T(8,128)(2,1)}, bf16[144,1536]{1,0:T(8,128)(2,1)S(1)}, u32[]{:S(2)}) %copy-start.8) | copy-done | bytes 442392
  8.7 5.2 %all-to-all-start = ((f32[8,16,128]{2,1,0:T(8,128)}), f32[8,16,128]{2,1,0:T(8,128)S(1)}, u32[]{:S(2)}, u32[]{:S(2)}) async-start(f32[8,16,128]{2,1,0:T(8,128)} %bitcast.1), calls=%async_computation | async-start | bytes 131072 | tf_op jit(solution)/shard_map/all_to_all | solution.py:426
  13.9 1.6 %collective-permute-start = (f32[64,128]{1,0:T(8,128)S(1)}, f32[64,128]{1,0:T(8,128)S(1)}, u32[]{:S(2)}, u32[]{:S(2)}) collective-permute-start(f32[64,128]{1,0:T(8,128)S(1)} %get-tuple-element.28), channel_id=1, source_target_pairs={{0,8},{8,16},{16,24},{24,0},{1,9},{9,17},{17,25},{25,1},{2,10},{10... | collective-permute-start | bytes 98312 | tf_op jit(solution)/shard_map/ppermute | solution.py:427
  15.5 2.2 %collective-permute-start.1 = (f32[64,128]{1,0:T(8,128)S(1)}, f32[64,128]{1,0:T(8,128)S(1)}, u32[]{:S(2)}, u32[]{:S(2)}) collective-permute-start(f32[64,128]{1,0:T(8,128)S(1)} %get-tuple-element.29), channel_id=1, source_target_pairs={{8,0},{16,8},{24,16},{0,24},{9,1},{17,9},{25,17},{1,25},{10,2},{18... | collective-permute-start | bytes 98312 | tf_op jit(solution)/shard_map/ppermute | solution.py:427
  18.4 1.0 %copy-done.7 = f32[2,512,128]{2,1,0:T(8,128)S(1)} copy-done((f32[2,512,128]{2,1,0:T(8,128)S(1)}, f32[2,512,128]{2,1,0:T(8,128)}, u32[]{:S(2)}) %copy-start.7) | copy-done | bytes 524312
  19.4 1.0 %copy-done.9 = bf16[144,1536]{1,0:T(8,128)(2,1)S(1)} copy-done((bf16[144,1536]{1,0:T(8,128)(2,1)S(1)}, bf16[144,1536]{1,0:T(8,128)(2,1)}, u32[]{:S(2)}) %copy-start.9) | copy-done | bytes 442392
  21.1 2.7 %local.1 = (f32[64,512]{1,0:T(8,128)S(1)}, f32[64,384]{1,0:T(8,128)S(1)}, bf16[384,384]{1,0:T(8,128)(2,1)S(1)}, bf16[512,1536]{1,0:T(8,128)(2,1)S(1)}, bf16[384,...) custom-call(bf16[144,1536]{1,0:T(8,128)(2,1)S(1)} %copy-done.9, bf16[256,192]{1,0:T(8,128)(2,1)S(1)} %get-tuple-element.32.maps_ref, ...), custom_call_target="tpu_custom_call" | custom-call | flops 1500000000 | bytes 6000000 | tf_op jit(solution)/shard_map/local/pallas_call | solution.py:465
  23.9 1.2 %copy-done.11 = bf16[512,1536]{1,0:T(8,128)(2,1)} copy-done((bf16[512,1536]{1,0:T(8,128)(2,1)}, bf16[512,1536]{1,0:T(8,128)(2,1)S(1)}, u32[]{:S(2)}) %copy-start.11) | copy-done | bytes 1572888
  25.0 0.8 %copy-done.13 = f32[512,256]{1,0:T(8,128)} copy-done((f32[512,256]{1,0:T(8,128)}, f32[512,256]{1,0:T(8,128)S(1)}, u32[]{:S(2)}) %copy-start.13) | copy-done | bytes 524312
  25.8 0.8 %copy-done.15 = bf16[384,512]{1,0:T(8,128)(2,1)} copy-done((bf16[384,512]{1,0:T(8,128)(2,1)}, bf16[384,512]{1,0:T(8,128)(2,1)S(1)}, u32[]{:S(2)}) %copy-start.15) | copy-done | bytes 393240
  26.6 1.0 %answer.1 = (f32[72,128]{1,0:T(8,128)S(1)}, f32[72,128]{1,0:T(8,128)S(1)}, f32[128,128]{1,0:T(8,128)}, f32[64,384]{1,0:T(8,128)S(1)}, f32[16,128]{1,0:T(8,128)S(1)}) custom-call(f32[64,128]{1,0:T(8,128)S(1)} %collective-permute-done.from_up_ref, f32[64,128]{1,0:T(8,128)S(1)} %collective-permute-done.1.from_down_ref, f32[128,128]{1,0:T(8,128)S(1)} %bitcast.6, ...), custom_call_target="tpu_custom_call" | custom-call | tf_op jit(solution)/shard_map/answer/pallas_call | solution.py:483
  27.6 4.2 %all-to-all-start.1 = ((f32[8,16,128]{2,1,0:T(8,128)}), f32[8,16,128]{2,1,0:T(8,128)S(1)}, u32[]{:S(2)}, u32[]{:S(2)}) async-start(f32[8,16,128]{2,1,0:T(8,128)} %bitcast.3), calls=%async_computation.1 | async-start | bytes 131072 | tf_op jit(solution)/shard_map/all_to_all | solution.py:426
  31.8 3.8 %collective-permute-start.3 = (f32[72,128]{1,0:T(8,128)S(1)}, f32[72,128]{1,0:T(8,128)S(1)}, u32[]{:S(2)}, u32[]{:S(2)}) collective-permute-start(f32[72,128]{1,0:T(8,128)S(1)} %get-tuple-element.38), channel_id=1, source_target_pairs={{8,0},{16,8},{24,16},{0,24},{9,1},{17,9},{25,17},{1,25},{10,2},{18... | collective-permute-start | bytes 110600 | tf_op jit(solution)/shard_map/ppermute | solution.py:427
  35.6 1.4 %copy-done.12 = bf16[512,1536]{1,0:T(8,128)(2,1)S(1)} copy-done((bf16[512,1536]{1,0:T(8,128)(2,1)S(1)}, bf16[512,1536]{1,0:T(8,128)(2,1)}, u32[]{:S(2)}) %copy-start.12) | copy-done | bytes 1572888
  37.0 1.0 %copy-done.14 = f32[512,256]{1,0:T(8,128)S(1)} copy-done((f32[512,256]{1,0:T(8,128)S(1)}, f32[512,256]{1,0:T(8,128)}, u32[]{:S(2)}) %copy-start.14) | copy-done | bytes 524312
  38.1 1.0 %copy-done.16 = bf16[384,512]{1,0:T(8,128)(2,1)S(1)} copy-done((bf16[384,512]{1,0:T(8,128)(2,1)S(1)}, bf16[384,512]{1,0:T(8,128)(2,1)}, u32[]{:S(2)}) %copy-start.16) | copy-done | bytes 393240
  39.1 1.0 %gather.1 = (f32[2,512,128]{2,1,0:T(8,128)S(1)}, bf16[256,192]{1,0:T(8,128)(2,1)S(1)}) custom-call(f32[64,512]{1,0:T(8,128)S(1)} %get-tuple-element.41.mortar_ref, f32[64,384]{1,0:T(8,128)S(1)} %get-tuple-element.42.incoming_ref, bf16[384,512]{1,0:T(8,128)(2,1)S(1)} %copy-done.16, bf16[512,1536]{1,0:T(8,128)(2,1)S(1)} %copy-done.12, ...), custom_call_target="tpu_custom_call" | custom-call | flops 1000000000 | bytes 4000000 | tf_op jit(solution)/shard_map/gather/pallas_call | solution.py:500
  40.1 1.5 %final.1 = f32[512,256]{1,0:T(8,128)} custom-call(s32[1]{0:T(128)} %bitcast.elem_ref, f32[72,128]{1,0:T(8,128)S(1)} %collective-permute-done.2.from_up_ref, f32[72,128]{1,0:T(8,128)S(1)} %collective-permute-done.3.from_down_ref, f32[128,128]{1,0:T(8,128)S(1)} %bitcast.5, f32[8,384]{1,0:T(8,128)S(1)} %get-tuple-element.40.slot_level_ref, ...), custom_call_target="tpu_custom_call" | custom-call | tf_op jit(solution)/shard_map/final/pallas_call | solution.py:510
  (30 shorter events, 2.8 us)
Async XLA Ops:
  1.4 1.1 %copy-start = (bf16[3,512,256]{2,1,0:T(8,128)(2,1)S(1)}, bf16[3,512,256]{2,1,0:T(8,128)(2,1)}, u32[]{:S(2)}) copy-start(bf16[3,512,256]{2,1,0:T(8,128)(2,1)} %metric_hbm.1) | copy-start | bytes 2359300
  2.5 1.0 %copy-start.1 = (f32[512,256]{1,0:T(8,128)S(1)}, f32[512,256]{1,0:T(8,128)}, u32[]{:S(2)}) copy-start(f32[512,256]{1,0:T(8,128)} %nodal_hbm.1) | copy-start | bytes 1572868
  3.6 0.7 %copy-start.2 = (s32[8,256]{1,0:T(8,128)S(1)}, s32[8,256]{1,0:T(8,128)}, u32[]{:S(2)}) copy-start(s32[8,256]{1,0:T(8,128)} %vertex_ref.3) | copy-start | bytes 24580
  4.3 0.7 %copy-start.4 = (f32[2,8,8]{2,1,0:T(8,128)S(1)}, f32[2,8,8]{2,1,0:T(8,128)}, u32[]{:S(2)}) copy-start(f32[2,8,8]{2,1,0:T(8,128)} %interp_ref.3) | copy-start | bytes 1540
  7.1 0.8 %copy-start.6 = (f32[2,512,128]{2,1,0:T(8,128)}, f32[2,512,128]{2,1,0:T(8,128)S(1)}, u32[]{:S(2)}) copy-start(f32[2,512,128]{2,1,0:T(8,128)S(1)} %get-tuple-element.33.nodal_ref) | copy-start | bytes 1572868
  7.9 0.8 %copy-start.8 = (bf16[144,1536]{1,0:T(8,128)(2,1)}, bf16[144,1536]{1,0:T(8,128)(2,1)S(1)}, u32[]{:S(2)}) copy-start(bf16[144,1536]{1,0:T(8,128)(2,1)S(1)} %get-tuple-element.31.traces_ref) | copy-start | bytes 1327108
  8.7 17.9 %all-to-all-start = ((f32[8,16,128]{2,1,0:T(8,128)}), f32[8,16,128]{2,1,0:T(8,128)S(1)}, u32[]{:S(2)}, u32[]{:S(2)}) async-start(f32[8,16,128]{2,1,0:T(8,128)} %bitcast.1), calls=%async_computation | async-start | bytes 131072 | tf_op jit(solution)/shard_map/all_to_all | solution.py:426
  13.9 12.7 %collective-permute-start = (f32[64,128]{1,0:T(8,128)S(1)}, f32[64,128]{1,0:T(8,128)S(1)}, u32[]{:S(2)}, u32[]{:S(2)}) collective-permute-start(f32[64,128]{1,0:T(8,128)S(1)} %get-tuple-element.28), channel_id=1, source_target_pairs={{0,8},{8,16},{16,24},{24,0},{1,9},{9,17},{17,25},{25,1},{2,10},{10... | collective-permute-start | bytes 98312 | tf_op jit(solution)/shard_map/ppermute | solution.py:427
  15.5 11.1 %collective-permute-start.1 = (f32[64,128]{1,0:T(8,128)S(1)}, f32[64,128]{1,0:T(8,128)S(1)}, u32[]{:S(2)}, u32[]{:S(2)}) collective-permute-start(f32[64,128]{1,0:T(8,128)S(1)} %get-tuple-element.29), channel_id=1, source_target_pairs={{8,0},{16,8},{24,16},{0,24},{9,1},{17,9},{25,17},{1,25},{10,2},{18... | collective-permute-start | bytes 98312 | tf_op jit(solution)/shard_map/ppermute | solution.py:427
  18.4 1.0 %copy-start.7 = (f32[2,512,128]{2,1,0:T(8,128)S(1)}, f32[2,512,128]{2,1,0:T(8,128)}, u32[]{:S(2)}) copy-start(f32[2,512,128]{2,1,0:T(8,128)} %copy-done.6) | copy-start | bytes 1572868
  19.4 1.0 %copy-start.9 = (bf16[144,1536]{1,0:T(8,128)(2,1)S(1)}, bf16[144,1536]{1,0:T(8,128)(2,1)}, u32[]{:S(2)}) copy-start(bf16[144,1536]{1,0:T(8,128)(2,1)} %copy-done.8) | copy-start | bytes 1327108
  20.4 0.7 %copy-start.10 = (f32[8,8]{1,0:T(8,128)S(1)}, f32[8,8]{1,0:T(8,128)}, u32[]{:S(2)}) copy-start(f32[8,8]{1,0:T(8,128)} %derivative_ref.1) | copy-start | bytes 772
  21.1 14.5 %copy-start.5 = (f32[2,8,8]{2,1,0:T(8,128)S(1)}, f32[2,8,8]{2,1,0:T(8,128)}, u32[]{:S(2)}) copy-start(f32[2,8,8]{2,1,0:T(8,128)} %interp_ref.3) | copy-start | bytes 1540
  23.8 1.2 %copy-start.11 = (bf16[512,1536]{1,0:T(8,128)(2,1)}, bf16[512,1536]{1,0:T(8,128)(2,1)S(1)}, u32[]{:S(2)}) copy-start(bf16[512,1536]{1,0:T(8,128)(2,1)S(1)} %get-tuple-element.44.local_ref) | copy-start | bytes 4718596
  25.0 0.8 %copy-start.13 = (f32[512,256]{1,0:T(8,128)}, f32[512,256]{1,0:T(8,128)S(1)}, u32[]{:S(2)}) copy-start(f32[512,256]{1,0:T(8,128)S(1)} %get-tuple-element.45.stiff_ref) | copy-start | bytes 1572868
  25.8 0.8 %copy-start.15 = (bf16[384,512]{1,0:T(8,128)(2,1)}, bf16[384,512]{1,0:T(8,128)(2,1)S(1)}, u32[]{:S(2)}) copy-start(bf16[384,512]{1,0:T(8,128)(2,1)S(1)} %get-tuple-element.43.slot_hot_ref) | copy-start | bytes 1179652
  27.6 12.5 %all-to-all-start.1 = ((f32[8,16,128]{2,1,0:T(8,128)}), f32[8,16,128]{2,1,0:T(8,128)S(1)}, u32[]{:S(2)}, u32[]{:S(2)}) async-start(f32[8,16,128]{2,1,0:T(8,128)} %bitcast.3), calls=%async_computation.1 | async-start | bytes 131072 | tf_op jit(solution)/shard_map/all_to_all | solution.py:426
  31.8 8.3 %collective-permute-start.2 = (f32[72,128]{1,0:T(8,128)S(1)}, f32[72,128]{1,0:T(8,128)S(1)}, u32[]{:S(2)}, u32[]{:S(2)}) collective-permute-start(f32[72,128]{1,0:T(8,128)S(1)} %get-tuple-element.37), channel_id=1, source_target_pairs={{0,8},{8,16},{16,24},{24,0},{1,9},{9,17},{17,25},{25,1},{2,10},{10... | collective-permute-start | bytes 110600 | tf_op jit(solution)/shard_map/ppermute | solution.py:427
  31.8 8.3 %collective-permute-start.3 = (f32[72,128]{1,0:T(8,128)S(1)}, f32[72,128]{1,0:T(8,128)S(1)}, u32[]{:S(2)}, u32[]{:S(2)}) collective-permute-start(f32[72,128]{1,0:T(8,128)S(1)} %get-tuple-element.38), channel_id=1, source_target_pairs={{8,0},{16,8},{24,16},{0,24},{9,1},{17,9},{25,17},{1,25},{10,2},{18... | collective-permute-start | bytes 110600 | tf_op jit(solution)/shard_map/ppermute | solution.py:427
  35.6 1.4 %copy-start.12 = (bf16[512,1536]{1,0:T(8,128)(2,1)S(1)}, bf16[512,1536]{1,0:T(8,128)(2,1)}, u32[]{:S(2)}) copy-start(bf16[512,1536]{1,0:T(8,128)(2,1)} %copy-done.11) | copy-start | bytes 4718596
  37.0 1.0 %copy-start.14 = (f32[512,256]{1,0:T(8,128)S(1)}, f32[512,256]{1,0:T(8,128)}, u32[]{:S(2)}) copy-start(f32[512,256]{1,0:T(8,128)} %copy-done.13) | copy-start | bytes 1572868
  38.1 1.0 %copy-start.16 = (bf16[384,512]{1,0:T(8,128)(2,1)S(1)}, bf16[384,512]{1,0:T(8,128)(2,1)}, u32[]{:S(2)}) copy-start(bf16[384,512]{1,0:T(8,128)(2,1)} %copy-done.15) | copy-start | bytes 1179652
  39.1 1.0 %copy-start.3 = (s32[8,256]{1,0:T(8,128)S(1)}, s32[8,256]{1,0:T(8,128)}, u32[]{:S(2)}) copy-start(s32[8,256]{1,0:T(8,128)} %vertex_ref.3) | copy-start | bytes 24580

commit v2 on v1

--- a/solution.py
+++ b/solution.py
@@ -119,9 +119,28 @@
     return (iota((count, ids.shape[1]), 0) + first == ids).astype(f32).astype(bf16)
 
 
+def columns_of(row):
+    return jnp.broadcast_to(row, (LANES, row.shape[1])).T
+
+
+def one_hot_lanes(columns, first, count):
+    lane = iota((columns.shape[0], LANES), 1) + first
+    blocks = [columns == lane + start for start in range(0, count, LANES)]
+    return jnp.concatenate([block.astype(f32).astype(bf16) for block in blocks], axis=1)
+
+
 def window_ids(vertex_ids, elem_index, total):
     shifted = vertex_ids - elem_index * NV_DEV
-    return jnp.where(shifted < 0, shifted + total, shifted)
+    window = jnp.where(shifted < 0, shifted + total, shifted)
+    return window // HALF, window % HALF
+
+
+def low_one_hot(low_id):
+    parts = []
+    for corner in range(8):
+        hot = one_hot_rows(low_id[corner : corner + 1], 0, HALF)
+        parts.append(jnp.concatenate([jnp.zeros_like(hot), hot], axis=0))
+    return jnp.concatenate(parts, axis=1)
 
 
 def corner_row(corner):
@@ -133,47 +152,60 @@
     total_vertices,
     elem_ref,
     nodal_hbm,
-    metric_hbm,
+    level_hbm,
+    target_hbm,
+    slot_hbm,
+    interp_hbm,
+    derivative_hbm,
+    vertex_hbm,
+    down_ref,
+    up_ref,
+    group_hbm,
+    traces_ref,
+    columns_ref,
+    slot_level_ref,
+    maps_ref,
     level_ref,
     target_ref,
+    slot_mortar_ref,
     interp_ref,
+    derivative_ref,
     vertex_ref,
-    down_ref,
-    up_ref,
+    nodal_ref,
     group_ref,
-    nodal_ref,
-    metric_ref,
-    traces_ref,
-    remote_ref,
-    slot_level_ref,
-    maps_ref,
-    low_ids_ref,
+    nodal_sems,
     sems,
 ):
-    nodal_copies = lane_copies(nodal_hbm, nodal_ref, sems, False)
-    metric_copy = pltpu.make_async_copy(metric_hbm, metric_ref, sems.at[len(nodal_copies)])
+    target_copy = pltpu.make_async_copy(target_hbm, target_ref.at[0], sems.at[0])
+    level_copy = pltpu.make_async_copy(level_hbm, level_ref.at[0], sems.at[1])
+    interp_copy = pltpu.make_async_copy(interp_hbm, interp_ref, sems.at[2])
+    vertex_copy = pltpu.make_async_copy(vertex_hbm, vertex_ref, sems.at[3])
+    slot_copy = pltpu.make_async_copy(slot_hbm, slot_mortar_ref.at[0], sems.at[4])
+    derivative_copy = pltpu.make_async_copy(derivative_hbm, derivative_ref, sems.at[5])
+    nodal_copies = lane_copies(nodal_hbm, nodal_ref, nodal_sems, False)
+    target_copy.start()
+    interp_copy.start()
     for copy in nodal_copies:
         copy.start()
-    metric_copy.start()
-    slots = remote_ref.shape[0]
+    for copy in (level_copy, vertex_copy, slot_copy, derivative_copy):
+        copy.start()
+    slots = slot_level_ref.shape[1]
     elems = nodal_hbm.shape[1]
-    level = level_ref[...]
-    remote_ref[...] = one_hot_rows(target_ref[...], M_DEV, slots)
+    target_copy.wait()
+    columns = columns_of(target_ref[...])
+    columns_ref[...] = columns
+    remote = one_hot_lanes(columns, M_DEV, -(-slots // 256) * 256)
+    interp_copy.wait()
     maps = kron_four(interp_ref[0], interp_ref[1])
     maps_ref[...] = maps
-    window = window_ids(vertex_ref[...], elem_ref[0], total_vertices)
-    high_id = window // HALF
-    low_id = window % HALF
-    zeros = jnp.zeros((HALF, elems), bf16)
-    low_hot = []
-    for corner in range(8):
-        hot = one_hot_rows(low_id[corner : corner + 1], 0, HALF)
-        low_hot.append(jnp.concatenate([zeros, hot], axis=0))
-    low_hot = jnp.concatenate(low_hot, axis=1)
-    low_ids_ref[...] = low_hot
+    vertex_copy.wait()
+    high_id, low_id = window_ids(vertex_ref[...], elem_ref[0], total_vertices)
+    low_hot = low_one_hot(low_id)
 
     for copy in nodal_copies:
         copy.wait()
+    level_copy.wait()
+    level = level_ref[...]
     faces = [
         load_rows(nodal_ref, pl.ds(0, SQ)),
         load_rows(nodal_ref, pl.ds(7 * SQ, SQ)),
@@ -188,15 +220,12 @@
     traces_ref[SQ : 2 * SQ, :] = lo
     traces_ref[2 * SQ :, :] = jnp.broadcast_to(level, (16, level.shape[1])).astype(f32).astype(bf16)
 
-    picked = mm_nt(traces_ref[...], remote_ref[...])
+    picked = mm(traces_ref[...], remote)[:, 0:slots]
     plain = picked[0:SQ] + picked[SQ : 2 * SQ]
     slot_level = picked[2 * SQ : 2 * SQ + 8]
     slot_level_ref[...] = slot_level
     mapped = mm(maps, stack3(plain))
     sent = pick_level(plain, mapped, slot_level[0:1])
-    down_ref[...] = sent[:, 0:CAP_E]
-    up_ref[...] = sent[:, CAP_E : 2 * CAP_E]
-
     row = iota((16, elems), 0)
     row_high = row % 4 + 4 * (row // 8)
     is_count = row // 4 % 2 == 1
@@ -214,78 +243,101 @@
     group = sent[:, 2 * CAP_E :]
     group = jnp.concatenate([group, jnp.zeros_like(group)], axis=0).T
     group_ref[...] = group + jnp.concatenate([sums] * (group.shape[0] // 16), axis=0)
-    metric_copy.wait()
+    group_copy = pltpu.make_async_copy(group_ref, group_hbm, sems.at[6])
+    group_copy.start()
+    down_ref[...] = sent[:, 0:CAP_E]
+    up_ref[...] = sent[:, CAP_E : 2 * CAP_E]
+    slot_copy.wait()
+    derivative_copy.wait()
+    group_copy.wait()
+
+
+def stiffness_maps(matrix):
+    row = iota((SQ, 3 * SQ), 0)
+    lane = iota((SQ, 3 * SQ), 1) % SQ
+    first, second = expand(matrix, 3)
+    outer = jnp.where(row % 8 == lane % 8, first, 0.0)
+    inner = jnp.where(row // 8 == lane // 8, second, 0.0)
+    return hi_hi_lo(outer), hi_hi_lo(inner)
 
 
 def local_kernel(
+    nodal_hbm,
+    metric_hbm,
     traces_ref,
     maps_ref,
     level_ref,
-    target_ref,
+    columns_ref,
     slot_mortar_ref,
-    nodal_ref,
-    metric_ref,
+    interp_ref,
     derivative_ref,
     mortar_ref,
     answers_ref,
     equal_ref,
-    local_ref,
-    slot_hot_ref,
     stiff_ref,
+    back_maps_ref,
+    grad_map_ref,
+    div_map_ref,
+    nodal_ref,
+    metric_ref,
     by_row,
-    by_col,
+    nodal_sems,
+    sem,
 ):
+    nodal_copies = lane_copies(nodal_hbm, nodal_ref, nodal_sems, False)
+    metric_copy = pltpu.make_async_copy(metric_hbm.at[0], metric_ref, sem)
+    for copy in nodal_copies:
+        copy.start()
+    metric_copy.start()
     hi = traces_ref[0:SQ, :]
     lo = traces_ref[SQ : 2 * SQ, :]
     plain = hi.astype(f32) + lo.astype(f32)
     mapped = mm(maps_ref[...], jnp.concatenate([hi, lo, hi], axis=0))
     projected = pick_level(plain, mapped, level_ref[...])
-    local_ref[...] = one_hot_rows(target_ref[...], 0, M_DEV)
-    mortar = mm_nt(stack2(projected), local_ref[...])
+    mortar = mm(stack2(projected), one_hot_lanes(columns_ref[...], 0, M_DEV))
     mortar = mortar[0:SQ] + mortar[SQ:]
     mortar_ref[...] = mortar
     slot_row = slot_mortar_ref[...]
-    slots = slot_row.shape[1]
-    slot_hot_t = one_hot_rows(slot_row, 0, M_DEV)
-    answers = mm(stack2(mortar), slot_hot_t)
+    answers = mm(stack2(mortar), one_hot_rows(slot_row, 0, M_DEV))
     answers_ref[...] = answers[0:SQ] + answers[SQ:]
-    slot_col = jnp.broadcast_to(slot_row, (128, slots)).T[:, 0:1]
-    equal_ref[...] = (slot_col == slot_row).astype(f32).astype(bf16)
-    slot_hot_ref[...] = (slot_col == iota((slots, M_DEV), 1)).astype(f32).astype(bf16)
-    stiffness(nodal_ref, metric_ref, derivative_ref, stiff_ref, by_row, by_col)
-
-
-def stiffness(nodal_ref, metric_ref, derivative_ref, stiff_ref, by_row, by_col):
-    derivative = derivative_ref[...]
-    row = iota((SQ, 3 * SQ), 0)
-    lane = iota((SQ, 3 * SQ), 1) % SQ
-
-    def pair(matrix):
-        first, second = expand(matrix, 3)
-        outer = jnp.where(row % 8 == lane % 8, first, 0.0)
-        inner = jnp.where(row // 8 == lane // 8, second, 0.0)
-        return hi_hi_lo(outer), hi_hi_lo(inner)
-
-    outer, inner = pair(derivative)
-    outer_t, inner_t = pair(derivative.T)
-    both = jnp.concatenate([outer, inner], axis=0)
+    equal_ref[...] = (columns_of(slot_row)[:, 0:1] == slot_row).astype(f32).astype(bf16)
+
+    back_maps_ref[...] = kron_four(interp_ref[0].T, interp_ref[1].T)
+    outer, inner = stiffness_maps(derivative_ref[...])
+    outer_t, inner_t = stiffness_maps(derivative_ref[...].T)
+    grad_map_ref[0:SQ, :] = outer
+    grad_map_ref[SQ:, :] = inner
+    div_map_ref[...] = jnp.concatenate([outer_t, inner_t], axis=1)
+    for copy in nodal_copies:
+        copy.wait()
+    metric_copy.wait()
+    first_direction(nodal_ref, metric_ref, outer, outer_t, stiff_ref, by_row)
+
+
+def first_direction(nodal_ref, metric_ref, outer, outer_t, stiff_ref, by_row):
     for i in range(8):
-        slab = load_rows(nodal_ref, pl.ds(i * SQ, SQ))
-        grad = mm(outer, stack3(slab))
-        weighted = grad * metric_ref[1, i * SQ : (i + 1) * SQ, :].astype(f32)
-        stiff_ref[i * SQ : (i + 1) * SQ, :] = mm(outer_t, stack3(weighted))
-        by_row[i * SQ : (i + 1) * SQ, :] = metric_ref[0, i * SQ : (i + 1) * SQ, :].astype(f32)
-        by_col[i * SQ : (i + 1) * SQ, :] = metric_ref[2, i * SQ : (i + 1) * SQ, :].astype(f32)
-
-    def comb(ref, j):
-        return jnp.concatenate([ref[i * SQ + j * 8 : i * SQ + j * 8 + 8, :] for i in range(8)], axis=0)
-
+        by_row[i * SQ : (i + 1) * SQ, :] = metric_ref[i * SQ : (i + 1) * SQ, :].astype(f32)
+    grads = [mm(outer, stack3(load_comb(nodal_ref, j))) for j in range(8)]
+    weighted = []
     for j in range(8):
-        grad = mm(both, stack3(load_comb(nodal_ref, j)))
-        out = mm(outer_t, stack3(grad[0:SQ] * comb(by_row, j)))
-        out = out + mm(inner_t, stack3(grad[SQ:] * comb(by_col, j)))
+        factor = [by_row[i * SQ + j * 8 : i * SQ + j * 8 + 8, :] for i in range(8)]
+        weighted.append(stack3(grads[j] * jnp.concatenate(factor, axis=0)))
+    for j in range(8):
+        out = mm(outer_t, weighted[j])
         for i in range(8):
-            stiff_ref[i * SQ + j * 8 : i * SQ + j * 8 + 8, :] += out[i * 8 : i * 8 + 8]
+            stiff_ref[i * SQ + j * 8 : i * SQ + j * 8 + 8, :] = out[i * 8 : i * 8 + 8]
+
+
+def other_directions(nodal_ref, metric_ref, grad_map, div_map, stiff_ref, result_ref):
+    slabs = [pl.ds(i * SQ, SQ) for i in range(8)]
+    grads = [mm(grad_map, stack3(load_rows(nodal_ref, slab))) for slab in slabs]
+    weighted = []
+    for slab, grad in zip(slabs, grads):
+        second = stack3(grad[0:SQ] * metric_ref[0, slab, :].astype(f32))
+        third = stack3(grad[SQ:] * metric_ref[1, slab, :].astype(f32))
+        weighted.append(jnp.concatenate([second, third], axis=0))
+    for slab, part in zip(slabs, weighted):
+        store_rows(result_ref, slab, stiff_ref[slab, :] + mm(div_map, part))
 
 
 def answer_kernel(
@@ -296,15 +348,21 @@
     local_answers_ref,
     down_ref,
     up_ref,
-    group_out_ref,
+    group_hbm,
     incoming_ref,
     sums_ref,
+    group_out_ref,
+    sem,
 ):
     group_in = group_ref[...]
     incoming = jnp.concatenate([from_up_ref[...], from_down_ref[...], group_in.T[0:SQ]], axis=1)
     incoming_ref[...] = incoming
     added = mm(stack2(incoming), equal_ref[...])
     answers = local_answers_ref[...] + added[0:SQ] + added[SQ:]
+    group = answers[:, 2 * CAP_E :]
+    group_out_ref[...] = jnp.concatenate([group, jnp.zeros_like(group)], axis=0).T
+    group_copy = pltpu.make_async_copy(group_out_ref, group_hbm, sem)
+    group_copy.start()
     sums = group_in[0:16]
     for block in range(1, group_in.shape[0] // 16):
         sums = sums + group_in[block * 16 : block * 16 + 16]
@@ -313,29 +371,55 @@
     up_ref[0:SQ, :] = answers[:, CAP_E : 2 * CAP_E]
     down_ref[SQ:, :] = sums[0:8]
     up_ref[SQ:, :] = sums[8:16]
-    group = answers[:, 2 * CAP_E :]
-    group_out_ref[...] = jnp.concatenate([group, jnp.zeros_like(group)], axis=0).T
+    group_copy.wait()
 
 
 def gather_kernel(
+    total_vertices,
+    elem_ref,
+    nodal_hbm,
+    metric_hbm,
     mortar_ref,
     incoming_ref,
-    slot_hot_ref,
-    local_ref,
+    slot_mortar_ref,
+    target_ref,
     level_ref,
-    interp_ref,
+    back_maps_ref,
+    grad_map_ref,
+    div_map_ref,
+    vertex_ref,
     stiff_ref,
     result_ref,
-    maps_ref,
+    remote_ref,
+    low_ids_ref,
+    high_ids_ref,
+    nodal_ref,
+    metric_ref,
+    nodal_sems,
+    sem,
 ):
-    added = mm(stack2(incoming_ref[...]), slot_hot_ref[...])
+    nodal_copies = lane_copies(nodal_hbm, nodal_ref, nodal_sems, False)
+    metric_copy = pltpu.make_async_copy(metric_hbm.at[1:3], metric_ref, sem)
+    for copy in nodal_copies:
+        copy.start()
+    metric_copy.start()
+    slot_hot = one_hot_lanes(columns_of(slot_mortar_ref[...]), 0, M_DEV)
+    added = mm(stack2(incoming_ref[...]), slot_hot)
     mortar = mortar_ref[...] + added[0:SQ] + added[SQ:]
-    picked = mm(stack2(mortar), local_ref[...])
+    target = target_ref[...]
+    picked = mm(stack2(mortar), one_hot_rows(target, 0, M_DEV))
     picked = picked[0:SQ] + picked[SQ:]
-    maps = kron_four(interp_ref[0].T, interp_ref[1].T)
-    maps_ref[...] = maps
-    back = pick_level(picked, mm(maps, stack3(picked)), level_ref[...])
-    store_rows(result_ref, slice(None), stiff_ref[...])
+    back = pick_level(picked, mm(back_maps_ref[...], stack3(picked)), level_ref[...])
+    remote_ref[...] = one_hot_rows(target, M_DEV, remote_ref.shape[0])
+    high_id, low_id = window_ids(vertex_ref[...], elem_ref[0], total_vertices)
+    high_ids_ref[...] = high_id
+    low_ids_ref[...] = low_one_hot(low_id)
+    for copy in nodal_copies:
+        copy.wait()
+    metric_copy.wait()
+    other_directions(
+        nodal_ref, metric_ref, grad_map_ref[...], div_map_ref[...], stiff_ref, result_ref
+    )
     add_faces(result_ref, back)
 
 
@@ -352,8 +436,6 @@
 
 
 def final_kernel(
-    total_vertices,
-    elem_ref,
     from_up_ref,
     from_down_ref,
     group_ref,
@@ -361,7 +443,7 @@
     maps_ref,
     remote_ref,
     sums_ref,
-    vertex_ref,
+    high_ids_ref,
     low_ids_ref,
     result_ref,
     out_hbm,
@@ -384,7 +466,7 @@
     table = jnp.concatenate([coarse_hi, coarse - coarse_hi], axis=0).astype(bf16)
     found = mm(table, low_ids_ref[...])
     found = found[0:8] + found[8:16]
-    high_id = window_ids(vertex_ref[...], elem_ref[0], total_vertices) // HALF
+    high_id = high_ids_ref[...]
 
     out_ref[...] = result_ref[...]
     add_faces(out_ref, back)
@@ -431,102 +513,129 @@
     elems = nodal.shape[1]
     faces = face_level.shape[0]
     slots = slot_mortar.shape[0]
+    blocked = (elems // LANES, nodal.shape[0], LANES)
     total_vertices = NV_DEV * lax.axis_size("elem")
     elem_index = lax.axis_index("elem").astype(jnp.int32).reshape(1)
-    level = face_level.reshape(1, faces)
-    target = face_target.reshape(1, faces)
-    slot_row = slot_mortar.reshape(1, slots)
-    blocked = (elems // LANES, nodal.shape[0], LANES)
     group_slots = slots - 2 * CAP_E
-
-    down, up, group, nodal_in, metric_in, traces, remote, slot_level, maps, low_ids = pl.pallas_call(
+    nodal, metric, derivative, interp, face_level, face_target, slot_mortar, vertex_ids = (
+        pltpu.with_memory_space_constraint(array, pltpu.HBM)
+        for array in (
+            nodal, metric, derivative, interp, face_level, face_target, slot_mortar, vertex_ids
+        )
+    )
+    maps_shape = pltpu.VMEM((4 * SQ, 3 * SQ), bf16)
+
+    (
+        down, up, group, traces, columns, slot_level, maps,
+        level, target, slot_row, interp_in, derivative_in, vertex_in,
+    ) = pl.pallas_call(
         functools.partial(send_kernel, total_vertices),
-        in_specs=[SMEM, HBM, HBM] + [VMEM] * 4,
-        out_specs=[VMEM] * 10,
+        in_specs=[SMEM] + [HBM] * 7,
+        out_specs=[VMEM, VMEM, HBM] + [VMEM] * 10,
         out_shape=[
             pltpu.VMEM((SQ, CAP_E), f32),
             pltpu.VMEM((SQ, CAP_E), f32),
-            pltpu.VMEM((group_slots, 128), f32),
+            jax.ShapeDtypeStruct((group_slots, LANES), f32),
+            pltpu.VMEM((2 * SQ + 16, faces), bf16),
+            pltpu.VMEM((faces, LANES), jnp.int32),
+            pltpu.VMEM((8, slots), f32),
+            maps_shape,
+            pltpu.VMEM((1, faces), jnp.int32),
+            pltpu.VMEM((1, faces), jnp.int32),
+            pltpu.VMEM((1, slots), jnp.int32),
+            pltpu.VMEM(interp.shape, f32),
+            pltpu.VMEM(derivative.shape, f32),
+            pltpu.VMEM(vertex_ids.shape, jnp.int32),
+        ],
+        scratch_shapes=[
             pltpu.VMEM(blocked, f32),
-            pltpu.VMEM(metric.shape, bf16),
-            pltpu.VMEM((2 * SQ + 16, faces), bf16),
-            pltpu.VMEM((slots, faces), bf16),
-            pltpu.VMEM((8, slots), f32),
-            pltpu.VMEM((4 * SQ, 3 * SQ), bf16),
-            pltpu.VMEM((2 * HALF, 8 * elems), bf16),
+            pltpu.VMEM((group_slots, LANES), f32),
+            pltpu.SemaphoreType.DMA((blocked[0],)),
+            pltpu.SemaphoreType.DMA((7,)),
         ],
-        scratch_shapes=[pltpu.SemaphoreType.DMA((blocked[0] + 1,))],
         compiler_params=params(16),
         name="send",
-    )(elem_index, nodal, metric, level, target, interp, vertex_ids)
+    )(elem_index, nodal, face_level, face_target, slot_mortar, interp, derivative, vertex_ids)
 
     from_up, from_down, group_in = exchange(down, up, group)
 
-    mortar, local_answers, equal, local, slot_hot, stiff = pl.pallas_call(
+    mortar, local_answers, equal, stiff, back_maps, grad_map, div_map = pl.pallas_call(
         local_kernel,
-        in_specs=[VMEM] * 8,
-        out_specs=[VMEM] * 6,
+        in_specs=[HBM, HBM] + [VMEM] * 7,
+        out_specs=[VMEM] * 7,
         out_shape=[
             pltpu.VMEM((SQ, M_DEV), f32),
             pltpu.VMEM((SQ, slots), f32),
             pltpu.VMEM((slots, slots), bf16),
-            pltpu.VMEM((M_DEV, faces), bf16),
-            pltpu.VMEM((slots, M_DEV), bf16),
             pltpu.VMEM(nodal.shape, f32),
+            maps_shape,
+            pltpu.VMEM((2 * SQ, 3 * SQ), bf16),
+            pltpu.VMEM((SQ, 6 * SQ), bf16),
         ],
-        scratch_shapes=[pltpu.VMEM(nodal.shape, f32), pltpu.VMEM(nodal.shape, f32)],
+        scratch_shapes=[
+            pltpu.VMEM(blocked, f32),
+            pltpu.VMEM(nodal.shape, bf16),
+            pltpu.VMEM(nodal.shape, f32),
+            pltpu.SemaphoreType.DMA((blocked[0],)),
+            pltpu.SemaphoreType.DMA,
+        ],
         compiler_params=params(16),
         cost_estimate=cost(3),
         name="local",
-    )(traces, maps, level, target, slot_row, nodal_in, metric_in, derivative)
+    )(nodal, metric, traces, maps, level, columns, slot_row, interp_in, derivative_in)
 
     down, up, group, incoming, sums = pl.pallas_call(
         answer_kernel,
         in_specs=[VMEM] * 5,
-        out_specs=[VMEM] * 5,
+        out_specs=[VMEM, VMEM, HBM, VMEM, VMEM],
         out_shape=[
             pltpu.VMEM((SQ + 8, CAP_E), f32),
             pltpu.VMEM((SQ + 8, CAP_E), f32),
-            pltpu.VMEM((group_slots, 128), f32),
+            jax.ShapeDtypeStruct((group_slots, LANES), f32),
             pltpu.VMEM((SQ, slots), f32),
-            pltpu.VMEM((16, 128), f32),
+            pltpu.VMEM((16, LANES), f32),
         ],
+        scratch_shapes=[pltpu.VMEM((group_slots, LANES), f32), pltpu.SemaphoreType.DMA],
         compiler_params=params(16),
         name="answer",
     )(from_up, from_down, group_in, equal, local_answers)
 
     from_up, from_down, group_in = exchange(down, up, group)
 
-    result, back_maps = pl.pallas_call(
-        gather_kernel,
-        in_specs=[VMEM] * 7,
-        out_specs=[VMEM] * 2,
-        out_shape=[pltpu.VMEM(blocked, f32), pltpu.VMEM((4 * SQ, 3 * SQ), bf16)],
+    result, remote, low_ids, high_ids = pl.pallas_call(
+        functools.partial(gather_kernel, total_vertices),
+        in_specs=[SMEM, HBM, HBM] + [VMEM] * 10,
+        out_specs=[VMEM] * 4,
+        out_shape=[
+            pltpu.VMEM(blocked, f32),
+            pltpu.VMEM((slots, faces), bf16),
+            pltpu.VMEM((2 * HALF, 8 * elems), bf16),
+            pltpu.VMEM((8, elems), jnp.int32),
+        ],
+        scratch_shapes=[
+            pltpu.VMEM(blocked, f32),
+            pltpu.VMEM((2,) + nodal.shape, bf16),
+            pltpu.SemaphoreType.DMA((blocked[0],)),
+            pltpu.SemaphoreType.DMA,
+        ],
         compiler_params=params(16),
-        cost_estimate=cost(2),
+        cost_estimate=cost(3),
         name="gather",
-    )(mortar, incoming, slot_hot, local, level, interp, stiff)
+    )(
+        elem_index, nodal, metric, mortar, incoming, slot_row, target, level, back_maps,
+        grad_map, div_map, vertex_in, stiff,
+    )
 
     return pl.pallas_call(
-        functools.partial(final_kernel, total_vertices),
-        in_specs=[SMEM] + [VMEM] * 10,
+        final_kernel,
+        in_specs=[VMEM] * 10,
         out_specs=HBM,
         out_shape=jax.ShapeDtypeStruct(nodal.shape, f32),
         scratch_shapes=[pltpu.VMEM(blocked, f32), pltpu.SemaphoreType.DMA((blocked[0],))],
         compiler_params=params(16),
         name="final",
     )(
-        elem_index,
-        from_up,
-        from_down,
-        group_in,
-        slot_level,
-        back_maps,
-        remote,
-        sums,
-        vertex_ids,
-        low_ids,
-        result,
+        from_up, from_down, group_in, slot_level, back_maps, remote, sums, high_ids, low_ids, result
     )
 
 

time: 42.4 us -> 27.5 us (0.65); the launches traced: 41.6 us -> 27.1 us
  local copies, waits for them, and re-layouts: 16.2 us -> 0 us
  Pallas kernels: 8.29 us -> 9.98 us
    unnamed x34 -> x0, local copies, waits for them, and re-layouts: 14.1 us -> none
    reshape x3 -> x0, local copies, waits for them, and re-layouts: 2.08 us -> none  [the longest x1 0.7 us: on_device(): level = face_level.reshape(1, faces)]
    pallas_call x4, Pallas kernels: 6.13 us -> 7.27 us  [the longest x1 2.64 us: on_device(): pl.pallas_call(local_kernel, in_specs=[HBM, HBM] + [VMEM] * 7, out_specs=...]
    pallas_call x1, Pallas kernels: 2.16 us -> 2.72 us  [on_device(): pl.pallas_call(functools.partial(send_kernel, total_vertices), in_specs=[...]
    ppermute x2, starting transfers between devices: 1.58 us -> 2.14 us  [exchange(): lax.ppermute(up, 'elem', up_pairs)]
    ppermute x2, starting transfers between devices: 6.06 us -> 5.51 us  [exchange(): lax.ppermute(down, 'elem', down_pairs)]
  transfers between devices with their start and end apart: 6 -> 6, of which waited for: 0 -> 0; matrix products, arithmetic and copies ran while one was open for 2% -> 0% of each run, Pallas kernels for 9% -> 18%
where the time goes in v2:
time: 27.5 us; the launch traced here: 27.1 us
  starting transfers between devices  17 us (62%)
  Pallas kernels  9.98 us (36%)
    all_to_all x2, starting transfers between devices, exchange(): lax.all_to_all(group, 'clus', split_axis=0, concat_axis=0, tiled=True)  9.4 us
    ppermute x2, starting transfers between devices, exchange(): lax.ppermute(down, 'elem', down_pairs)  5.51 us
    pallas_call x1, Pallas kernels, on_device(): pl.pallas_call(functools.partial(send_kernel, total_vertices), in_specs=[...  2.72 us
    pallas_call x1, Pallas kernels, on_device(): pl.pallas_call(local_kernel, in_specs=[HBM, HBM] + [VMEM] * 7, out_specs=...  2.64 us
    pallas_call x1, Pallas kernels, on_device(): pl.pallas_call(functools.partial(gather_kernel, total_vertices), in_specs...  2.18 us
    ppermute x2, starting transfers between devices, exchange(): lax.ppermute(up, 'elem', up_pairs)  2.14 us
    pallas_call x1, Pallas kernels, on_device(): pl.pallas_call(final_kernel, in_specs=[VMEM] * 10, out_specs=HBM, out_sha...  1.45 us
    pallas_call x1, Pallas kernels, on_device(): pl.pallas_call(answer_kernel, in_specs=[VMEM] * 5, out_specs=[VMEM, VMEM,...  0.99 us
  transfers between devices with their start and end apart: 6, of which 0 were waited for; matrix products, arithmetic and copies ran while one was open for 0% of the time, Pallas kernels for 18%

profile of v2, /device:TPU:0, one launch (start us, length us, event | category | flops | bytes accessed | tf_op | source)
XLA Modules:
  0.0 27.1 jit_solution(14627847752775244709)
XLA Ops:
  0.0 2.7 %send.1 = (f32[64,128]{1,0:T(8,128)S(1)}, f32[64,128]{1,0:T(8,128)S(1)}, f32[128,128]{1,0:T(8,128)}, bf16[144,1536]{1,0:T(8,128)(2,1)S(1)}, s32[1536,128]{1,0:T(...) custom-call(s32[1]{0:T(128)} %bitcast.elem_ref, ...), custom_call_target="tpu_custom_call" | custom-call | tf_op jit(solution)/shard_map/send/pallas_call | solution.py:531
  2.7 5.2 %all-to-all-start = ((f32[8,16,128]{2,1,0:T(8,128)}), f32[8,16,128]{2,1,0:T(8,128)S(1)}, u32[]{:S(2)}, u32[]{:S(2)}) async-start(f32[8,16,128]{2,1,0:T(8,128)} %bitcast.1), calls=%async_computation | async-start | bytes 131072 | tf_op jit(solution)/shard_map/all_to_all | solution.py:508
  7.9 1.6 %collective-permute-start = (f32[64,128]{1,0:T(8,128)S(1)}, f32[64,128]{1,0:T(8,128)S(1)}, u32[]{:S(2)}, u32[]{:S(2)}) collective-permute-start(f32[64,128]{1,0:T(8,128)S(1)} %get-tuple-element.34), channel_id=1, source_target_pairs={{0,8},{8,16},{16,24},{24,0},{1,9},{9,17},{17,25},{25,1},{2,10},{10... | collective-permute-start | bytes 98312 | tf_op jit(solution)/shard_map/ppermute | solution.py:509
  9.5 2.2 %collective-permute-start.1 = (f32[64,128]{1,0:T(8,128)S(1)}, f32[64,128]{1,0:T(8,128)S(1)}, u32[]{:S(2)}, u32[]{:S(2)}) collective-permute-start(f32[64,128]{1,0:T(8,128)S(1)} %get-tuple-element.35), channel_id=1, source_target_pairs={{8,0},{16,8},{24,16},{0,24},{9,1},{17,9},{25,17},{1,25},{10,2},{18... | collective-permute-start | bytes 98312 | tf_op jit(solution)/shard_map/ppermute | solution.py:509
  11.7 2.6 %local.1 = (f32[64,512]{1,0:T(8,128)S(1)}, f32[64,384]{1,0:T(8,128)S(1)}, bf16[384,384]{1,0:T(8,128)(2,1)S(1)}, f32[512,256]{1,0:T(8,128)S(1)}, bf16[256,192]{1,...) custom-call(f32[512,256]{1,0:T(8,128)} %nodal_hbm.5, bf16[3,512,256]{2,1,0:T(8,128)(2,1)} %metric_hbm.3, ...), custom_call_target="tpu_custom_call" | custom-call | flops 1500000000 | bytes 6000000 | tf_op jit(solution)/shard_map/local/pallas_call | solution.py:562
  14.4 0.0 collective-permute-done.from_up_ref
  14.4 0.0 collective-permute-done.1.from_down_ref
  14.4 0.0 all-to-all-done
  14.4 1.0 %answer.1 = (f32[72,128]{1,0:T(8,128)S(1)}, f32[72,128]{1,0:T(8,128)S(1)}, f32[128,128]{1,0:T(8,128)}, f32[64,384]{1,0:T(8,128)S(1)}, f32[16,128]{1,0:T(8,128)S(1)}) custom-call(f32[64,128]{1,0:T(8,128)S(1)} %collective-permute-done.from_up_ref, f32[64,128]{1,0:T(8,128)S(1)} %collective-permute-done.1.from_down_ref, f32[128,128]{1,0:T(8,128)S(1)} %bitcast.6, ...), custom_call_target="tpu_custom_call" | custom-call | tf_op jit(solution)/shard_map/answer/pallas_call | solution.py:587
  15.4 4.2 %all-to-all-start.1 = ((f32[8,16,128]{2,1,0:T(8,128)}), f32[8,16,128]{2,1,0:T(8,128)S(1)}, u32[]{:S(2)}, u32[]{:S(2)}) async-start(f32[8,16,128]{2,1,0:T(8,128)} %bitcast.3), calls=%async_computation.1 | async-start | bytes 131072 | tf_op jit(solution)/shard_map/all_to_all | solution.py:508
  19.6 0.6 %collective-permute-start.2 = (f32[72,128]{1,0:T(8,128)S(1)}, f32[72,128]{1,0:T(8,128)S(1)}, u32[]{:S(2)}, u32[]{:S(2)}) collective-permute-start(f32[72,128]{1,0:T(8,128)S(1)} %get-tuple-element.46), channel_id=1, source_target_pairs={{0,8},{8,16},{16,24},{24,0},{1,9},{9,17},{17,25},{25,1},{2,10},{10... | collective-permute-start | bytes 110600 | tf_op jit(solution)/shard_map/ppermute | solution.py:509
  20.2 3.3 %collective-permute-start.3 = (f32[72,128]{1,0:T(8,128)S(1)}, f32[72,128]{1,0:T(8,128)S(1)}, u32[]{:S(2)}, u32[]{:S(2)}) collective-permute-start(f32[72,128]{1,0:T(8,128)S(1)} %get-tuple-element.47), channel_id=1, source_target_pairs={{8,0},{16,8},{24,16},{0,24},{9,1},{17,9},{25,17},{1,25},{10,2},{18... | collective-permute-start | bytes 110600 | tf_op jit(solution)/shard_map/ppermute | solution.py:509
  23.5 2.2 %gather.1 = (f32[2,512,128]{2,1,0:T(8,128)S(1)}, bf16[384,1536]{1,0:T(8,128)(2,1)S(1)}, bf16[128,2048]{1,0:T(8,128)(2,1)S(1)}, s32[8,256]{1,0:T(8,128)S(1)}) custom-call(s32[1]{0:T(128)} %bitcast.elem_ref, f32[512,256]{1,0:T(8,128)} %nodal_hbm.5, bf16[3,512,256]{2,1,0:T(8,128)(2,1)} %metric_hbm.3, f32[64,512]{1,0:T(8,128)S(1)} %get-tuple-element.51.mortar_ref, ...), custom_call_target="tpu_custom_call" | custom-call | flops 1500000000 | bytes 6000000 | tf_op jit(solution)/shard_map/gather/pallas_call | solution.py:605
  25.6 0.0 collective-permute-done.2.from_up_ref
  25.7 0.0 collective-permute-done.3.from_down_ref
  25.7 0.0 all-to-all-done.1
  25.7 1.5 %final.1 = f32[512,256]{1,0:T(8,128)} custom-call(f32[72,128]{1,0:T(8,128)S(1)} %collective-permute-done.2.from_up_ref, f32[72,128]{1,0:T(8,128)S(1)} %collective-permute-done.3.from_down_ref, f32[128,128]{1,0:T(8,128)S(1)} %bitcast.5, f32[8,384]{1,0:T(8,128)S(1)} %get-tuple-element.49.slot_level_ref, ...), custom_call_target="tpu_custom_call" | custom-call | tf_op jit(solution)/shard_map/final/pallas_call | solution.py:629
Async XLA Ops:
  2.7 11.7 %all-to-all-start = ((f32[8,16,128]{2,1,0:T(8,128)}), f32[8,16,128]{2,1,0:T(8,128)S(1)}, u32[]{:S(2)}, u32[]{:S(2)}) async-start(f32[8,16,128]{2,1,0:T(8,128)} %bitcast.1), calls=%async_computation | async-start | bytes 131072 | tf_op jit(solution)/shard_map/all_to_all | solution.py:508
  7.9 6.5 %collective-permute-start = (f32[64,128]{1,0:T(8,128)S(1)}, f32[64,128]{1,0:T(8,128)S(1)}, u32[]{:S(2)}, u32[]{:S(2)}) collective-permute-start(f32[64,128]{1,0:T(8,128)S(1)} %get-tuple-element.34), channel_id=1, source_target_pairs={{0,8},{8,16},{16,24},{24,0},{1,9},{9,17},{17,25},{25,1},{2,10},{10... | collective-permute-start | bytes 98312 | tf_op jit(solution)/shard_map/ppermute | solution.py:509
  9.5 4.9 %collective-permute-start.1 = (f32[64,128]{1,0:T(8,128)S(1)}, f32[64,128]{1,0:T(8,128)S(1)}, u32[]{:S(2)}, u32[]{:S(2)}) collective-permute-start(f32[64,128]{1,0:T(8,128)S(1)} %get-tuple-element.35), channel_id=1, source_target_pairs={{8,0},{16,8},{24,16},{0,24},{9,1},{17,9},{25,17},{1,25},{10,2},{18... | collective-permute-start | bytes 98312 | tf_op jit(solution)/shard_map/ppermute | solution.py:509
  15.4 10.3 %all-to-all-start.1 = ((f32[8,16,128]{2,1,0:T(8,128)}), f32[8,16,128]{2,1,0:T(8,128)S(1)}, u32[]{:S(2)}, u32[]{:S(2)}) async-start(f32[8,16,128]{2,1,0:T(8,128)} %bitcast.3), calls=%async_computation.1 | async-start | bytes 131072 | tf_op jit(solution)/shard_map/all_to_all | solution.py:508
  19.6 6.0 %collective-permute-start.2 = (f32[72,128]{1,0:T(8,128)S(1)}, f32[72,128]{1,0:T(8,128)S(1)}, u32[]{:S(2)}, u32[]{:S(2)}) collective-permute-start(f32[72,128]{1,0:T(8,128)S(1)} %get-tuple-element.46), channel_id=1, source_target_pairs={{0,8},{8,16},{16,24},{24,0},{1,9},{9,17},{17,25},{25,1},{2,10},{10... | collective-permute-start | bytes 110600 | tf_op jit(solution)/shard_map/ppermute | solution.py:509
  20.2 5.5 %collective-permute-start.3 = (f32[72,128]{1,0:T(8,128)S(1)}, f32[72,128]{1,0:T(8,128)S(1)}, u32[]{:S(2)}, u32[]{:S(2)}) collective-permute-start(f32[72,128]{1,0:T(8,128)S(1)} %get-tuple-element.47), channel_id=1, source_target_pairs={{8,0},{16,8},{24,16},{0,24},{9,1},{17,9},{25,17},{1,25},{10,2},{18... | collective-permute-start | bytes 110600 | tf_op jit(solution)/shard_map/ppermute | solution.py:509

commit v3 on v2

--- a/solution.py
+++ b/solution.py
@@ -148,9 +148,51 @@
     return corner // 4 * last * SQ + corner // 2 % 2 * last * POINTS + corner % 2 * last
 
 
+def up_goes_near(paired):
+    return lax.axis_index("elem") % 2 == 0 if paired else lax.axis_index("elem") >= 0
+
+
+def up_came_near(paired):
+    return lax.axis_index("elem") % 2 == 1 if paired else lax.axis_index("elem") >= 0
+
+
+def swap_if(flag, first, second):
+    return jnp.where(flag, first, second), jnp.where(flag, second, first)
+
+
+def member_rows(mask):
+    member = lax.axis_index("clus")
+    same = jnp.bitwise_xor(member, 2 * mask)
+    other = jnp.bitwise_xor(same, 1)
+    return pl.ds(pl.multiple_of(same * 16, 16), 16), pl.ds(pl.multiple_of(other * 16, 16), 16)
+
+
+def part_group(group_ref, keep_ref, cross_ref):
+    for mask in range(group_ref.shape[0] // 32):
+        same, other = member_rows(mask)
+        keep_ref[mask * 16 : mask * 16 + 16, :] = group_ref[same, :]
+        cross_ref[mask * 16 : mask * 16 + 16, :] = group_ref[other, :]
+
+
+def join_group(message_refs, group_ref):
+    for mask, message_ref in enumerate(message_refs):
+        same, other = member_rows(mask)
+        group_ref[same, :] = message_ref[0:16, :]
+        group_ref[other, :] = message_ref[16:32, :]
+
+
+def merge_kernel(keep_ref, cross_ref, *message_refs):
+    upper = iota((16, LANES), 1) >= HALF
+    sums = jnp.where(upper, keep_ref[0:16, :] + cross_ref[0:16, :], 0.0)
+    for mask, message_ref in enumerate(message_refs):
+        block = keep_ref[mask * 16 : mask * 16 + 16, :]
+        message_ref[0:16, :] = jnp.where(upper, sums, block)
+        message_ref[16:32, :] = cross_ref[mask * 16 : mask * 16 + 16, :]
+
+
 def send_kernel(
     total_vertices,
-    elem_ref,
+    paired,
     nodal_hbm,
     level_hbm,
     target_hbm,
@@ -158,9 +200,10 @@
     interp_hbm,
     derivative_hbm,
     vertex_hbm,
-    down_ref,
-    up_ref,
-    group_hbm,
+    near_ref,
+    far_ref,
+    keep_ref,
+    cross_ref,
     traces_ref,
     columns_ref,
     slot_level_ref,
@@ -199,7 +242,7 @@
     maps = kron_four(interp_ref[0], interp_ref[1])
     maps_ref[...] = maps
     vertex_copy.wait()
-    high_id, low_id = window_ids(vertex_ref[...], elem_ref[0], total_vertices)
+    high_id, low_id = window_ids(vertex_ref[...], lax.axis_index("elem"), total_vertices)
     low_hot = low_one_hot(low_id)
 
     for copy in nodal_copies:
@@ -242,14 +285,15 @@
     sums = sums[0:16] + sums[16:32]
     group = sent[:, 2 * CAP_E :]
     group = jnp.concatenate([group, jnp.zeros_like(group)], axis=0).T
-    group_ref[...] = group + jnp.concatenate([sums] * (group.shape[0] // 16), axis=0)
-    group_copy = pltpu.make_async_copy(group_ref, group_hbm, sems.at[6])
-    group_copy.start()
-    down_ref[...] = sent[:, 0:CAP_E]
-    up_ref[...] = sent[:, CAP_E : 2 * CAP_E]
+    group_ref[...] = group
+    part_group(group_ref, keep_ref, cross_ref)
+    keep_ref[0:16, :] += sums
+    cross_ref[0:16, :] += sums
+    near_ref[...], far_ref[...] = swap_if(
+        up_goes_near(paired), sent[:, CAP_E : 2 * CAP_E], sent[:, 0:CAP_E]
+    )
     slot_copy.wait()
     derivative_copy.wait()
-    group_copy.wait()
 
 
 def stiffness_maps(matrix):
@@ -341,42 +385,36 @@
 
 
 def answer_kernel(
-    from_up_ref,
-    from_down_ref,
-    group_ref,
+    paired,
+    near_in_ref,
+    far_in_ref,
     equal_ref,
     local_answers_ref,
-    down_ref,
-    up_ref,
-    group_hbm,
-    incoming_ref,
-    sums_ref,
-    group_out_ref,
-    sem,
+    *refs,
 ):
-    group_in = group_ref[...]
-    incoming = jnp.concatenate([from_up_ref[...], from_down_ref[...], group_in.T[0:SQ]], axis=1)
+    *message_refs, near_ref, far_ref, keep_ref, cross_ref, incoming_ref, sums_ref, group_ref = refs
+    join_group(message_refs, group_ref)
+    from_up, from_down = swap_if(
+        up_came_near(paired), near_in_ref[...], far_in_ref[...]
+    )
+    incoming = jnp.concatenate([from_up, from_down, group_ref[...].T[0:SQ]], axis=1)
     incoming_ref[...] = incoming
     added = mm(stack2(incoming), equal_ref[...])
     answers = local_answers_ref[...] + added[0:SQ] + added[SQ:]
     group = answers[:, 2 * CAP_E :]
-    group_out_ref[...] = jnp.concatenate([group, jnp.zeros_like(group)], axis=0).T
-    group_copy = pltpu.make_async_copy(group_out_ref, group_hbm, sem)
-    group_copy.start()
-    sums = group_in[0:16]
-    for block in range(1, group_in.shape[0] // 16):
-        sums = sums + group_in[block * 16 : block * 16 + 16]
+    group_ref[...] = jnp.concatenate([group, jnp.zeros_like(group)], axis=0).T
+    part_group(group_ref, keep_ref, cross_ref)
+    sums = message_refs[0][0:16, :]
+    for message_ref in message_refs[1:]:
+        sums = sums + message_ref[0:16, :]
     sums_ref[...] = sums
-    down_ref[0:SQ, :] = answers[:, 0:CAP_E]
-    up_ref[0:SQ, :] = answers[:, CAP_E : 2 * CAP_E]
-    down_ref[SQ:, :] = sums[0:8]
-    up_ref[SQ:, :] = sums[8:16]
-    group_copy.wait()
+    down = jnp.concatenate([answers[:, 0:CAP_E], sums[0:8]], axis=0)
+    up = jnp.concatenate([answers[:, CAP_E : 2 * CAP_E], sums[8:16]], axis=0)
+    near_ref[...], far_ref[...] = swap_if(up_goes_near(paired), up, down)
 
 
 def gather_kernel(
     total_vertices,
-    elem_ref,
     nodal_hbm,
     metric_hbm,
     mortar_ref,
@@ -411,7 +449,7 @@
     picked = picked[0:SQ] + picked[SQ:]
     back = pick_level(picked, mm(back_maps_ref[...], stack3(picked)), level_ref[...])
     remote_ref[...] = one_hot_rows(target, M_DEV, remote_ref.shape[0])
-    high_id, low_id = window_ids(vertex_ref[...], elem_ref[0], total_vertices)
+    high_id, low_id = window_ids(vertex_ref[...], lax.axis_index("elem"), total_vertices)
     high_ids_ref[...] = high_id
     low_ids_ref[...] = low_one_hot(low_id)
     for copy in nodal_copies:
@@ -436,9 +474,9 @@
 
 
 def final_kernel(
-    from_up_ref,
-    from_down_ref,
-    group_ref,
+    paired,
+    near_in_ref,
+    far_in_ref,
     slot_level_ref,
     maps_ref,
     remote_ref,
@@ -446,19 +484,20 @@
     high_ids_ref,
     low_ids_ref,
     result_ref,
-    out_hbm,
-    out_ref,
-    sems,
+    *refs,
 ):
-    arrived = jnp.concatenate(
-        [from_up_ref[0:SQ, :], from_down_ref[0:SQ, :], group_ref[...].T[0:SQ]], axis=1
-    )
+    *message_refs, out_hbm, out_ref, group_ref, sems = refs
+    join_group(message_refs, group_ref)
+    from_up, from_down = swap_if(
+        up_came_near(paired), near_in_ref[...], far_in_ref[...]
+    )
+    arrived = jnp.concatenate([from_up[0:SQ], from_down[0:SQ], group_ref[...].T[0:SQ]], axis=1)
     slot_back = pick_level(arrived, mm(maps_ref[...], stack3(arrived)), slot_level_ref[0:1, :])
     back = mm(stack2(slot_back), remote_ref[...])
     back = back[0:SQ] + back[SQ:]
 
-    first = sums_ref[0:8, :] + from_up_ref[SQ:, :]
-    second = sums_ref[8:16, :] + from_down_ref[SQ:, :]
+    first = sums_ref[0:8, :] + from_up[SQ:]
+    second = sums_ref[8:16, :] + from_down[SQ:]
     totals = jnp.concatenate([first[0:4], second[0:4]], axis=0)
     counts = jnp.concatenate([first[4:8], second[4:8]], axis=0)
     coarse = jnp.where(iota(totals.shape, 1) < HALF, 0.0, totals / (1.0 + counts))
@@ -485,7 +524,6 @@
 
 
 VMEM = pl.BlockSpec(memory_space=pltpu.VMEM)
-SMEM = pl.BlockSpec(memory_space=pltpu.SMEM)
 HBM = pl.BlockSpec(memory_space=pltpu.HBM)
 
 
@@ -497,16 +535,32 @@
     return pl.CostEstimate(flops=int(us * 5e8), bytes_accessed=int(us * 2e6), transcendentals=0)
 
 
-def neighbours(axis):
-    peers = lax.axis_size(axis)
+def curve_swap(near, far):
+    peers = lax.axis_size("elem")
     up = [(i, (i + 1) % peers) for i in range(peers)]
-    return up, [(j, i) for i, j in up]
-
-
-def exchange(down, up, group):
-    up_pairs, down_pairs = neighbours("elem")
-    group = lax.all_to_all(group, "clus", split_axis=0, concat_axis=0, tiled=True)
-    return lax.ppermute(up, "elem", up_pairs), lax.ppermute(down, "elem", down_pairs), group
+    near_pairs, far_pairs = up, [(j, i) for i, j in up]
+    if peers % 2 == 0:
+        near_pairs = [(i, i ^ 1) for i in range(peers)]
+        far_pairs = [(i, (i + 1 if i % 2 else i - 1) % peers) for i in range(peers)]
+    return lax.ppermute(near, "elem", near_pairs), lax.ppermute(far, "elem", far_pairs)
+
+
+def group_swap(keep, cross):
+    members = lax.axis_size("clus")
+    chips = members // 2
+    cross = lax.ppermute(cross, "clus", [(i, i ^ 1) for i in range(members)])
+    messages = pl.pallas_call(
+        merge_kernel,
+        in_specs=[VMEM] * 2,
+        out_specs=[VMEM] * chips,
+        out_shape=[pltpu.VMEM((32, LANES), f32)] * chips,
+        compiler_params=params(16),
+        name="merge",
+    )(keep, cross)
+    return [messages[0]] + [
+        lax.ppermute(messages[mask], "clus", [(i, i ^ (2 * mask)) for i in range(members)])
+        for mask in range(1, chips)
+    ]
 
 
 def on_device(nodal, metric, derivative, interp, face_level, face_target, slot_mortar, vertex_ids):
@@ -515,8 +569,9 @@
     slots = slot_mortar.shape[0]
     blocked = (elems // LANES, nodal.shape[0], LANES)
     total_vertices = NV_DEV * lax.axis_size("elem")
-    elem_index = lax.axis_index("elem").astype(jnp.int32).reshape(1)
+    paired = lax.axis_size("elem") % 2 == 0
     group_slots = slots - 2 * CAP_E
+    half_group = pltpu.VMEM((group_slots // 2, LANES), f32)
     nodal, metric, derivative, interp, face_level, face_target, slot_mortar, vertex_ids = (
         pltpu.with_memory_space_constraint(array, pltpu.HBM)
         for array in (
@@ -526,16 +581,17 @@
     maps_shape = pltpu.VMEM((4 * SQ, 3 * SQ), bf16)
 
     (
-        down, up, group, traces, columns, slot_level, maps,
+        near, far, keep, cross, traces, columns, slot_level, maps,
         level, target, slot_row, interp_in, derivative_in, vertex_in,
     ) = pl.pallas_call(
-        functools.partial(send_kernel, total_vertices),
-        in_specs=[SMEM] + [HBM] * 7,
-        out_specs=[VMEM, VMEM, HBM] + [VMEM] * 10,
+        functools.partial(send_kernel, total_vertices, paired),
+        in_specs=[HBM] * 7,
+        out_specs=[VMEM] * 14,
         out_shape=[
             pltpu.VMEM((SQ, CAP_E), f32),
             pltpu.VMEM((SQ, CAP_E), f32),
-            jax.ShapeDtypeStruct((group_slots, LANES), f32),
+            half_group,
+            half_group,
             pltpu.VMEM((2 * SQ + 16, faces), bf16),
             pltpu.VMEM((faces, LANES), jnp.int32),
             pltpu.VMEM((8, slots), f32),
@@ -551,13 +607,14 @@
             pltpu.VMEM(blocked, f32),
             pltpu.VMEM((group_slots, LANES), f32),
             pltpu.SemaphoreType.DMA((blocked[0],)),
-            pltpu.SemaphoreType.DMA((7,)),
+            pltpu.SemaphoreType.DMA((6,)),
         ],
         compiler_params=params(16),
         name="send",
-    )(elem_index, nodal, face_level, face_target, slot_mortar, interp, derivative, vertex_ids)
-
-    from_up, from_down, group_in = exchange(down, up, group)
+    )(nodal, face_level, face_target, slot_mortar, interp, derivative, vertex_ids)
+
+    near, far = curve_swap(near, far)
+    messages = group_swap(keep, cross)
 
     mortar, local_answers, equal, stiff, back_maps, grad_map, div_map = pl.pallas_call(
         local_kernel,
@@ -584,27 +641,29 @@
         name="local",
     )(nodal, metric, traces, maps, level, columns, slot_row, interp_in, derivative_in)
 
-    down, up, group, incoming, sums = pl.pallas_call(
-        answer_kernel,
-        in_specs=[VMEM] * 5,
-        out_specs=[VMEM, VMEM, HBM, VMEM, VMEM],
+    near, far, keep, cross, incoming, sums = pl.pallas_call(
+        functools.partial(answer_kernel, paired),
+        in_specs=[VMEM] * (4 + len(messages)),
+        out_specs=[VMEM] * 6,
         out_shape=[
             pltpu.VMEM((SQ + 8, CAP_E), f32),
             pltpu.VMEM((SQ + 8, CAP_E), f32),
-            jax.ShapeDtypeStruct((group_slots, LANES), f32),
+            half_group,
+            half_group,
             pltpu.VMEM((SQ, slots), f32),
             pltpu.VMEM((16, LANES), f32),
         ],
-        scratch_shapes=[pltpu.VMEM((group_slots, LANES), f32), pltpu.SemaphoreType.DMA],
+        scratch_shapes=[pltpu.VMEM((group_slots, LANES), f32)],
         compiler_params=params(16),
         name="answer",
-    )(from_up, from_down, group_in, equal, local_answers)
-
-    from_up, from_down, group_in = exchange(down, up, group)
+    )(near, far, equal, local_answers, *messages)
+
+    near, far = curve_swap(near, far)
+    messages = group_swap(keep, cross)
 
     result, remote, low_ids, high_ids = pl.pallas_call(
         functools.partial(gather_kernel, total_vertices),
-        in_specs=[SMEM, HBM, HBM] + [VMEM] * 10,
+        in_specs=[HBM, HBM] + [VMEM] * 10,
         out_specs=[VMEM] * 4,
         out_shape=[
             pltpu.VMEM(blocked, f32),
@@ -622,20 +681,24 @@
         cost_estimate=cost(3),
         name="gather",
     )(
-        elem_index, nodal, metric, mortar, incoming, slot_row, target, level, back_maps,
+        nodal, metric, mortar, incoming, slot_row, target, level, back_maps,
         grad_map, div_map, vertex_in, stiff,
     )
 
     return pl.pallas_call(
-        final_kernel,
-        in_specs=[VMEM] * 10,
+        functools.partial(final_kernel, paired),
+        in_specs=[VMEM] * (9 + len(messages)),
         out_specs=HBM,
         out_shape=jax.ShapeDtypeStruct(nodal.shape, f32),
-        scratch_shapes=[pltpu.VMEM(blocked, f32), pltpu.SemaphoreType.DMA((blocked[0],))],
+        scratch_shapes=[
+            pltpu.VMEM(blocked, f32),
+            pltpu.VMEM((group_slots, LANES), f32),
+            pltpu.SemaphoreType.DMA((blocked[0],)),
+        ],
         compiler_params=params(16),
         name="final",
     )(
-        from_up, from_down, group_in, slot_level, back_maps, remote, sums, high_ids, low_ids, result
+        near, far, slot_level, back_maps, remote, sums, high_ids, low_ids, result, *messages
     )
 
 

time: 27.5 us -> 25.5 us (0.927)
  starting transfers between devices: 17 us -> 14.5 us
  waiting for transfers between devices: 0.02 us -> 1.98 us
  Pallas kernels: 9.98 us -> 8.77 us
    all_to_all x2 -> x0, starting transfers between devices: 9.4 us -> none  [exchange(): lax.all_to_all(group, 'clus', split_axis=0, concat_axis=0, tiled=True)]
    ppermute x4 -> x12, starting transfers between devices: 7.65 us -> 14.5 us  [the longest x6 7.11 us: group_swap(): lax.ppermute(messages[mask], 'clus', [(i, i ^ 2 * mask) for i in range(me...]
    ppermute x4 -> x12, waiting for transfers between devices: 0.01 us -> 1.98 us  [the longest x6 1.96 us: group_swap(): lax.ppermute(messages[mask], 'clus', [(i, i ^ 2 * mask) for i in range(me...]
    pallas_call x3 -> x5, Pallas kernels: 5.16 us -> 3.95 us  [the longest x1 2.09 us: on_device(): pl.pallas_call(functools.partial(send_kernel, total_vertices, paired), in...]
  transfers between devices with their start and end apart: 6 -> 12, of which waited for: 0 -> 2; matrix products, arithmetic and copies ran while one was open for 0% -> 0% of each run, Pallas kernels for 18% -> 19%
where the time goes in v3:
time: 25.5 us; the launch traced here: 25.3 us
  starting transfers between devices  14.5 us (57%)
  Pallas kernels  8.77 us (34%)
  waiting for transfers between devices  1.98 us (8%)
    ppermute x6, starting transfers between devices, group_swap(): lax.ppermute(messages[mask], 'clus', [(i, i ^ 2 * mask) for i in range(me...  7.11 us
    ppermute x2, starting transfers between devices, curve_swap(): lax.ppermute(near, 'elem', near_pairs)  3.4 us
    ppermute x2, starting transfers between devices, curve_swap(): lax.ppermute(far, 'elem', far_pairs)  3.38 us
    pallas_call x1, Pallas kernels, on_device(): pl.pallas_call(local_kernel, in_specs=[HBM, HBM] + [VMEM] * 7, out_specs=...  2.65 us
    pallas_call x1, Pallas kernels, on_device(): pl.pallas_call(functools.partial(gather_kernel, total_vertices), in_specs...  2.17 us
    pallas_call x1, Pallas kernels, on_device(): pl.pallas_call(functools.partial(send_kernel, total_vertices, paired), in...  2.09 us
    ppermute x6, waiting for transfers between devices, group_swap(): lax.ppermute(messages[mask], 'clus', [(i, i ^ 2 * mask) for i in range(me...  1.96 us
    pallas_call x1, Pallas kernels, on_device(): pl.pallas_call(functools.partial(final_kernel, paired), in_specs=[VMEM] *...  1.46 us
  transfers between devices with their start and end apart: 12, of which 2 were waited for; matrix products, arithmetic and copies ran while one was open for 0% of the time, Pallas kernels for 19%

profile of v3, /device:TPU:0, one launch (start us, length us, event | category | flops | bytes accessed | tf_op | source)
XLA Modules:
  0.0 25.3 jit_solution(14717181991514956354)
XLA Ops:
  0.0 2.1 %send.1 = (f32[64,128]{1,0:T(8,128)S(1)}, f32[64,128]{1,0:T(8,128)S(1)}, f32[64,128]{1,0:T(8,128)S(1)}, f32[64,128]{1,0:T(8,128)S(1)}, bf16[144,1536]{1,0:T(8,12...) custom-call(f32[512,256]{1,0:T(8,128)} %nodal_hbm.5, ...), custom_call_target="tpu_custom_call" | custom-call | tf_op jit(solution)/shard_map/send/pallas_call | solution.py:586
  2.1 0.5 %collective-permute-start.2 = (f32[64,128]{1,0:T(8,128)S(1)}, f32[64,128]{1,0:T(8,128)S(1)}, u32[]{:S(2)}, u32[]{:S(2)}) collective-permute-start(f32[64,128]{1,0:T(8,128)S(1)} %get-tuple-element.56), channel_id=1, source_target_pairs={{0,1},{1,0},{2,3},{3,2},{4,5},{5,4},{6,7},{7,6},{8,9},{9,8},{10,11... | collective-permute-start | bytes 98312 | tf_op jit(solution)/shard_map/ppermute | solution.py:551
  2.6 2.7 %collective-permute-start = (f32[64,128]{1,0:T(8,128)S(1)}, f32[64,128]{1,0:T(8,128)S(1)}, u32[]{:S(2)}, u32[]{:S(2)}) collective-permute-start(f32[64,128]{1,0:T(8,128)S(1)} %get-tuple-element.44), channel_id=1, source_target_pairs={{0,8},{8,0},{16,24},{24,16},{1,9},{9,1},{17,25},{25,17},{2,10},{10... | collective-permute-start | bytes 98312 | tf_op jit(solution)/shard_map/ppermute | solution.py:545
  5.3 2.5 %collective-permute-start.1 = (f32[64,128]{1,0:T(8,128)S(1)}, f32[64,128]{1,0:T(8,128)S(1)}, u32[]{:S(2)}, u32[]{:S(2)}) collective-permute-start(f32[64,128]{1,0:T(8,128)S(1)} %get-tuple-element.45), channel_id=1, source_target_pairs={{0,24},{8,16},{16,8},{24,0},{1,25},{9,17},{17,9},{25,1},{2,26},{10... | collective-permute-start | bytes 98312 | tf_op jit(solution)/shard_map/ppermute | solution.py:545
  7.7 0.0 collective-permute-done.2.cross_ref
  7.8 1.6 %collective-permute-start.3 = (f32[32,128]{1,0:T(8,128)S(1)}, f32[32,128]{1,0:T(8,128)S(1)}, u32[]{:S(2)}, u32[]{:S(2)}) collective-permute-start(f32[32,128]{1,0:T(8,128)S(1)} %get-tuple-element.58), channel_id=1, source_target_pairs={{0,2},{1,3},{2,0},{3,1},{4,6},{5,7},{6,4},{7,5},{8,10},{9,11},{10,... | collective-permute-start | bytes 49160 | tf_op jit(solution)/shard_map/ppermute | solution.py:561
  9.3 1.5 %collective-permute-start.4 = (f32[32,128]{1,0:T(8,128)S(1)}, f32[32,128]{1,0:T(8,128)S(1)}, u32[]{:S(2)}, u32[]{:S(2)}) collective-permute-start(f32[32,128]{1,0:T(8,128)S(1)} %get-tuple-element.59), channel_id=1, source_target_pairs={{0,4},{1,5},{2,6},{3,7},{4,0},{5,1},{6,2},{7,3},{8,12},{9,13},{10,... | collective-permute-start | bytes 49160 | tf_op jit(solution)/shard_map/ppermute | solution.py:561
  10.8 0.5 %collective-permute-start.5 = (f32[32,128]{1,0:T(8,128)S(1)}, f32[32,128]{1,0:T(8,128)S(1)}, u32[]{:S(2)}, u32[]{:S(2)}) collective-permute-start(f32[32,128]{1,0:T(8,128)S(1)} %get-tuple-element.60), channel_id=1, source_target_pairs={{0,6},{1,7},{2,4},{3,5},{4,2},{5,3},{6,0},{7,1},{8,14},{9,15},{10,... | collective-permute-start | bytes 49160 | tf_op jit(solution)/shard_map/ppermute | solution.py:561
  11.3 2.6 %local.1 = (f32[64,512]{1,0:T(8,128)S(1)}, f32[64,384]{1,0:T(8,128)S(1)}, bf16[384,384]{1,0:T(8,128)(2,1)S(1)}, f32[512,256]{1,0:T(8,128)S(1)}, bf16[256,192]{1,...) custom-call(f32[512,256]{1,0:T(8,128)} %nodal_hbm.5, bf16[3,512,256]{2,1,0:T(8,128)(2,1)} %metric_hbm.3, ...), custom_call_target="tpu_custom_call" | custom-call | flops 1500000000 | bytes 6000000 | tf_op jit(solution)/shard_map/local/pallas_call | solution.py:619
  14.0 0.0 collective-permute-done.near_in_ref
  14.0 0.0 collective-permute-done.1.far_in_ref
  14.0 1.5 %collective-permute-done.5.refs_3_ = f32[32,128]{1,0:T(8,128)S(1)} collective-permute-done((f32[32,128]{1,0:T(8,128)S(1)}, f32[32,128]{1,0:T(8,128)S(1)}, u32[]{:S(2)}, u32[]{:S(2)}) %collective-permute-start.5) | collective-permute-done | bytes 16416 | tf_op jit(solution)/shard_map/ppermute | solution.py:561
  15.5 0.4 %answer.1 = (f32[72,128]{1,0:T(8,128)S(1)}, f32[72,128]{1,0:T(8,128)S(1)}, f32[64,128]{1,0:T(8,128)S(1)}, f32[64,128]{1,0:T(8,128)S(1)}, f32[64,384]{1,0:T(8,128)S(1)}, /*index=5*/f32[16,128]{1,0:T(8,128)S(1)}) custom-call(f32[64,128]{1,0:T(8,128)S(1)} %collective-permute-done.near_in_ref, f32[64,128]{1,0:T(8,128)S(1)} %collective-permute-done.1.far_in_ref, ...), custom_call_target="tpu_custom_call" | custom-call | tf_op jit(solution)/shard_map/answer/pallas_call | solution.py:644
  15.9 0.1 collective-permute-start.8
  15.9 0.7 %collective-permute-start.6 = (f32[72,128]{1,0:T(8,128)S(1)}, f32[72,128]{1,0:T(8,128)S(1)}, u32[]{:S(2)}, u32[]{:S(2)}) collective-permute-start(f32[72,128]{1,0:T(8,128)S(1)} %get-tuple-element.61), channel_id=1, source_target_pairs={{0,8},{8,0},{16,24},{24,16},{1,9},{9,1},{17,25},{25,17},{2,10},{10... | collective-permute-start | bytes 110600 | tf_op jit(solution)/shard_map/ppermute | solution.py:545
  16.7 0.9 %collective-permute-start.7 = (f32[72,128]{1,0:T(8,128)S(1)}, f32[72,128]{1,0:T(8,128)S(1)}, u32[]{:S(2)}, u32[]{:S(2)}) collective-permute-start(f32[72,128]{1,0:T(8,128)S(1)} %get-tuple-element.62), channel_id=1, source_target_pairs={{0,24},{8,16},{16,8},{24,0},{1,25},{9,17},{17,9},{25,1},{2,26},{10... | collective-permute-start | bytes 110600 | tf_op jit(solution)/shard_map/ppermute | solution.py:545
  17.6 0.0 collective-permute-done.8.cross_ref
  17.6 0.6 %collective-permute-start.9 = (f32[32,128]{1,0:T(8,128)S(1)}, f32[32,128]{1,0:T(8,128)S(1)}, u32[]{:S(2)}, u32[]{:S(2)}) collective-permute-start(f32[32,128]{1,0:T(8,128)S(1)} %get-tuple-element.80), channel_id=1, source_target_pairs={{0,2},{1,3},{2,0},{3,1},{4,6},{5,7},{6,4},{7,5},{8,10},{9,11},{10,... | collective-permute-start | bytes 49160 | tf_op jit(solution)/shard_map/ppermute | solution.py:561
  18.2 1.0 %collective-permute-start.10 = (f32[32,128]{1,0:T(8,128)S(1)}, f32[32,128]{1,0:T(8,128)S(1)}, u32[]{:S(2)}, u32[]{:S(2)}) collective-permute-start(f32[32,128]{1,0:T(8,128)S(1)} %get-tuple-element.81), channel_id=1, source_target_pairs={{0,4},{1,5},{2,6},{3,7},{4,0},{5,1},{6,2},{7,3},{8,12},{9,13},{10,... | collective-permute-start | bytes 49160 | tf_op jit(solution)/shard_map/ppermute | solution.py:561
  19.2 1.9 %collective-permute-start.11 = (f32[32,128]{1,0:T(8,128)S(1)}, f32[32,128]{1,0:T(8,128)S(1)}, u32[]{:S(2)}, u32[]{:S(2)}) collective-permute-start(f32[32,128]{1,0:T(8,128)S(1)} %get-tuple-element.82), channel_id=1, source_target_pairs={{0,6},{1,7},{2,4},{3,5},{4,2},{5,3},{6,0},{7,1},{8,14},{9,15},{10,... | collective-permute-start | bytes 49160 | tf_op jit(solution)/shard_map/ppermute | solution.py:561
  21.2 2.2 %gather.1 = (f32[2,512,128]{2,1,0:T(8,128)S(1)}, bf16[384,1536]{1,0:T(8,128)(2,1)S(1)}, bf16[128,2048]{1,0:T(8,128)(2,1)S(1)}, s32[8,256]{1,0:T(8,128)S(1)}) custom-call(f32[512,256]{1,0:T(8,128)} %nodal_hbm.5, bf16[3,512,256]{2,1,0:T(8,128)(2,1)} %metric_hbm.3, f32[64,512]{1,0:T(8,128)S(1)} %get-tuple-element.65.mortar_ref, ...), custom_call_target="tpu_custom_call" | custom-call | flops 1500000000 | bytes 6000000 | tf_op jit(solution)/shard_map/gather/pallas_call | solution.py:664
  23.3 0.0 collective-permute-done.7.far_in_ref
  23.4 0.5 %collective-permute-done.11.refs_3_ = f32[32,128]{1,0:T(8,128)S(1)} collective-permute-done((f32[32,128]{1,0:T(8,128)S(1)}, f32[32,128]{1,0:T(8,128)S(1)}, u32[]{:S(2)}, u32[]{:S(2)}) %collective-permute-start.11) | collective-permute-done | bytes 16416 | tf_op jit(solution)/shard_map/ppermute | solution.py:561
  23.9 1.5 %final.1 = f32[512,256]{1,0:T(8,128)} custom-call(f32[72,128]{1,0:T(8,128)S(1)} %collective-permute-done.6.near_in_ref, f32[72,128]{1,0:T(8,128)S(1)} %collective-permute-done.7.far_in_ref, f32[8,384]{1,0:T(8,128)S(1)} %get-tuple-element.63.slot_level_ref, bf16[256,192]{1,0:T(8,128)(2,1)S(1)} %get-tuple-element.64.back_maps_ref.maps_ref, ...), custom_call_target="tpu_custom_call" | custom-call | tf_op jit(solution)/shard_map/final/pallas_call | solution.py:688
  (7 shorter events, 0.0 us)
Async XLA Ops:
  2.1 5.6 %collective-permute-start.2 = (f32[64,128]{1,0:T(8,128)S(1)}, f32[64,128]{1,0:T(8,128)S(1)}, u32[]{:S(2)}, u32[]{:S(2)}) collective-permute-start(f32[64,128]{1,0:T(8,128)S(1)} %get-tuple-element.56), channel_id=1, source_target_pairs={{0,1},{1,0},{2,3},{3,2},{4,5},{5,4},{6,7},{7,6},{8,9},{9,8},{10,11... | collective-permute-start | bytes 98312 | tf_op jit(solution)/shard_map/ppermute | solution.py:551
  2.6 11.4 %collective-permute-start = (f32[64,128]{1,0:T(8,128)S(1)}, f32[64,128]{1,0:T(8,128)S(1)}, u32[]{:S(2)}, u32[]{:S(2)}) collective-permute-start(f32[64,128]{1,0:T(8,128)S(1)} %get-tuple-element.44), channel_id=1, source_target_pairs={{0,8},{8,0},{16,24},{24,16},{1,9},{9,1},{17,25},{25,17},{2,10},{10... | collective-permute-start | bytes 98312 | tf_op jit(solution)/shard_map/ppermute | solution.py:545
  5.3 8.7 %collective-permute-start.1 = (f32[64,128]{1,0:T(8,128)S(1)}, f32[64,128]{1,0:T(8,128)S(1)}, u32[]{:S(2)}, u32[]{:S(2)}) collective-permute-start(f32[64,128]{1,0:T(8,128)S(1)} %get-tuple-element.45), channel_id=1, source_target_pairs={{0,24},{8,16},{16,8},{24,0},{1,25},{9,17},{17,9},{25,1},{2,26},{10... | collective-permute-start | bytes 98312 | tf_op jit(solution)/shard_map/ppermute | solution.py:545
  7.8 6.2 %collective-permute-start.3 = (f32[32,128]{1,0:T(8,128)S(1)}, f32[32,128]{1,0:T(8,128)S(1)}, u32[]{:S(2)}, u32[]{:S(2)}) collective-permute-start(f32[32,128]{1,0:T(8,128)S(1)} %get-tuple-element.58), channel_id=1, source_target_pairs={{0,2},{1,3},{2,0},{3,1},{4,6},{5,7},{6,4},{7,5},{8,10},{9,11},{10,... | collective-permute-start | bytes 49160 | tf_op jit(solution)/shard_map/ppermute | solution.py:561
  9.3 4.7 %collective-permute-start.4 = (f32[32,128]{1,0:T(8,128)S(1)}, f32[32,128]{1,0:T(8,128)S(1)}, u32[]{:S(2)}, u32[]{:S(2)}) collective-permute-start(f32[32,128]{1,0:T(8,128)S(1)} %get-tuple-element.59), channel_id=1, source_target_pairs={{0,4},{1,5},{2,6},{3,7},{4,0},{5,1},{6,2},{7,3},{8,12},{9,13},{10,... | collective-permute-start | bytes 49160 | tf_op jit(solution)/shard_map/ppermute | solution.py:561
  10.8 4.6 %collective-permute-start.5 = (f32[32,128]{1,0:T(8,128)S(1)}, f32[32,128]{1,0:T(8,128)S(1)}, u32[]{:S(2)}, u32[]{:S(2)}) collective-permute-start(f32[32,128]{1,0:T(8,128)S(1)} %get-tuple-element.60), channel_id=1, source_target_pairs={{0,6},{1,7},{2,4},{3,5},{4,2},{5,3},{6,0},{7,1},{8,14},{9,15},{10,... | collective-permute-start | bytes 49160 | tf_op jit(solution)/shard_map/ppermute | solution.py:561
  15.9 1.7 %collective-permute-start.8 = (f32[64,128]{1,0:T(8,128)S(1)}, f32[64,128]{1,0:T(8,128)S(1)}, u32[]{:S(2)}, u32[]{:S(2)}) collective-permute-start(f32[64,128]{1,0:T(8,128)S(1)} %get-tuple-element.78), channel_id=1, source_target_pairs={{0,1},{1,0},{2,3},{3,2},{4,5},{5,4},{6,7},{7,6},{8,9},{9,8},{10,11... | collective-permute-start | bytes 98312 | tf_op jit(solution)/shard_map/ppermute | solution.py:551
  15.9 7.4 %collective-permute-start.6 = (f32[72,128]{1,0:T(8,128)S(1)}, f32[72,128]{1,0:T(8,128)S(1)}, u32[]{:S(2)}, u32[]{:S(2)}) collective-permute-start(f32[72,128]{1,0:T(8,128)S(1)} %get-tuple-element.61), channel_id=1, source_target_pairs={{0,8},{8,0},{16,24},{24,16},{1,9},{9,1},{17,25},{25,17},{2,10},{10... | collective-permute-start | bytes 110600 | tf_op jit(solution)/shard_map/ppermute | solution.py:545
  16.7 6.7 %collective-permute-start.7 = (f32[72,128]{1,0:T(8,128)S(1)}, f32[72,128]{1,0:T(8,128)S(1)}, u32[]{:S(2)}, u32[]{:S(2)}) collective-permute-start(f32[72,128]{1,0:T(8,128)S(1)} %get-tuple-element.62), channel_id=1, source_target_pairs={{0,24},{8,16},{16,8},{24,0},{1,25},{9,17},{17,9},{25,1},{2,26},{10... | collective-permute-start | bytes 110600 | tf_op jit(solution)/shard_map/ppermute | solution.py:545
  17.6 5.8 %collective-permute-start.9 = (f32[32,128]{1,0:T(8,128)S(1)}, f32[32,128]{1,0:T(8,128)S(1)}, u32[]{:S(2)}, u32[]{:S(2)}) collective-permute-start(f32[32,128]{1,0:T(8,128)S(1)} %get-tuple-element.80), channel_id=1, source_target_pairs={{0,2},{1,3},{2,0},{3,1},{4,6},{5,7},{6,4},{7,5},{8,10},{9,11},{10,... | collective-permute-start | bytes 49160 | tf_op jit(solution)/shard_map/ppermute | solution.py:561
  18.2 5.2 %collective-permute-start.10 = (f32[32,128]{1,0:T(8,128)S(1)}, f32[32,128]{1,0:T(8,128)S(1)}, u32[]{:S(2)}, u32[]{:S(2)}) collective-permute-start(f32[32,128]{1,0:T(8,128)S(1)} %get-tuple-element.81), channel_id=1, source_target_pairs={{0,4},{1,5},{2,6},{3,7},{4,0},{5,1},{6,2},{7,3},{8,12},{9,13},{10,... | collective-permute-start | bytes 49160 | tf_op jit(solution)/shard_map/ppermute | solution.py:561
  19.2 4.6 %collective-permute-start.11 = (f32[32,128]{1,0:T(8,128)S(1)}, f32[32,128]{1,0:T(8,128)S(1)}, u32[]{:S(2)}, u32[]{:S(2)}) collective-permute-start(f32[32,128]{1,0:T(8,128)S(1)} %get-tuple-element.82), channel_id=1, source_target_pairs={{0,6},{1,7},{2,4},{3,5},{4,2},{5,3},{6,0},{7,1},{8,14},{9,15},{10,... | collective-permute-start | bytes 49160 | tf_op jit(solution)/shard_map/ppermute | solution.py:561

commit v4 on v3

--- a/solution.py
+++ b/solution.py
@@ -99,13 +99,11 @@
         ref[h, rows, :] += value[:, h * LANES : (h + 1) * LANES]
 
 
-def lane_copies(hbm, blocks, sems, outward):
-    copies = []
-    for h in range(blocks.shape[0]):
-        outer = hbm.at[:, pl.ds(h * LANES, LANES)]
-        ends = (blocks.at[h], outer) if outward else (outer, blocks.at[h])
-        copies.append(pltpu.make_async_copy(*ends, sems.at[h]))
-    return copies
+def lane_copies(hbm, blocks, sems):
+    return [
+        pltpu.make_async_copy(hbm.at[:, pl.ds(h * LANES, LANES)], blocks.at[h], sems.at[h])
+        for h in range(blocks.shape[0])
+    ]
 
 
 def pick_level(plain, mapped, level):
@@ -167,6 +165,10 @@
     return pl.ds(pl.multiple_of(same * 16, 16), 16), pl.ds(pl.multiple_of(other * 16, 16), 16)
 
 
+def chip_masks(chips):
+    return [0] + list(range(chips - 1, 0, -1))
+
+
 def part_group(group_ref, keep_ref, cross_ref):
     for mask in range(group_ref.shape[0] // 32):
         same, other = member_rows(mask)
@@ -175,7 +177,7 @@
 
 
 def join_group(message_refs, group_ref):
-    for mask, message_ref in enumerate(message_refs):
+    for mask, message_ref in zip(chip_masks(len(message_refs)), message_refs):
         same, other = member_rows(mask)
         group_ref[same, :] = message_ref[0:16, :]
         group_ref[other, :] = message_ref[16:32, :]
@@ -225,7 +227,7 @@
     vertex_copy = pltpu.make_async_copy(vertex_hbm, vertex_ref, sems.at[3])
     slot_copy = pltpu.make_async_copy(slot_hbm, slot_mortar_ref.at[0], sems.at[4])
     derivative_copy = pltpu.make_async_copy(derivative_hbm, derivative_ref, sems.at[5])
-    nodal_copies = lane_copies(nodal_hbm, nodal_ref, nodal_sems, False)
+    nodal_copies = lane_copies(nodal_hbm, nodal_ref, nodal_sems)
     target_copy.start()
     interp_copy.start()
     for copy in nodal_copies:
@@ -267,8 +269,8 @@
     plain = picked[0:SQ] + picked[SQ : 2 * SQ]
     slot_level = picked[2 * SQ : 2 * SQ + 8]
     slot_level_ref[...] = slot_level
-    mapped = mm(maps, stack3(plain))
-    sent = pick_level(plain, mapped, slot_level[0:1])
+    sent = pick_level(plain, mm(maps, stack3(plain)), slot_level[0:1])
+
     row = iota((16, elems), 0)
     row_high = row % 4 + 4 * (row // 8)
     is_count = row // 4 % 2 == 1
@@ -284,8 +286,7 @@
     sums = mm_nt(jnp.concatenate(weighted, axis=1), low_hot)
     sums = sums[0:16] + sums[16:32]
     group = sent[:, 2 * CAP_E :]
-    group = jnp.concatenate([group, jnp.zeros_like(group)], axis=0).T
-    group_ref[...] = group
+    group_ref[...] = jnp.concatenate([group, jnp.zeros_like(group)], axis=0).T
     part_group(group_ref, keep_ref, cross_ref)
     keep_ref[0:16, :] += sums
     cross_ref[0:16, :] += sums
@@ -306,8 +307,6 @@
 
 
 def local_kernel(
-    nodal_hbm,
-    metric_hbm,
     traces_ref,
     maps_ref,
     level_ref,
@@ -318,21 +317,13 @@
     mortar_ref,
     answers_ref,
     equal_ref,
-    stiff_ref,
     back_maps_ref,
     grad_map_ref,
     div_map_ref,
-    nodal_ref,
-    metric_ref,
-    by_row,
-    nodal_sems,
-    sem,
 ):
-    nodal_copies = lane_copies(nodal_hbm, nodal_ref, nodal_sems, False)
-    metric_copy = pltpu.make_async_copy(metric_hbm.at[0], metric_ref, sem)
-    for copy in nodal_copies:
-        copy.start()
-    metric_copy.start()
+    back_maps_ref[...] = kron_four(interp_ref[0].T, interp_ref[1].T)
+    slot_row = slot_mortar_ref[...]
+    equal_ref[...] = (columns_of(slot_row)[:, 0:1] == slot_row).astype(f32).astype(bf16)
     hi = traces_ref[0:SQ, :]
     lo = traces_ref[SQ : 2 * SQ, :]
     plain = hi.astype(f32) + lo.astype(f32)
@@ -341,21 +332,13 @@
     mortar = mm(stack2(projected), one_hot_lanes(columns_ref[...], 0, M_DEV))
     mortar = mortar[0:SQ] + mortar[SQ:]
     mortar_ref[...] = mortar
-    slot_row = slot_mortar_ref[...]
     answers = mm(stack2(mortar), one_hot_rows(slot_row, 0, M_DEV))
     answers_ref[...] = answers[0:SQ] + answers[SQ:]
-    equal_ref[...] = (columns_of(slot_row)[:, 0:1] == slot_row).astype(f32).astype(bf16)
-
-    back_maps_ref[...] = kron_four(interp_ref[0].T, interp_ref[1].T)
     outer, inner = stiffness_maps(derivative_ref[...])
     outer_t, inner_t = stiffness_maps(derivative_ref[...].T)
     grad_map_ref[0:SQ, :] = outer
     grad_map_ref[SQ:, :] = inner
     div_map_ref[...] = jnp.concatenate([outer_t, inner_t], axis=1)
-    for copy in nodal_copies:
-        copy.wait()
-    metric_copy.wait()
-    first_direction(nodal_ref, metric_ref, outer, outer_t, stiff_ref, by_row)
 
 
 def first_direction(nodal_ref, metric_ref, outer, outer_t, stiff_ref, by_row):
@@ -426,18 +409,19 @@
     grad_map_ref,
     div_map_ref,
     vertex_ref,
-    stiff_ref,
     result_ref,
     remote_ref,
     low_ids_ref,
     high_ids_ref,
     nodal_ref,
     metric_ref,
+    stiff_ref,
+    by_row,
     nodal_sems,
     sem,
 ):
-    nodal_copies = lane_copies(nodal_hbm, nodal_ref, nodal_sems, False)
-    metric_copy = pltpu.make_async_copy(metric_hbm.at[1:3], metric_ref, sem)
+    nodal_copies = lane_copies(nodal_hbm, nodal_ref, nodal_sems)
+    metric_copy = pltpu.make_async_copy(metric_hbm, metric_ref, sem)
     for copy in nodal_copies:
         copy.start()
     metric_copy.start()
@@ -455,8 +439,9 @@
     for copy in nodal_copies:
         copy.wait()
     metric_copy.wait()
+    first_direction(nodal_ref, metric_ref.at[0], grad_map_ref[0:SQ, :], div_map_ref[:, 0:3 * SQ], stiff_ref, by_row)
     other_directions(
-        nodal_ref, metric_ref, grad_map_ref[...], div_map_ref[...], stiff_ref, result_ref
+        nodal_ref, metric_ref.at[1:3], grad_map_ref[...], div_map_ref[...], stiff_ref, result_ref
     )
     add_faces(result_ref, back)
 
@@ -507,18 +492,37 @@
     found = found[0:8] + found[8:16]
     high_id = high_ids_ref[...]
 
-    out_ref[...] = result_ref[...]
-    add_faces(out_ref, back)
     elems = out_hbm.shape[1]
     row = iota((8, elems), 0)
+    fixes = []
     for corner in range(8):
         mine = row == high_id[corner : corner + 1]
         fix = jnp.where(mine, found[:, corner * elems : (corner + 1) * elems], 0.0)
-        at = corner_row(corner)
-        add_rows(out_ref, pl.ds(at, 1), jnp.sum(fix, axis=0, keepdims=True))
-    copies = lane_copies(out_hbm, out_ref, sems, True)
-    for copy in copies:
-        copy.start()
+        fixes.append(jnp.sum(fix, axis=0, keepdims=True))
+    parts = [back[:, f * elems : (f + 1) * elems] for f in range(6)]
+    copies = []
+    for i in range(POINTS):
+        rows = slice(i * POINTS, (i + 1) * POINTS)
+        slab = load_rows(result_ref, pl.ds(i * SQ, SQ))
+        if i in (0, POINTS - 1):
+            slab = slab + parts[min(i, 1)]
+        pieces = [slab[0:8] + parts[2][rows], slab[8:56], slab[56:64] + parts[3][rows]]
+        store_rows(out_ref, pl.ds(i * SQ, SQ), jnp.concatenate(pieces, axis=0))
+        add_rows(out_ref, pl.ds(i * SQ, 8, stride=8), parts[4][rows])
+        add_rows(out_ref, pl.ds(i * SQ + 7, 8, stride=8), parts[5][rows])
+        for corner in range(8):
+            if corner_row(corner) // SQ == i:
+                add_rows(out_ref, pl.ds(corner_row(corner), 1), fixes[corner])
+        if i % 2:
+            rows = pl.ds((i - 1) * SQ, 2 * SQ)
+            for h in range(out_ref.shape[0]):
+                lanes = pl.ds(h * LANES, LANES)
+                copies.append(
+                    pltpu.make_async_copy(
+                        out_ref.at[h, rows], out_hbm.at[rows, lanes], sems.at[len(copies)]
+                    )
+                )
+                copies[-1].start()
     for copy in copies:
         copy.wait()
 
@@ -559,7 +563,7 @@
     )(keep, cross)
     return [messages[0]] + [
         lax.ppermute(messages[mask], "clus", [(i, i ^ (2 * mask)) for i in range(members)])
-        for mask in range(1, chips)
+        for mask in chip_masks(chips)[1:]
     ]
 
 
@@ -616,30 +620,22 @@
     near, far = curve_swap(near, far)
     messages = group_swap(keep, cross)
 
-    mortar, local_answers, equal, stiff, back_maps, grad_map, div_map = pl.pallas_call(
+    mortar, local_answers, equal, back_maps, grad_map, div_map = pl.pallas_call(
         local_kernel,
-        in_specs=[HBM, HBM] + [VMEM] * 7,
-        out_specs=[VMEM] * 7,
+        in_specs=[VMEM] * 7,
+        out_specs=[VMEM] * 6,
         out_shape=[
             pltpu.VMEM((SQ, M_DEV), f32),
             pltpu.VMEM((SQ, slots), f32),
             pltpu.VMEM((slots, slots), bf16),
-            pltpu.VMEM(nodal.shape, f32),
             maps_shape,
             pltpu.VMEM((2 * SQ, 3 * SQ), bf16),
             pltpu.VMEM((SQ, 6 * SQ), bf16),
         ],
-        scratch_shapes=[
-            pltpu.VMEM(blocked, f32),
-            pltpu.VMEM(nodal.shape, bf16),
-            pltpu.VMEM(nodal.shape, f32),
-            pltpu.SemaphoreType.DMA((blocked[0],)),
-            pltpu.SemaphoreType.DMA,
-        ],
         compiler_params=params(16),
         cost_estimate=cost(3),
         name="local",
-    )(nodal, metric, traces, maps, level, columns, slot_row, interp_in, derivative_in)
+    )(traces, maps, level, columns, slot_row, interp_in, derivative_in)
 
     near, far, keep, cross, incoming, sums = pl.pallas_call(
         functools.partial(answer_kernel, paired),
@@ -663,7 +659,7 @@
 
     result, remote, low_ids, high_ids = pl.pallas_call(
         functools.partial(gather_kernel, total_vertices),
-        in_specs=[HBM, HBM] + [VMEM] * 10,
+        in_specs=[HBM, HBM] + [VMEM] * 9,
         out_specs=[VMEM] * 4,
         out_shape=[
             pltpu.VMEM(blocked, f32),
@@ -673,7 +669,9 @@
         ],
         scratch_shapes=[
             pltpu.VMEM(blocked, f32),
-            pltpu.VMEM((2,) + nodal.shape, bf16),
+            pltpu.VMEM(metric.shape, bf16),
+            pltpu.VMEM(nodal.shape, f32),
+            pltpu.VMEM(nodal.shape, f32),
             pltpu.SemaphoreType.DMA((blocked[0],)),
             pltpu.SemaphoreType.DMA,
         ],
@@ -682,7 +680,7 @@
         name="gather",
     )(
         nodal, metric, mortar, incoming, slot_row, target, level, back_maps,
-        grad_map, div_map, vertex_in, stiff,
+        grad_map, div_map, vertex_in,
     )
 
     return pl.pallas_call(
@@ -693,7 +691,7 @@
         scratch_shapes=[
             pltpu.VMEM(blocked, f32),
             pltpu.VMEM((group_slots, LANES), f32),
-            pltpu.SemaphoreType.DMA((blocked[0],)),
+            pltpu.SemaphoreType.DMA((POINTS // 2 * blocked[0],)),
         ],
         compiler_params=params(16),
         name="final",

time: 25.5 us -> 24.2 us (0.949)
  Pallas kernels: 8.77 us -> 7.53 us
    pallas_call x1, Pallas kernels: 2.65 us -> 1.33 us  [on_device(): pl.pallas_call(local_kernel, in_specs=[VMEM] * 7, out_specs=[VMEM] * 6, o...]
  transfers between devices with their start and end apart: 12 -> 12, of which waited for: 2 -> 2; matrix products, arithmetic and copies ran while one was open for 0% -> 0% of each run, Pallas kernels for 19% -> 15%
where the time goes in v4:
time: 24.2 us; the launch traced here: 24 us
  starting transfers between devices  14.5 us (60%)
  Pallas kernels  7.53 us (31%)
  waiting for transfers between devices  1.86 us (8%)
    ppermute x6, starting transfers between devices, group_swap(): lax.ppermute(messages[mask], 'clus', [(i, i ^ 2 * mask) for i in range(me...  7.11 us
    ppermute x2, starting transfers between devices, curve_swap(): lax.ppermute(near, 'elem', near_pairs)  3.41 us
    ppermute x2, starting transfers between devices, curve_swap(): lax.ppermute(far, 'elem', far_pairs)  3.38 us
    pallas_call x1, Pallas kernels, on_device(): pl.pallas_call(functools.partial(gather_kernel, total_vertices), in_specs...  2.24 us
    pallas_call x1, Pallas kernels, on_device(): pl.pallas_call(functools.partial(send_kernel, total_vertices, paired), in...  2.09 us
    ppermute x6, waiting for transfers between devices, group_swap(): lax.ppermute(messages[mask], 'clus', [(i, i ^ 2 * mask) for i in range(me...  1.85 us
    pallas_call x1, Pallas kernels, on_device(): pl.pallas_call(functools.partial(final_kernel, paired), in_specs=[VMEM] *...  1.48 us
    pallas_call x1, Pallas kernels, on_device(): pl.pallas_call(local_kernel, in_specs=[VMEM] * 7, out_specs=[VMEM] * 6, o...  1.33 us
  transfers between devices with their start and end apart: 12, of which 2 were waited for; matrix products, arithmetic and copies ran while one was open for 0% of the time, Pallas kernels for 15%

profile of v4, /device:TPU:0, one launch (start us, length us, event | category | flops | bytes accessed | tf_op | source)
XLA Modules:
  0.0 24.0 jit_solution(8240847619354166118)
XLA Ops:
  0.0 2.1 %send.1 = (f32[64,128]{1,0:T(8,128)S(1)}, f32[64,128]{1,0:T(8,128)S(1)}, f32[64,128]{1,0:T(8,128)S(1)}, f32[64,128]{1,0:T(8,128)S(1)}, bf16[144,1536]{1,0:T(8,12...) custom-call(f32[512,256]{1,0:T(8,128)} %nodal_hbm.3, ...), custom_call_target="tpu_custom_call" | custom-call | tf_op jit(solution)/shard_map/send/pallas_call | solution.py:590
  2.1 0.5 %collective-permute-start.2 = (f32[64,128]{1,0:T(8,128)S(1)}, f32[64,128]{1,0:T(8,128)S(1)}, u32[]{:S(2)}, u32[]{:S(2)}) collective-permute-start(f32[64,128]{1,0:T(8,128)S(1)} %get-tuple-element.55), channel_id=1, source_target_pairs={{0,1},{1,0},{2,3},{3,2},{4,5},{5,4},{6,7},{7,6},{8,9},{9,8},{10,11... | collective-permute-start | bytes 98312 | tf_op jit(solution)/shard_map/ppermute | solution.py:555
  2.6 2.7 %collective-permute-start = (f32[64,128]{1,0:T(8,128)S(1)}, f32[64,128]{1,0:T(8,128)S(1)}, u32[]{:S(2)}, u32[]{:S(2)}) collective-permute-start(f32[64,128]{1,0:T(8,128)S(1)} %get-tuple-element.43), channel_id=1, source_target_pairs={{0,8},{8,0},{16,24},{24,16},{1,9},{9,1},{17,25},{25,17},{2,10},{10... | collective-permute-start | bytes 98312 | tf_op jit(solution)/shard_map/ppermute | solution.py:549
  5.3 2.5 %collective-permute-start.1 = (f32[64,128]{1,0:T(8,128)S(1)}, f32[64,128]{1,0:T(8,128)S(1)}, u32[]{:S(2)}, u32[]{:S(2)}) collective-permute-start(f32[64,128]{1,0:T(8,128)S(1)} %get-tuple-element.44), channel_id=1, source_target_pairs={{0,24},{8,16},{16,8},{24,0},{1,25},{9,17},{17,9},{25,1},{2,26},{10... | collective-permute-start | bytes 98312 | tf_op jit(solution)/shard_map/ppermute | solution.py:549
  7.7 0.0 collective-permute-done.2.cross_ref
  7.8 2.5 %collective-permute-start.3 = (f32[32,128]{1,0:T(8,128)S(1)}, f32[32,128]{1,0:T(8,128)S(1)}, u32[]{:S(2)}, u32[]{:S(2)}) collective-permute-start(f32[32,128]{1,0:T(8,128)S(1)} %get-tuple-element.57), channel_id=1, source_target_pairs={{0,6},{1,7},{2,4},{3,5},{4,2},{5,3},{6,0},{7,1},{8,14},{9,15},{10,... | collective-permute-start | bytes 49160 | tf_op jit(solution)/shard_map/ppermute | solution.py:565
  10.3 0.5 %collective-permute-start.4 = (f32[32,128]{1,0:T(8,128)S(1)}, f32[32,128]{1,0:T(8,128)S(1)}, u32[]{:S(2)}, u32[]{:S(2)}) collective-permute-start(f32[32,128]{1,0:T(8,128)S(1)} %get-tuple-element.58), channel_id=1, source_target_pairs={{0,4},{1,5},{2,6},{3,7},{4,0},{5,1},{6,2},{7,3},{8,12},{9,13},{10,... | collective-permute-start | bytes 49160 | tf_op jit(solution)/shard_map/ppermute | solution.py:565
  10.8 0.5 %collective-permute-start.5 = (f32[32,128]{1,0:T(8,128)S(1)}, f32[32,128]{1,0:T(8,128)S(1)}, u32[]{:S(2)}, u32[]{:S(2)}) collective-permute-start(f32[32,128]{1,0:T(8,128)S(1)} %get-tuple-element.59), channel_id=1, source_target_pairs={{0,2},{1,3},{2,0},{3,1},{4,6},{5,7},{6,4},{7,5},{8,10},{9,11},{10,... | collective-permute-start | bytes 49160 | tf_op jit(solution)/shard_map/ppermute | solution.py:565
  11.3 1.3 %local.1 = (f32[64,512]{1,0:T(8,128)S(1)}, f32[64,384]{1,0:T(8,128)S(1)}, bf16[384,384]{1,0:T(8,128)(2,1)S(1)}, bf16[256,192]{1,0:T(8,128)(2,1)S(1)}, bf16[128,1...) custom-call(bf16[144,1536]{1,0:T(8,128)(2,1)S(1)} %get-tuple-element.45.traces_ref, ...), custom_call_target="tpu_custom_call" | custom-call | flops 1500000000 | bytes 6000000 | tf_op jit(solution)/shard_map/local/pallas_call | solution.py:623
  12.7 0.0 collective-permute-done.1.far_in_ref
  12.7 1.3 %collective-permute-done.4.refs_2_ = f32[32,128]{1,0:T(8,128)S(1)} collective-permute-done((f32[32,128]{1,0:T(8,128)S(1)}, f32[32,128]{1,0:T(8,128)S(1)}, u32[]{:S(2)}, u32[]{:S(2)}) %collective-permute-start.4) | collective-permute-done | bytes 16416 | tf_op jit(solution)/shard_map/ppermute | solution.py:565
  14.0 0.5 %collective-permute-done.5.refs_3_ = f32[32,128]{1,0:T(8,128)S(1)} collective-permute-done((f32[32,128]{1,0:T(8,128)S(1)}, f32[32,128]{1,0:T(8,128)S(1)}, u32[]{:S(2)}, u32[]{:S(2)}) %collective-permute-start.5) | collective-permute-done | bytes 16416 | tf_op jit(solution)/shard_map/ppermute | solution.py:565
  14.5 0.4 %answer.1 = (f32[72,128]{1,0:T(8,128)S(1)}, f32[72,128]{1,0:T(8,128)S(1)}, f32[64,128]{1,0:T(8,128)S(1)}, f32[64,128]{1,0:T(8,128)S(1)}, f32[64,384]{1,0:T(8,128)S(1)}, /*index=5*/f32[16,128]{1,0:T(8,128)S(1)}) custom-call(f32[64,128]{1,0:T(8,128)S(1)} %collective-permute-done.near_in_ref, f32[64,128]{1,0:T(8,128)S(1)} %collective-permute-done.1.far_in_ref, ...), custom_call_target="tpu_custom_call" | custom-call | tf_op jit(solution)/shard_map/answer/pallas_call | solution.py:640
  14.9 0.1 collective-permute-start.8
  15.0 0.7 %collective-permute-start.6 = (f32[72,128]{1,0:T(8,128)S(1)}, f32[72,128]{1,0:T(8,128)S(1)}, u32[]{:S(2)}, u32[]{:S(2)}) collective-permute-start(f32[72,128]{1,0:T(8,128)S(1)} %get-tuple-element.60), channel_id=1, source_target_pairs={{0,8},{8,0},{16,24},{24,16},{1,9},{9,1},{17,25},{25,17},{2,10},{10... | collective-permute-start | bytes 110600 | tf_op jit(solution)/shard_map/ppermute | solution.py:549
  15.7 0.9 %collective-permute-start.7 = (f32[72,128]{1,0:T(8,128)S(1)}, f32[72,128]{1,0:T(8,128)S(1)}, u32[]{:S(2)}, u32[]{:S(2)}) collective-permute-start(f32[72,128]{1,0:T(8,128)S(1)} %get-tuple-element.61), channel_id=1, source_target_pairs={{0,24},{8,16},{16,8},{24,0},{1,25},{9,17},{17,9},{25,1},{2,26},{10... | collective-permute-start | bytes 110600 | tf_op jit(solution)/shard_map/ppermute | solution.py:549
  16.6 1.6 %collective-permute-start.9 = (f32[32,128]{1,0:T(8,128)S(1)}, f32[32,128]{1,0:T(8,128)S(1)}, u32[]{:S(2)}, u32[]{:S(2)}) collective-permute-start(f32[32,128]{1,0:T(8,128)S(1)} %get-tuple-element.78), channel_id=1, source_target_pairs={{0,6},{1,7},{2,4},{3,5},{4,2},{5,3},{6,0},{7,1},{8,14},{9,15},{10,... | collective-permute-start | bytes 49160 | tf_op jit(solution)/shard_map/ppermute | solution.py:565
  18.2 0.5 %collective-permute-start.10 = (f32[32,128]{1,0:T(8,128)S(1)}, f32[32,128]{1,0:T(8,128)S(1)}, u32[]{:S(2)}, u32[]{:S(2)}) collective-permute-start(f32[32,128]{1,0:T(8,128)S(1)} %get-tuple-element.79), channel_id=1, source_target_pairs={{0,4},{1,5},{2,6},{3,7},{4,0},{5,1},{6,2},{7,3},{8,12},{9,13},{10,... | collective-permute-start | bytes 49160 | tf_op jit(solution)/shard_map/ppermute | solution.py:565
  18.7 1.5 %collective-permute-start.11 = (f32[32,128]{1,0:T(8,128)S(1)}, f32[32,128]{1,0:T(8,128)S(1)}, u32[]{:S(2)}, u32[]{:S(2)}) collective-permute-start(f32[32,128]{1,0:T(8,128)S(1)} %get-tuple-element.80), channel_id=1, source_target_pairs={{0,2},{1,3},{2,0},{3,1},{4,6},{5,7},{6,4},{7,5},{8,10},{9,11},{10,... | collective-permute-start | bytes 49160 | tf_op jit(solution)/shard_map/ppermute | solution.py:565
  20.2 2.2 %gather.1 = (f32[2,512,128]{2,1,0:T(8,128)S(1)}, bf16[384,1536]{1,0:T(8,128)(2,1)S(1)}, bf16[128,2048]{1,0:T(8,128)(2,1)S(1)}, s32[8,256]{1,0:T(8,128)S(1)}) custom-call(f32[512,256]{1,0:T(8,128)} %nodal_hbm.3, bf16[3,512,256]{2,1,0:T(8,128)(2,1)} %metric_hbm.1, f32[64,512]{1,0:T(8,128)S(1)} %get-tuple-element.64.mortar_ref, ...), custom_call_target="tpu_custom_call" | custom-call | flops 1500000000 | bytes 6000000 | tf_op jit(solution)/shard_map/gather/pallas_call | solution.py:660
  22.5 0.0 collective-permute-done.6.near_in_ref
  22.5 0.0 collective-permute-done.7.far_in_ref
  22.5 0.0 collective-permute-done.10.refs_2_
  22.5 1.5 %final.1 = f32[512,256]{1,0:T(8,128)} custom-call(f32[72,128]{1,0:T(8,128)S(1)} %collective-permute-done.6.near_in_ref, f32[72,128]{1,0:T(8,128)S(1)} %collective-permute-done.7.far_in_ref, f32[8,384]{1,0:T(8,128)S(1)} %get-tuple-element.62.slot_level_ref, bf16[256,192]{1,0:T(8,128)(2,1)S(1)} %get-tuple-element.63.back_maps_ref.maps_ref, ...), custom_call_target="tpu_custom_call" | custom-call | tf_op jit(solution)/shard_map/final/pallas_call | solution.py:686
  (7 shorter events, 0.0 us)
Async XLA Ops:
  2.1 5.6 %collective-permute-start.2 = (f32[64,128]{1,0:T(8,128)S(1)}, f32[64,128]{1,0:T(8,128)S(1)}, u32[]{:S(2)}, u32[]{:S(2)}) collective-permute-start(f32[64,128]{1,0:T(8,128)S(1)} %get-tuple-element.55), channel_id=1, source_target_pairs={{0,1},{1,0},{2,3},{3,2},{4,5},{5,4},{6,7},{7,6},{8,9},{9,8},{10,11... | collective-permute-start | bytes 98312 | tf_op jit(solution)/shard_map/ppermute | solution.py:555
  2.6 10.0 %collective-permute-start = (f32[64,128]{1,0:T(8,128)S(1)}, f32[64,128]{1,0:T(8,128)S(1)}, u32[]{:S(2)}, u32[]{:S(2)}) collective-permute-start(f32[64,128]{1,0:T(8,128)S(1)} %get-tuple-element.43), channel_id=1, source_target_pairs={{0,8},{8,0},{16,24},{24,16},{1,9},{9,1},{17,25},{25,17},{2,10},{10... | collective-permute-start | bytes 98312 | tf_op jit(solution)/shard_map/ppermute | solution.py:549
  5.3 7.4 %collective-permute-start.1 = (f32[64,128]{1,0:T(8,128)S(1)}, f32[64,128]{1,0:T(8,128)S(1)}, u32[]{:S(2)}, u32[]{:S(2)}) collective-permute-start(f32[64,128]{1,0:T(8,128)S(1)} %get-tuple-element.44), channel_id=1, source_target_pairs={{0,24},{8,16},{16,8},{24,0},{1,25},{9,17},{17,9},{25,1},{2,26},{10... | collective-permute-start | bytes 98312 | tf_op jit(solution)/shard_map/ppermute | solution.py:549
  7.8 4.9 %collective-permute-start.3 = (f32[32,128]{1,0:T(8,128)S(1)}, f32[32,128]{1,0:T(8,128)S(1)}, u32[]{:S(2)}, u32[]{:S(2)}) collective-permute-start(f32[32,128]{1,0:T(8,128)S(1)} %get-tuple-element.57), channel_id=1, source_target_pairs={{0,6},{1,7},{2,4},{3,5},{4,2},{5,3},{6,0},{7,1},{8,14},{9,15},{10,... | collective-permute-start | bytes 49160 | tf_op jit(solution)/shard_map/ppermute | solution.py:565
  10.3 3.7 %collective-permute-start.4 = (f32[32,128]{1,0:T(8,128)S(1)}, f32[32,128]{1,0:T(8,128)S(1)}, u32[]{:S(2)}, u32[]{:S(2)}) collective-permute-start(f32[32,128]{1,0:T(8,128)S(1)} %get-tuple-element.58), channel_id=1, source_target_pairs={{0,4},{1,5},{2,6},{3,7},{4,0},{5,1},{6,2},{7,3},{8,12},{9,13},{10,... | collective-permute-start | bytes 49160 | tf_op jit(solution)/shard_map/ppermute | solution.py:565
  10.8 3.7 %collective-permute-start.5 = (f32[32,128]{1,0:T(8,128)S(1)}, f32[32,128]{1,0:T(8,128)S(1)}, u32[]{:S(2)}, u32[]{:S(2)}) collective-permute-start(f32[32,128]{1,0:T(8,128)S(1)} %get-tuple-element.59), channel_id=1, source_target_pairs={{0,2},{1,3},{2,0},{3,1},{4,6},{5,7},{6,4},{7,5},{8,10},{9,11},{10,... | collective-permute-start | bytes 49160 | tf_op jit(solution)/shard_map/ppermute | solution.py:565
  14.9 1.7 %collective-permute-start.8 = (f32[64,128]{1,0:T(8,128)S(1)}, f32[64,128]{1,0:T(8,128)S(1)}, u32[]{:S(2)}, u32[]{:S(2)}) collective-permute-start(f32[64,128]{1,0:T(8,128)S(1)} %get-tuple-element.76), channel_id=1, source_target_pairs={{0,1},{1,0},{2,3},{3,2},{4,5},{5,4},{6,7},{7,6},{8,9},{9,8},{10,11... | collective-permute-start | bytes 98312 | tf_op jit(solution)/shard_map/ppermute | solution.py:555
  15.0 7.5 %collective-permute-start.6 = (f32[72,128]{1,0:T(8,128)S(1)}, f32[72,128]{1,0:T(8,128)S(1)}, u32[]{:S(2)}, u32[]{:S(2)}) collective-permute-start(f32[72,128]{1,0:T(8,128)S(1)} %get-tuple-element.60), channel_id=1, source_target_pairs={{0,8},{8,0},{16,24},{24,16},{1,9},{9,1},{17,25},{25,17},{2,10},{10... | collective-permute-start | bytes 110600 | tf_op jit(solution)/shard_map/ppermute | solution.py:549
  15.7 6.7 %collective-permute-start.7 = (f32[72,128]{1,0:T(8,128)S(1)}, f32[72,128]{1,0:T(8,128)S(1)}, u32[]{:S(2)}, u32[]{:S(2)}) collective-permute-start(f32[72,128]{1,0:T(8,128)S(1)} %get-tuple-element.61), channel_id=1, source_target_pairs={{0,24},{8,16},{16,8},{24,0},{1,25},{9,17},{17,9},{25,1},{2,26},{10... | collective-permute-start | bytes 110600 | tf_op jit(solution)/shard_map/ppermute | solution.py:549
  16.6 5.8 %collective-permute-start.9 = (f32[32,128]{1,0:T(8,128)S(1)}, f32[32,128]{1,0:T(8,128)S(1)}, u32[]{:S(2)}, u32[]{:S(2)}) collective-permute-start(f32[32,128]{1,0:T(8,128)S(1)} %get-tuple-element.78), channel_id=1, source_target_pairs={{0,6},{1,7},{2,4},{3,5},{4,2},{5,3},{6,0},{7,1},{8,14},{9,15},{10,... | collective-permute-start | bytes 49160 | tf_op jit(solution)/shard_map/ppermute | solution.py:565
  18.2 4.3 %collective-permute-start.10 = (f32[32,128]{1,0:T(8,128)S(1)}, f32[32,128]{1,0:T(8,128)S(1)}, u32[]{:S(2)}, u32[]{:S(2)}) collective-permute-start(f32[32,128]{1,0:T(8,128)S(1)} %get-tuple-element.79), channel_id=1, source_target_pairs={{0,4},{1,5},{2,6},{3,7},{4,0},{5,1},{6,2},{7,3},{8,12},{9,13},{10,... | collective-permute-start | bytes 49160 | tf_op jit(solution)/shard_map/ppermute | solution.py:565
  18.7 3.8 %collective-permute-start.11 = (f32[32,128]{1,0:T(8,128)S(1)}, f32[32,128]{1,0:T(8,128)S(1)}, u32[]{:S(2)}, u32[]{:S(2)}) collective-permute-start(f32[32,128]{1,0:T(8,128)S(1)} %get-tuple-element.80), channel_id=1, source_target_pairs={{0,2},{1,3},{2,0},{3,1},{4,6},{5,7},{6,4},{7,5},{8,10},{9,11},{10,... | collective-permute-start | bytes 49160 | tf_op jit(solution)/shard_map/ppermute | solution.py:565

commit v5 on v4

--- a/solution.py
+++ b/solution.py
@@ -160,7 +160,7 @@
 
 def member_rows(mask):
     member = lax.axis_index("clus")
-    same = jnp.bitwise_xor(member, 2 * mask)
+    same = jnp.bitwise_xor(member, 2 * mask + (mask > 0))
     other = jnp.bitwise_xor(same, 1)
     return pl.ds(pl.multiple_of(same * 16, 16), 16), pl.ds(pl.multiple_of(other * 16, 16), 16)
 
@@ -562,7 +562,7 @@
         name="merge",
     )(keep, cross)
     return [messages[0]] + [
-        lax.ppermute(messages[mask], "clus", [(i, i ^ (2 * mask)) for i in range(members)])
+        lax.ppermute(messages[mask], "clus", [(i, i ^ (2 * mask + 1)) for i in range(members)])
         for mask in chip_masks(chips)[1:]
     ]
 

time: 24.2 us -> 22.8 us (0.942)
  starting transfers between devices: 14.5 us -> 13 us
    ppermute x6, starting transfers between devices: 7.11 us -> 5.69 us  [group_swap(): lax.ppermute(messages[mask], 'clus', [(i, i ^ 2 * mask + 1) for i in rang...]
  transfers between devices with their start and end apart: 12 -> 12, of which waited for: 2 -> 2; matrix products, arithmetic and copies ran while one was open for 0% -> 0% of each run, Pallas kernels for 15% -> 16%
where the time goes in v5:
time: 22.8 us; the launch traced here: 22.5 us
  starting transfers between devices  13 us (57%)
  Pallas kernels  7.52 us (33%)
  waiting for transfers between devices  1.8 us (8%)
    ppermute x6, starting transfers between devices, group_swap(): lax.ppermute(messages[mask], 'clus', [(i, i ^ 2 * mask + 1) for i in rang...  5.69 us
    ppermute x2, starting transfers between devices, curve_swap(): lax.ppermute(near, 'elem', near_pairs)  3.38 us
    ppermute x2, starting transfers between devices, curve_swap(): lax.ppermute(far, 'elem', far_pairs)  3.29 us
    pallas_call x1, Pallas kernels, on_device(): pl.pallas_call(functools.partial(gather_kernel, total_vertices), in_specs...  2.24 us
    pallas_call x1, Pallas kernels, on_device(): pl.pallas_call(functools.partial(send_kernel, total_vertices, paired), in...  2.09 us
    ppermute x6, waiting for transfers between devices, group_swap(): lax.ppermute(messages[mask], 'clus', [(i, i ^ 2 * mask + 1) for i in rang...  1.78 us
    pallas_call x1, Pallas kernels, on_device(): pl.pallas_call(functools.partial(final_kernel, paired), in_specs=[VMEM] *...  1.48 us
    pallas_call x1, Pallas kernels, on_device(): pl.pallas_call(local_kernel, in_specs=[VMEM] * 7, out_specs=[VMEM] * 6, o...  1.31 us
  transfers between devices with their start and end apart: 12, of which 2 were waited for; matrix products, arithmetic and copies ran while one was open for 0% of the time, Pallas kernels for 16%

profile of v5, /device:TPU:0, one launch (start us, length us, event | category | flops | bytes accessed | tf_op | source)
XLA Modules:
  0.0 22.5 jit_solution(285290961146151382)
XLA Ops:
  0.0 2.1 %send.1 = (f32[64,128]{1,0:T(8,128)S(1)}, f32[64,128]{1,0:T(8,128)S(1)}, f32[64,128]{1,0:T(8,128)S(1)}, f32[64,128]{1,0:T(8,128)S(1)}, bf16[144,1536]{1,0:T(8,12...) custom-call(f32[512,256]{1,0:T(8,128)} %nodal_hbm.3, ...), custom_call_target="tpu_custom_call" | custom-call | tf_op jit(solution)/shard_map/send/pallas_call | solution.py:590
  2.1 0.5 %collective-permute-start.2 = (f32[64,128]{1,0:T(8,128)S(1)}, f32[64,128]{1,0:T(8,128)S(1)}, u32[]{:S(2)}, u32[]{:S(2)}) collective-permute-start(f32[64,128]{1,0:T(8,128)S(1)} %get-tuple-element.55), channel_id=1, source_target_pairs={{0,1},{1,0},{2,3},{3,2},{4,5},{5,4},{6,7},{7,6},{8,9},{9,8},{10,11... | collective-permute-start | bytes 98312 | tf_op jit(solution)/shard_map/ppermute | solution.py:555
  2.6 2.7 %collective-permute-start = (f32[64,128]{1,0:T(8,128)S(1)}, f32[64,128]{1,0:T(8,128)S(1)}, u32[]{:S(2)}, u32[]{:S(2)}) collective-permute-start(f32[64,128]{1,0:T(8,128)S(1)} %get-tuple-element.43), channel_id=1, source_target_pairs={{0,8},{8,0},{16,24},{24,16},{1,9},{9,1},{17,25},{25,17},{2,10},{10... | collective-permute-start | bytes 98312 | tf_op jit(solution)/shard_map/ppermute | solution.py:549
  5.3 2.5 %collective-permute-start.1 = (f32[64,128]{1,0:T(8,128)S(1)}, f32[64,128]{1,0:T(8,128)S(1)}, u32[]{:S(2)}, u32[]{:S(2)}) collective-permute-start(f32[64,128]{1,0:T(8,128)S(1)} %get-tuple-element.44), channel_id=1, source_target_pairs={{0,24},{8,16},{16,8},{24,0},{1,25},{9,17},{17,9},{25,1},{2,26},{10... | collective-permute-start | bytes 98312 | tf_op jit(solution)/shard_map/ppermute | solution.py:549
  7.8 0.0 collective-permute-done.2.cross_ref
  7.8 2.0 %collective-permute-start.3 = (f32[32,128]{1,0:T(8,128)S(1)}, f32[32,128]{1,0:T(8,128)S(1)}, u32[]{:S(2)}, u32[]{:S(2)}) collective-permute-start(f32[32,128]{1,0:T(8,128)S(1)} %get-tuple-element.57), channel_id=1, source_target_pairs={{0,7},{1,6},{2,5},{3,4},{4,3},{5,2},{6,1},{7,0},{8,15},{9,14},{10,... | collective-permute-start | bytes 49160 | tf_op jit(solution)/shard_map/ppermute | solution.py:565
  9.8 0.7 %collective-permute-start.4 = (f32[32,128]{1,0:T(8,128)S(1)}, f32[32,128]{1,0:T(8,128)S(1)}, u32[]{:S(2)}, u32[]{:S(2)}) collective-permute-start(f32[32,128]{1,0:T(8,128)S(1)} %get-tuple-element.58), channel_id=1, source_target_pairs={{0,5},{1,4},{2,7},{3,6},{4,1},{5,0},{6,3},{7,2},{8,13},{9,12},{10,... | collective-permute-start | bytes 49160 | tf_op jit(solution)/shard_map/ppermute | solution.py:565
  10.5 0.1 collective-permute-start.5
  10.6 1.3 %local.1 = (f32[64,512]{1,0:T(8,128)S(1)}, f32[64,384]{1,0:T(8,128)S(1)}, bf16[384,384]{1,0:T(8,128)(2,1)S(1)}, bf16[256,192]{1,0:T(8,128)(2,1)S(1)}, bf16[128,1...) custom-call(bf16[144,1536]{1,0:T(8,128)(2,1)S(1)} %get-tuple-element.45.traces_ref, ...), custom_call_target="tpu_custom_call" | custom-call | flops 1500000000 | bytes 6000000 | tf_op jit(solution)/shard_map/local/pallas_call | solution.py:623
  12.0 0.0 collective-permute-done.near_in_ref
  12.0 0.0 collective-permute-done.1.far_in_ref
  12.0 0.0 collective-permute-done.3.refs_1_
  12.0 0.9 %collective-permute-done.4.refs_2_ = f32[32,128]{1,0:T(8,128)S(1)} collective-permute-done((f32[32,128]{1,0:T(8,128)S(1)}, f32[32,128]{1,0:T(8,128)S(1)}, u32[]{:S(2)}, u32[]{:S(2)}) %collective-permute-start.4) | collective-permute-done | bytes 16416 | tf_op jit(solution)/shard_map/ppermute | solution.py:565
  12.9 0.8 %collective-permute-done.5.refs_3_ = f32[32,128]{1,0:T(8,128)S(1)} collective-permute-done((f32[32,128]{1,0:T(8,128)S(1)}, f32[32,128]{1,0:T(8,128)S(1)}, u32[]{:S(2)}, u32[]{:S(2)}) %collective-permute-start.5) | collective-permute-done | bytes 16416 | tf_op jit(solution)/shard_map/ppermute | solution.py:565
  13.8 0.4 %answer.1 = (f32[72,128]{1,0:T(8,128)S(1)}, f32[72,128]{1,0:T(8,128)S(1)}, f32[64,128]{1,0:T(8,128)S(1)}, f32[64,128]{1,0:T(8,128)S(1)}, f32[64,384]{1,0:T(8,128)S(1)}, /*index=5*/f32[16,128]{1,0:T(8,128)S(1)}) custom-call(f32[64,128]{1,0:T(8,128)S(1)} %collective-permute-done.near_in_ref, f32[64,128]{1,0:T(8,128)S(1)} %collective-permute-done.1.far_in_ref, ...), custom_call_target="tpu_custom_call" | custom-call | tf_op jit(solution)/shard_map/answer/pallas_call | solution.py:640
  14.2 0.2 collective-permute-start.8
  14.3 0.7 %collective-permute-start.6 = (f32[72,128]{1,0:T(8,128)S(1)}, f32[72,128]{1,0:T(8,128)S(1)}, u32[]{:S(2)}, u32[]{:S(2)}) collective-permute-start(f32[72,128]{1,0:T(8,128)S(1)} %get-tuple-element.60), channel_id=1, source_target_pairs={{0,8},{8,0},{16,24},{24,16},{1,9},{9,1},{17,25},{25,17},{2,10},{10... | collective-permute-start | bytes 110600 | tf_op jit(solution)/shard_map/ppermute | solution.py:549
  15.1 0.8 %collective-permute-start.7 = (f32[72,128]{1,0:T(8,128)S(1)}, f32[72,128]{1,0:T(8,128)S(1)}, u32[]{:S(2)}, u32[]{:S(2)}) collective-permute-start(f32[72,128]{1,0:T(8,128)S(1)} %get-tuple-element.61), channel_id=1, source_target_pairs={{0,24},{8,16},{16,8},{24,0},{1,25},{9,17},{17,9},{25,1},{2,26},{10... | collective-permute-start | bytes 110600 | tf_op jit(solution)/shard_map/ppermute | solution.py:549
  15.9 1.1 %collective-permute-start.9 = (f32[32,128]{1,0:T(8,128)S(1)}, f32[32,128]{1,0:T(8,128)S(1)}, u32[]{:S(2)}, u32[]{:S(2)}) collective-permute-start(f32[32,128]{1,0:T(8,128)S(1)} %get-tuple-element.78), channel_id=1, source_target_pairs={{0,7},{1,6},{2,5},{3,4},{4,3},{5,2},{6,1},{7,0},{8,15},{9,14},{10,... | collective-permute-start | bytes 49160 | tf_op jit(solution)/shard_map/ppermute | solution.py:565
  17.0 0.7 %collective-permute-start.10 = (f32[32,128]{1,0:T(8,128)S(1)}, f32[32,128]{1,0:T(8,128)S(1)}, u32[]{:S(2)}, u32[]{:S(2)}) collective-permute-start(f32[32,128]{1,0:T(8,128)S(1)} %get-tuple-element.79), channel_id=1, source_target_pairs={{0,5},{1,4},{2,7},{3,6},{4,1},{5,0},{6,3},{7,2},{8,13},{9,12},{10,... | collective-permute-start | bytes 49160 | tf_op jit(solution)/shard_map/ppermute | solution.py:565
  17.7 1.0 %collective-permute-start.11 = (f32[32,128]{1,0:T(8,128)S(1)}, f32[32,128]{1,0:T(8,128)S(1)}, u32[]{:S(2)}, u32[]{:S(2)}) collective-permute-start(f32[32,128]{1,0:T(8,128)S(1)} %get-tuple-element.80), channel_id=1, source_target_pairs={{0,3},{1,2},{2,1},{3,0},{4,7},{5,6},{6,5},{7,4},{8,11},{9,10},{10,... | collective-permute-start | bytes 49160 | tf_op jit(solution)/shard_map/ppermute | solution.py:565
  18.7 2.2 %gather.1 = (f32[2,512,128]{2,1,0:T(8,128)S(1)}, bf16[384,1536]{1,0:T(8,128)(2,1)S(1)}, bf16[128,2048]{1,0:T(8,128)(2,1)S(1)}, s32[8,256]{1,0:T(8,128)S(1)}) custom-call(f32[512,256]{1,0:T(8,128)} %nodal_hbm.3, bf16[3,512,256]{2,1,0:T(8,128)(2,1)} %metric_hbm.1, f32[64,512]{1,0:T(8,128)S(1)} %get-tuple-element.64.mortar_ref, ...), custom_call_target="tpu_custom_call" | custom-call | flops 1500000000 | bytes 6000000 | tf_op jit(solution)/shard_map/gather/pallas_call | solution.py:660
  21.0 0.0 collective-permute-done.9.refs_1_
  21.0 1.5 %final.1 = f32[512,256]{1,0:T(8,128)} custom-call(f32[72,128]{1,0:T(8,128)S(1)} %collective-permute-done.6.near_in_ref, f32[72,128]{1,0:T(8,128)S(1)} %collective-permute-done.7.far_in_ref, f32[8,384]{1,0:T(8,128)S(1)} %get-tuple-element.62.slot_level_ref, bf16[256,192]{1,0:T(8,128)(2,1)S(1)} %get-tuple-element.63.back_maps_ref.maps_ref, ...), custom_call_target="tpu_custom_call" | custom-call | tf_op jit(solution)/shard_map/final/pallas_call | solution.py:686
  (7 shorter events, 0.0 us)
Async XLA Ops:
  2.1 5.6 %collective-permute-start.2 = (f32[64,128]{1,0:T(8,128)S(1)}, f32[64,128]{1,0:T(8,128)S(1)}, u32[]{:S(2)}, u32[]{:S(2)}) collective-permute-start(f32[64,128]{1,0:T(8,128)S(1)} %get-tuple-element.55), channel_id=1, source_target_pairs={{0,1},{1,0},{2,3},{3,2},{4,5},{5,4},{6,7},{7,6},{8,9},{9,8},{10,11... | collective-permute-start | bytes 98312 | tf_op jit(solution)/shard_map/ppermute | solution.py:555
  2.6 9.3 %collective-permute-start = (f32[64,128]{1,0:T(8,128)S(1)}, f32[64,128]{1,0:T(8,128)S(1)}, u32[]{:S(2)}, u32[]{:S(2)}) collective-permute-start(f32[64,128]{1,0:T(8,128)S(1)} %get-tuple-element.43), channel_id=1, source_target_pairs={{0,8},{8,0},{16,24},{24,16},{1,9},{9,1},{17,25},{25,17},{2,10},{10... | collective-permute-start | bytes 98312 | tf_op jit(solution)/shard_map/ppermute | solution.py:549
  5.3 6.7 %collective-permute-start.1 = (f32[64,128]{1,0:T(8,128)S(1)}, f32[64,128]{1,0:T(8,128)S(1)}, u32[]{:S(2)}, u32[]{:S(2)}) collective-permute-start(f32[64,128]{1,0:T(8,128)S(1)} %get-tuple-element.44), channel_id=1, source_target_pairs={{0,24},{8,16},{16,8},{24,0},{1,25},{9,17},{17,9},{25,1},{2,26},{10... | collective-permute-start | bytes 98312 | tf_op jit(solution)/shard_map/ppermute | solution.py:549
  7.8 4.2 %collective-permute-start.3 = (f32[32,128]{1,0:T(8,128)S(1)}, f32[32,128]{1,0:T(8,128)S(1)}, u32[]{:S(2)}, u32[]{:S(2)}) collective-permute-start(f32[32,128]{1,0:T(8,128)S(1)} %get-tuple-element.57), channel_id=1, source_target_pairs={{0,7},{1,6},{2,5},{3,4},{4,3},{5,2},{6,1},{7,0},{8,15},{9,14},{10,... | collective-permute-start | bytes 49160 | tf_op jit(solution)/shard_map/ppermute | solution.py:565
  9.8 3.2 %collective-permute-start.4 = (f32[32,128]{1,0:T(8,128)S(1)}, f32[32,128]{1,0:T(8,128)S(1)}, u32[]{:S(2)}, u32[]{:S(2)}) collective-permute-start(f32[32,128]{1,0:T(8,128)S(1)} %get-tuple-element.58), channel_id=1, source_target_pairs={{0,5},{1,4},{2,7},{3,6},{4,1},{5,0},{6,3},{7,2},{8,13},{9,12},{10,... | collective-permute-start | bytes 49160 | tf_op jit(solution)/shard_map/ppermute | solution.py:565
  10.5 3.3 %collective-permute-start.5 = (f32[32,128]{1,0:T(8,128)S(1)}, f32[32,128]{1,0:T(8,128)S(1)}, u32[]{:S(2)}, u32[]{:S(2)}) collective-permute-start(f32[32,128]{1,0:T(8,128)S(1)} %get-tuple-element.59), channel_id=1, source_target_pairs={{0,3},{1,2},{2,1},{3,0},{4,7},{5,6},{6,5},{7,4},{8,11},{9,10},{10,... | collective-permute-start | bytes 49160 | tf_op jit(solution)/shard_map/ppermute | solution.py:565
  14.2 1.7 %collective-permute-start.8 = (f32[64,128]{1,0:T(8,128)S(1)}, f32[64,128]{1,0:T(8,128)S(1)}, u32[]{:S(2)}, u32[]{:S(2)}) collective-permute-start(f32[64,128]{1,0:T(8,128)S(1)} %get-tuple-element.76), channel_id=1, source_target_pairs={{0,1},{1,0},{2,3},{3,2},{4,5},{5,4},{6,7},{7,6},{8,9},{9,8},{10,11... | collective-permute-start | bytes 98312 | tf_op jit(solution)/shard_map/ppermute | solution.py:555
  14.3 6.6 %collective-permute-start.6 = (f32[72,128]{1,0:T(8,128)S(1)}, f32[72,128]{1,0:T(8,128)S(1)}, u32[]{:S(2)}, u32[]{:S(2)}) collective-permute-start(f32[72,128]{1,0:T(8,128)S(1)} %get-tuple-element.60), channel_id=1, source_target_pairs={{0,8},{8,0},{16,24},{24,16},{1,9},{9,1},{17,25},{25,17},{2,10},{10... | collective-permute-start | bytes 110600 | tf_op jit(solution)/shard_map/ppermute | solution.py:549
  15.1 5.9 %collective-permute-start.7 = (f32[72,128]{1,0:T(8,128)S(1)}, f32[72,128]{1,0:T(8,128)S(1)}, u32[]{:S(2)}, u32[]{:S(2)}) collective-permute-start(f32[72,128]{1,0:T(8,128)S(1)} %get-tuple-element.61), channel_id=1, source_target_pairs={{0,24},{8,16},{16,8},{24,0},{1,25},{9,17},{17,9},{25,1},{2,26},{10... | collective-permute-start | bytes 110600 | tf_op jit(solution)/shard_map/ppermute | solution.py:549
  15.9 5.1 %collective-permute-start.9 = (f32[32,128]{1,0:T(8,128)S(1)}, f32[32,128]{1,0:T(8,128)S(1)}, u32[]{:S(2)}, u32[]{:S(2)}) collective-permute-start(f32[32,128]{1,0:T(8,128)S(1)} %get-tuple-element.78), channel_id=1, source_target_pairs={{0,7},{1,6},{2,5},{3,4},{4,3},{5,2},{6,1},{7,0},{8,15},{9,14},{10,... | collective-permute-start | bytes 49160 | tf_op jit(solution)/shard_map/ppermute | solution.py:565
  17.0 4.0 %collective-permute-start.10 = (f32[32,128]{1,0:T(8,128)S(1)}, f32[32,128]{1,0:T(8,128)S(1)}, u32[]{:S(2)}, u32[]{:S(2)}) collective-permute-start(f32[32,128]{1,0:T(8,128)S(1)} %get-tuple-element.79), channel_id=1, source_target_pairs={{0,5},{1,4},{2,7},{3,6},{4,1},{5,0},{6,3},{7,2},{8,13},{9,12},{10,... | collective-permute-start | bytes 49160 | tf_op jit(solution)/shard_map/ppermute | solution.py:565
  17.7 3.3 %collective-permute-start.11 = (f32[32,128]{1,0:T(8,128)S(1)}, f32[32,128]{1,0:T(8,128)S(1)}, u32[]{:S(2)}, u32[]{:S(2)}) collective-permute-start(f32[32,128]{1,0:T(8,128)S(1)} %get-tuple-element.80), channel_id=1, source_target_pairs={{0,3},{1,2},{2,1},{3,0},{4,7},{5,6},{6,5},{7,4},{8,11},{9,10},{10,... | collective-permute-start | bytes 49160 | tf_op jit(solution)/shard_map/ppermute | solution.py:565

commit v6 on v5

--- a/solution.py
+++ b/solution.py
@@ -307,6 +307,8 @@
 
 
 def local_kernel(
+    nodal_hbm,
+    metric_hbm,
     traces_ref,
     maps_ref,
     level_ref,
@@ -320,7 +322,16 @@
     back_maps_ref,
     grad_map_ref,
     div_map_ref,
+    nodal_ref,
+    metric_ref,
+    nodal_sems,
+    sem,
 ):
+    nodal_copies = lane_copies(nodal_hbm, nodal_ref, nodal_sems)
+    metric_copy = pltpu.make_async_copy(metric_hbm, metric_ref, sem)
+    for copy in nodal_copies:
+        copy.start()
+    metric_copy.start()
     back_maps_ref[...] = kron_four(interp_ref[0].T, interp_ref[1].T)
     slot_row = slot_mortar_ref[...]
     equal_ref[...] = (columns_of(slot_row)[:, 0:1] == slot_row).astype(f32).astype(bf16)
@@ -339,6 +350,9 @@
     grad_map_ref[0:SQ, :] = outer
     grad_map_ref[SQ:, :] = inner
     div_map_ref[...] = jnp.concatenate([outer_t, inner_t], axis=1)
+    for copy in nodal_copies:
+        copy.wait()
+    metric_copy.wait()
 
 
 def first_direction(nodal_ref, metric_ref, outer, outer_t, stiff_ref, by_row):
@@ -398,8 +412,8 @@
 
 def gather_kernel(
     total_vertices,
-    nodal_hbm,
-    metric_hbm,
+    nodal_ref,
+    metric_ref,
     mortar_ref,
     incoming_ref,
     slot_mortar_ref,
@@ -413,18 +427,9 @@
     remote_ref,
     low_ids_ref,
     high_ids_ref,
-    nodal_ref,
-    metric_ref,
     stiff_ref,
     by_row,
-    nodal_sems,
-    sem,
 ):
-    nodal_copies = lane_copies(nodal_hbm, nodal_ref, nodal_sems)
-    metric_copy = pltpu.make_async_copy(metric_hbm, metric_ref, sem)
-    for copy in nodal_copies:
-        copy.start()
-    metric_copy.start()
     slot_hot = one_hot_lanes(columns_of(slot_mortar_ref[...]), 0, M_DEV)
     added = mm(stack2(incoming_ref[...]), slot_hot)
     mortar = mortar_ref[...] + added[0:SQ] + added[SQ:]
@@ -436,9 +441,6 @@
     high_id, low_id = window_ids(vertex_ref[...], lax.axis_index("elem"), total_vertices)
     high_ids_ref[...] = high_id
     low_ids_ref[...] = low_one_hot(low_id)
-    for copy in nodal_copies:
-        copy.wait()
-    metric_copy.wait()
     first_direction(nodal_ref, metric_ref.at[0], grad_map_ref[0:SQ, :], div_map_ref[:, 0:3 * SQ], stiff_ref, by_row)
     other_directions(
         nodal_ref, metric_ref.at[1:3], grad_map_ref[...], div_map_ref[...], stiff_ref, result_ref
@@ -620,10 +622,10 @@
     near, far = curve_swap(near, far)
     messages = group_swap(keep, cross)
 
-    mortar, local_answers, equal, back_maps, grad_map, div_map = pl.pallas_call(
+    mortar, local_answers, equal, back_maps, grad_map, div_map, nodal_in, metric_in = pl.pallas_call(
         local_kernel,
-        in_specs=[VMEM] * 7,
-        out_specs=[VMEM] * 6,
+        in_specs=[HBM, HBM] + [VMEM] * 7,
+        out_specs=[VMEM] * 8,
         out_shape=[
             pltpu.VMEM((SQ, M_DEV), f32),
             pltpu.VMEM((SQ, slots), f32),
@@ -631,11 +633,14 @@
             maps_shape,
             pltpu.VMEM((2 * SQ, 3 * SQ), bf16),
             pltpu.VMEM((SQ, 6 * SQ), bf16),
+            pltpu.VMEM(blocked, f32),
+            pltpu.VMEM(metric.shape, bf16),
         ],
+        scratch_shapes=[pltpu.SemaphoreType.DMA((blocked[0],)), pltpu.SemaphoreType.DMA],
         compiler_params=params(16),
         cost_estimate=cost(3),
         name="local",
-    )(traces, maps, level, columns, slot_row, interp_in, derivative_in)
+    )(nodal, metric, traces, maps, level, columns, slot_row, interp_in, derivative_in)
 
     near, far, keep, cross, incoming, sums = pl.pallas_call(
         functools.partial(answer_kernel, paired),
@@ -659,7 +664,7 @@
 
     result, remote, low_ids, high_ids = pl.pallas_call(
         functools.partial(gather_kernel, total_vertices),
-        in_specs=[HBM, HBM] + [VMEM] * 9,
+        in_specs=[VMEM] * 11,
         out_specs=[VMEM] * 4,
         out_shape=[
             pltpu.VMEM(blocked, f32),
@@ -668,18 +673,14 @@
             pltpu.VMEM((8, elems), jnp.int32),
         ],
         scratch_shapes=[
-            pltpu.VMEM(blocked, f32),
-            pltpu.VMEM(metric.shape, bf16),
             pltpu.VMEM(nodal.shape, f32),
             pltpu.VMEM(nodal.shape, f32),
-            pltpu.SemaphoreType.DMA((blocked[0],)),
-            pltpu.SemaphoreType.DMA,
         ],
         compiler_params=params(16),
         cost_estimate=cost(3),
         name="gather",
     )(
-        nodal, metric, mortar, incoming, slot_row, target, level, back_maps,
+        nodal_in, metric_in, mortar, incoming, slot_row, target, level, back_maps,
         grad_map, div_map, vertex_in,
     )
 

time: 22.8 us -> 22.5 us (0.987)
  Pallas kernels: 7.52 us -> 7.25 us
    pallas_call x1, Pallas kernels: 2.24 us -> 1.9 us  [on_device(): pl.pallas_call(functools.partial(gather_kernel, total_vertices), in_specs...]
  transfers between devices with their start and end apart: 12 -> 12, of which waited for: 2 -> 3; matrix products, arithmetic and copies ran while one was open for 0% -> 0% of each run, Pallas kernels for 16% -> 15%
where the time goes in v6:
time: 22.5 us; the launch traced here: 22.3 us
  starting transfers between devices  13 us (58%)
  Pallas kernels  7.25 us (32%)
  waiting for transfers between devices  1.92 us (9%)
    ppermute x6, starting transfers between devices, group_swap(): lax.ppermute(messages[mask], 'clus', [(i, i ^ 2 * mask + 1) for i in rang...  5.69 us
    ppermute x2, starting transfers between devices, curve_swap(): lax.ppermute(near, 'elem', near_pairs)  3.38 us
    ppermute x2, starting transfers between devices, curve_swap(): lax.ppermute(far, 'elem', far_pairs)  3.29 us
    pallas_call x1, Pallas kernels, on_device(): pl.pallas_call(functools.partial(send_kernel, total_vertices, paired), in...  2.09 us
    pallas_call x1, Pallas kernels, on_device(): pl.pallas_call(functools.partial(gather_kernel, total_vertices), in_specs...  1.9 us
    ppermute x6, waiting for transfers between devices, group_swap(): lax.ppermute(messages[mask], 'clus', [(i, i ^ 2 * mask + 1) for i in rang...  1.7 us
    pallas_call x1, Pallas kernels, on_device(): pl.pallas_call(functools.partial(final_kernel, paired), in_specs=[VMEM] *...  1.48 us
    pallas_call x1, Pallas kernels, on_device(): pl.pallas_call(local_kernel, in_specs=[HBM, HBM] + [VMEM] * 7, out_specs=...  1.39 us
  transfers between devices with their start and end apart: 12, of which 3 were waited for; matrix products, arithmetic and copies ran while one was open for 0% of the time, Pallas kernels for 15%

profile of v6, /device:TPU:0, one launch (start us, length us, event | category | flops | bytes accessed | tf_op | source)
XLA Modules:
  0.0 22.3 jit_solution(7140219076395707944)
XLA Ops:
  0.0 2.1 %send.1 = (f32[64,128]{1,0:T(8,128)S(1)}, f32[64,128]{1,0:T(8,128)S(1)}, f32[64,128]{1,0:T(8,128)S(1)}, f32[64,128]{1,0:T(8,128)S(1)}, bf16[144,1536]{1,0:T(8,12...) custom-call(f32[512,256]{1,0:T(8,128)} %nodal_hbm.3, ...), custom_call_target="tpu_custom_call" | custom-call | tf_op jit(solution)/shard_map/send/pallas_call | solution.py:592
  2.1 0.5 %collective-permute-start.2 = (f32[64,128]{1,0:T(8,128)S(1)}, f32[64,128]{1,0:T(8,128)S(1)}, u32[]{:S(2)}, u32[]{:S(2)}) collective-permute-start(f32[64,128]{1,0:T(8,128)S(1)} %get-tuple-element.57), channel_id=1, source_target_pairs={{0,1},{1,0},{2,3},{3,2},{4,5},{5,4},{6,7},{7,6},{8,9},{9,8},{10,11... | collective-permute-start | bytes 98312 | tf_op jit(solution)/shard_map/ppermute | solution.py:557
  2.6 2.7 %collective-permute-start = (f32[64,128]{1,0:T(8,128)S(1)}, f32[64,128]{1,0:T(8,128)S(1)}, u32[]{:S(2)}, u32[]{:S(2)}) collective-permute-start(f32[64,128]{1,0:T(8,128)S(1)} %get-tuple-element.45), channel_id=1, source_target_pairs={{0,8},{8,0},{16,24},{24,16},{1,9},{9,1},{17,25},{25,17},{2,10},{10... | collective-permute-start | bytes 98312 | tf_op jit(solution)/shard_map/ppermute | solution.py:551
  5.3 2.5 %collective-permute-start.1 = (f32[64,128]{1,0:T(8,128)S(1)}, f32[64,128]{1,0:T(8,128)S(1)}, u32[]{:S(2)}, u32[]{:S(2)}) collective-permute-start(f32[64,128]{1,0:T(8,128)S(1)} %get-tuple-element.46), channel_id=1, source_target_pairs={{0,24},{8,16},{16,8},{24,0},{1,25},{9,17},{17,9},{25,1},{2,26},{10... | collective-permute-start | bytes 98312 | tf_op jit(solution)/shard_map/ppermute | solution.py:551
  7.8 0.0 collective-permute-done.2.cross_ref
  7.8 2.0 %collective-permute-start.3 = (f32[32,128]{1,0:T(8,128)S(1)}, f32[32,128]{1,0:T(8,128)S(1)}, u32[]{:S(2)}, u32[]{:S(2)}) collective-permute-start(f32[32,128]{1,0:T(8,128)S(1)} %get-tuple-element.59), channel_id=1, source_target_pairs={{0,7},{1,6},{2,5},{3,4},{4,3},{5,2},{6,1},{7,0},{8,15},{9,14},{10,... | collective-permute-start | bytes 49160 | tf_op jit(solution)/shard_map/ppermute | solution.py:567
  9.8 0.7 %collective-permute-start.4 = (f32[32,128]{1,0:T(8,128)S(1)}, f32[32,128]{1,0:T(8,128)S(1)}, u32[]{:S(2)}, u32[]{:S(2)}) collective-permute-start(f32[32,128]{1,0:T(8,128)S(1)} %get-tuple-element.60), channel_id=1, source_target_pairs={{0,5},{1,4},{2,7},{3,6},{4,1},{5,0},{6,3},{7,2},{8,13},{9,12},{10,... | collective-permute-start | bytes 49160 | tf_op jit(solution)/shard_map/ppermute | solution.py:567
  10.5 0.1 collective-permute-start.5
  10.6 1.4 %local.1 = (f32[64,512]{1,0:T(8,128)S(1)}, f32[64,384]{1,0:T(8,128)S(1)}, bf16[384,384]{1,0:T(8,128)(2,1)S(1)}, bf16[256,192]{1,0:T(8,128)(2,1)S(1)}, bf16[128,1...) custom-call(f32[512,256]{1,0:T(8,128)} %nodal_hbm.3, ...), custom_call_target="tpu_custom_call" | custom-call | flops 1500000000 | bytes 6000000 | tf_op jit(solution)/shard_map/local/pallas_call | solution.py:625
  12.0 0.0 collective-permute-done.near_in_ref
  12.1 0.9 %collective-permute-done.4.refs_2_ = f32[32,128]{1,0:T(8,128)S(1)} collective-permute-done((f32[32,128]{1,0:T(8,128)S(1)}, f32[32,128]{1,0:T(8,128)S(1)}, u32[]{:S(2)}, u32[]{:S(2)}) %collective-permute-start.4) | collective-permute-done | bytes 16416 | tf_op jit(solution)/shard_map/ppermute | solution.py:567
  12.9 0.8 %collective-permute-done.5.refs_3_ = f32[32,128]{1,0:T(8,128)S(1)} collective-permute-done((f32[32,128]{1,0:T(8,128)S(1)}, f32[32,128]{1,0:T(8,128)S(1)}, u32[]{:S(2)}, u32[]{:S(2)}) %collective-permute-start.5) | collective-permute-done | bytes 16416 | tf_op jit(solution)/shard_map/ppermute | solution.py:567
  13.8 0.4 %answer.1 = (f32[72,128]{1,0:T(8,128)S(1)}, f32[72,128]{1,0:T(8,128)S(1)}, f32[64,128]{1,0:T(8,128)S(1)}, f32[64,128]{1,0:T(8,128)S(1)}, f32[64,384]{1,0:T(8,128)S(1)}, /*index=5*/f32[16,128]{1,0:T(8,128)S(1)}) custom-call(f32[64,128]{1,0:T(8,128)S(1)} %collective-permute-done.near_in_ref, f32[64,128]{1,0:T(8,128)S(1)} %collective-permute-done.1.far_in_ref, ...), custom_call_target="tpu_custom_call" | custom-call | tf_op jit(solution)/shard_map/answer/pallas_call | solution.py:645
  14.2 0.2 collective-permute-start.8
  14.3 0.7 %collective-permute-start.6 = (f32[72,128]{1,0:T(8,128)S(1)}, f32[72,128]{1,0:T(8,128)S(1)}, u32[]{:S(2)}, u32[]{:S(2)}) collective-permute-start(f32[72,128]{1,0:T(8,128)S(1)} %get-tuple-element.62), channel_id=1, source_target_pairs={{0,8},{8,0},{16,24},{24,16},{1,9},{9,1},{17,25},{25,17},{2,10},{10... | collective-permute-start | bytes 110600 | tf_op jit(solution)/shard_map/ppermute | solution.py:551
  15.1 0.8 %collective-permute-start.7 = (f32[72,128]{1,0:T(8,128)S(1)}, f32[72,128]{1,0:T(8,128)S(1)}, u32[]{:S(2)}, u32[]{:S(2)}) collective-permute-start(f32[72,128]{1,0:T(8,128)S(1)} %get-tuple-element.63), channel_id=1, source_target_pairs={{0,24},{8,16},{16,8},{24,0},{1,25},{9,17},{17,9},{25,1},{2,26},{10... | collective-permute-start | bytes 110600 | tf_op jit(solution)/shard_map/ppermute | solution.py:551
  15.9 0.0 collective-permute-done.8.cross_ref
  15.9 1.1 %collective-permute-start.9 = (f32[32,128]{1,0:T(8,128)S(1)}, f32[32,128]{1,0:T(8,128)S(1)}, u32[]{:S(2)}, u32[]{:S(2)}) collective-permute-start(f32[32,128]{1,0:T(8,128)S(1)} %get-tuple-element.82), channel_id=1, source_target_pairs={{0,7},{1,6},{2,5},{3,4},{4,3},{5,2},{6,1},{7,0},{8,15},{9,14},{10,... | collective-permute-start | bytes 49160 | tf_op jit(solution)/shard_map/ppermute | solution.py:567
  17.0 0.7 %collective-permute-start.10 = (f32[32,128]{1,0:T(8,128)S(1)}, f32[32,128]{1,0:T(8,128)S(1)}, u32[]{:S(2)}, u32[]{:S(2)}) collective-permute-start(f32[32,128]{1,0:T(8,128)S(1)} %get-tuple-element.83), channel_id=1, source_target_pairs={{0,5},{1,4},{2,7},{3,6},{4,1},{5,0},{6,3},{7,2},{8,13},{9,12},{10,... | collective-permute-start | bytes 49160 | tf_op jit(solution)/shard_map/ppermute | solution.py:567
  17.7 1.0 %collective-permute-start.11 = (f32[32,128]{1,0:T(8,128)S(1)}, f32[32,128]{1,0:T(8,128)S(1)}, u32[]{:S(2)}, u32[]{:S(2)}) collective-permute-start(f32[32,128]{1,0:T(8,128)S(1)} %get-tuple-element.84), channel_id=1, source_target_pairs={{0,3},{1,2},{2,1},{3,0},{4,7},{5,6},{6,5},{7,4},{8,11},{9,10},{10,... | collective-permute-start | bytes 49160 | tf_op jit(solution)/shard_map/ppermute | solution.py:567
  18.7 1.9 %gather.1 = (f32[2,512,128]{2,1,0:T(8,128)S(1)}, bf16[384,1536]{1,0:T(8,128)(2,1)S(1)}, bf16[128,2048]{1,0:T(8,128)(2,1)S(1)}, s32[8,256]{1,0:T(8,128)S(1)}) custom-call(f32[2,512,128]{2,1,0:T(8,128)S(1)} %get-tuple-element.66.nodal_ref, bf16[3,512,256]{2,1,0:T(8,128)(2,1)S(1)} %get-tuple-element.67.metric_ref, f32[64,512]{1,0:T(8,128)S(1)} %get-tuple-element.68.mortar_ref, ...), custom_call_target="tpu_custom_call" | custom-call | flops 1500000000 | bytes 6000000 | tf_op jit(solution)/shard_map/gather/pallas_call | solution.py:665
  20.6 0.0 collective-permute-done.6.near_in_ref
  20.6 0.2 collective-permute-done.7.far_in_ref
  20.8 1.5 %final.1 = f32[512,256]{1,0:T(8,128)} custom-call(f32[72,128]{1,0:T(8,128)S(1)} %collective-permute-done.6.near_in_ref, f32[72,128]{1,0:T(8,128)S(1)} %collective-permute-done.7.far_in_ref, f32[8,384]{1,0:T(8,128)S(1)} %get-tuple-element.64.slot_level_ref, bf16[256,192]{1,0:T(8,128)(2,1)S(1)} %get-tuple-element.65.back_maps_ref.maps_ref, ...), custom_call_target="tpu_custom_call" | custom-call | tf_op jit(solution)/shard_map/final/pallas_call | solution.py:687
  (7 shorter events, 0.0 us)
Async XLA Ops:
  2.1 5.6 %collective-permute-start.2 = (f32[64,128]{1,0:T(8,128)S(1)}, f32[64,128]{1,0:T(8,128)S(1)}, u32[]{:S(2)}, u32[]{:S(2)}) collective-permute-start(f32[64,128]{1,0:T(8,128)S(1)} %get-tuple-element.57), channel_id=1, source_target_pairs={{0,1},{1,0},{2,3},{3,2},{4,5},{5,4},{6,7},{7,6},{8,9},{9,8},{10,11... | collective-permute-start | bytes 98312 | tf_op jit(solution)/shard_map/ppermute | solution.py:557
  2.6 9.4 %collective-permute-start = (f32[64,128]{1,0:T(8,128)S(1)}, f32[64,128]{1,0:T(8,128)S(1)}, u32[]{:S(2)}, u32[]{:S(2)}) collective-permute-start(f32[64,128]{1,0:T(8,128)S(1)} %get-tuple-element.45), channel_id=1, source_target_pairs={{0,8},{8,0},{16,24},{24,16},{1,9},{9,1},{17,25},{25,17},{2,10},{10... | collective-permute-start | bytes 98312 | tf_op jit(solution)/shard_map/ppermute | solution.py:551
  5.3 6.8 %collective-permute-start.1 = (f32[64,128]{1,0:T(8,128)S(1)}, f32[64,128]{1,0:T(8,128)S(1)}, u32[]{:S(2)}, u32[]{:S(2)}) collective-permute-start(f32[64,128]{1,0:T(8,128)S(1)} %get-tuple-element.46), channel_id=1, source_target_pairs={{0,24},{8,16},{16,8},{24,0},{1,25},{9,17},{17,9},{25,1},{2,26},{10... | collective-permute-start | bytes 98312 | tf_op jit(solution)/shard_map/ppermute | solution.py:551
  7.8 4.3 %collective-permute-start.3 = (f32[32,128]{1,0:T(8,128)S(1)}, f32[32,128]{1,0:T(8,128)S(1)}, u32[]{:S(2)}, u32[]{:S(2)}) collective-permute-start(f32[32,128]{1,0:T(8,128)S(1)} %get-tuple-element.59), channel_id=1, source_target_pairs={{0,7},{1,6},{2,5},{3,4},{4,3},{5,2},{6,1},{7,0},{8,15},{9,14},{10,... | collective-permute-start | bytes 49160 | tf_op jit(solution)/shard_map/ppermute | solution.py:567
  9.8 3.2 %collective-permute-start.4 = (f32[32,128]{1,0:T(8,128)S(1)}, f32[32,128]{1,0:T(8,128)S(1)}, u32[]{:S(2)}, u32[]{:S(2)}) collective-permute-start(f32[32,128]{1,0:T(8,128)S(1)} %get-tuple-element.60), channel_id=1, source_target_pairs={{0,5},{1,4},{2,7},{3,6},{4,1},{5,0},{6,3},{7,2},{8,13},{9,12},{10,... | collective-permute-start | bytes 49160 | tf_op jit(solution)/shard_map/ppermute | solution.py:567
  10.5 3.3 %collective-permute-start.5 = (f32[32,128]{1,0:T(8,128)S(1)}, f32[32,128]{1,0:T(8,128)S(1)}, u32[]{:S(2)}, u32[]{:S(2)}) collective-permute-start(f32[32,128]{1,0:T(8,128)S(1)} %get-tuple-element.61), channel_id=1, source_target_pairs={{0,3},{1,2},{2,1},{3,0},{4,7},{5,6},{6,5},{7,4},{8,11},{9,10},{10,... | collective-permute-start | bytes 49160 | tf_op jit(solution)/shard_map/ppermute | solution.py:567
  14.2 1.7 %collective-permute-start.8 = (f32[64,128]{1,0:T(8,128)S(1)}, f32[64,128]{1,0:T(8,128)S(1)}, u32[]{:S(2)}, u32[]{:S(2)}) collective-permute-start(f32[64,128]{1,0:T(8,128)S(1)} %get-tuple-element.80), channel_id=1, source_target_pairs={{0,1},{1,0},{2,3},{3,2},{4,5},{5,4},{6,7},{7,6},{8,9},{9,8},{10,11... | collective-permute-start | bytes 98312 | tf_op jit(solution)/shard_map/ppermute | solution.py:557
  14.3 6.3 %collective-permute-start.6 = (f32[72,128]{1,0:T(8,128)S(1)}, f32[72,128]{1,0:T(8,128)S(1)}, u32[]{:S(2)}, u32[]{:S(2)}) collective-permute-start(f32[72,128]{1,0:T(8,128)S(1)} %get-tuple-element.62), channel_id=1, source_target_pairs={{0,8},{8,0},{16,24},{24,16},{1,9},{9,1},{17,25},{25,17},{2,10},{10... | collective-permute-start | bytes 110600 | tf_op jit(solution)/shard_map/ppermute | solution.py:551
  15.1 5.8 %collective-permute-start.7 = (f32[72,128]{1,0:T(8,128)S(1)}, f32[72,128]{1,0:T(8,128)S(1)}, u32[]{:S(2)}, u32[]{:S(2)}) collective-permute-start(f32[72,128]{1,0:T(8,128)S(1)} %get-tuple-element.63), channel_id=1, source_target_pairs={{0,24},{8,16},{16,8},{24,0},{1,25},{9,17},{17,9},{25,1},{2,26},{10... | collective-permute-start | bytes 110600 | tf_op jit(solution)/shard_map/ppermute | solution.py:551
  15.9 4.9 %collective-permute-start.9 = (f32[32,128]{1,0:T(8,128)S(1)}, f32[32,128]{1,0:T(8,128)S(1)}, u32[]{:S(2)}, u32[]{:S(2)}) collective-permute-start(f32[32,128]{1,0:T(8,128)S(1)} %get-tuple-element.82), channel_id=1, source_target_pairs={{0,7},{1,6},{2,5},{3,4},{4,3},{5,2},{6,1},{7,0},{8,15},{9,14},{10,... | collective-permute-start | bytes 49160 | tf_op jit(solution)/shard_map/ppermute | solution.py:567
  17.0 3.8 %collective-permute-start.10 = (f32[32,128]{1,0:T(8,128)S(1)}, f32[32,128]{1,0:T(8,128)S(1)}, u32[]{:S(2)}, u32[]{:S(2)}) collective-permute-start(f32[32,128]{1,0:T(8,128)S(1)} %get-tuple-element.83), channel_id=1, source_target_pairs={{0,5},{1,4},{2,7},{3,6},{4,1},{5,0},{6,3},{7,2},{8,13},{9,12},{10,... | collective-permute-start | bytes 49160 | tf_op jit(solution)/shard_map/ppermute | solution.py:567
  17.7 3.2 %collective-permute-start.11 = (f32[32,128]{1,0:T(8,128)S(1)}, f32[32,128]{1,0:T(8,128)S(1)}, u32[]{:S(2)}, u32[]{:S(2)}) collective-permute-start(f32[32,128]{1,0:T(8,128)S(1)} %get-tuple-element.84), channel_id=1, source_target_pairs={{0,3},{1,2},{2,1},{3,0},{4,7},{5,6},{6,5},{7,4},{8,11},{9,10},{10,... | collective-permute-start | bytes 49160 | tf_op jit(solution)/shard_map/ppermute | solution.py:567

commit v7 on v6

--- a/solution.py
+++ b/solution.py
@@ -236,13 +236,13 @@
         copy.start()
     slots = slot_level_ref.shape[1]
     elems = nodal_hbm.shape[1]
+    interp_copy.wait()
+    maps = kron_four(interp_ref[0], interp_ref[1])
+    maps_ref[...] = maps
     target_copy.wait()
     columns = columns_of(target_ref[...])
     columns_ref[...] = columns
-    remote = one_hot_lanes(columns, M_DEV, -(-slots // 256) * 256)
-    interp_copy.wait()
-    maps = kron_four(interp_ref[0], interp_ref[1])
-    maps_ref[...] = maps
+    remote = one_hot_lanes(columns, M_DEV, slots)
     vertex_copy.wait()
     high_id, low_id = window_ids(vertex_ref[...], lax.axis_index("elem"), total_vertices)
     low_hot = low_one_hot(low_id)
@@ -261,11 +261,11 @@
     ]
     trace = jnp.concatenate(faces, axis=1)
     hi, lo = split(trace)
-    traces_ref[0:SQ, :] = hi
-    traces_ref[SQ : 2 * SQ, :] = lo
-    traces_ref[2 * SQ :, :] = jnp.broadcast_to(level, (16, level.shape[1])).astype(f32).astype(bf16)
-
-    picked = mm(traces_ref[...], remote)[:, 0:slots]
+    level_rows = jnp.broadcast_to(level, (16, level.shape[1])).astype(f32).astype(bf16)
+
+    traces = jnp.concatenate([hi, lo, level_rows], axis=0)
+    traces_ref[...] = traces
+    picked = mm(traces, remote)[:, 0:slots]
     plain = picked[0:SQ] + picked[SQ : 2 * SQ]
     slot_level = picked[2 * SQ : 2 * SQ + 8]
     slot_level_ref[...] = slot_level
@@ -430,6 +430,10 @@
     stiff_ref,
     by_row,
 ):
+    first_direction(nodal_ref, metric_ref.at[0], grad_map_ref[0:SQ, :], div_map_ref[:, 0:3 * SQ], stiff_ref, by_row)
+    other_directions(
+        nodal_ref, metric_ref.at[1:3], grad_map_ref[...], div_map_ref[...], stiff_ref, result_ref
+    )
     slot_hot = one_hot_lanes(columns_of(slot_mortar_ref[...]), 0, M_DEV)
     added = mm(stack2(incoming_ref[...]), slot_hot)
     mortar = mortar_ref[...] + added[0:SQ] + added[SQ:]
@@ -441,10 +445,6 @@
     high_id, low_id = window_ids(vertex_ref[...], lax.axis_index("elem"), total_vertices)
     high_ids_ref[...] = high_id
     low_ids_ref[...] = low_one_hot(low_id)
-    first_direction(nodal_ref, metric_ref.at[0], grad_map_ref[0:SQ, :], div_map_ref[:, 0:3 * SQ], stiff_ref, by_row)
-    other_directions(
-        nodal_ref, metric_ref.at[1:3], grad_map_ref[...], div_map_ref[...], stiff_ref, result_ref
-    )
     add_faces(result_ref, back)
 
 

time: 22.5 us -> 22.5 us (level)
  transfers between devices with their start and end apart: 12 -> 12, of which waited for: 3 -> 3; matrix products, arithmetic and copies ran while one was open for 0% -> 0% of each run, Pallas kernels for 15% -> 14%
where the time goes in v7:
time: 22.5 us; the launch traced here: 22.4 us
  starting transfers between devices  13 us (58%)
  Pallas kernels  7.21 us (32%)
  waiting for transfers between devices  2.03 us (9%)
    ppermute x6, starting transfers between devices, group_swap(): lax.ppermute(messages[mask], 'clus', [(i, i ^ 2 * mask + 1) for i in rang...  5.68 us
    ppermute x2, starting transfers between devices, curve_swap(): lax.ppermute(near, 'elem', near_pairs)  3.35 us
    ppermute x2, starting transfers between devices, curve_swap(): lax.ppermute(far, 'elem', far_pairs)  3.3 us
    pallas_call x1, Pallas kernels, on_device(): pl.pallas_call(functools.partial(send_kernel, total_vertices, paired), in...  2.14 us
    pallas_call x1, Pallas kernels, on_device(): pl.pallas_call(functools.partial(gather_kernel, total_vertices), in_specs...  1.8 us
    ppermute x6, waiting for transfers between devices, group_swap(): lax.ppermute(messages[mask], 'clus', [(i, i ^ 2 * mask + 1) for i in rang...  1.74 us
    pallas_call x1, Pallas kernels, on_device(): pl.pallas_call(functools.partial(final_kernel, paired), in_specs=[VMEM] *...  1.47 us
    pallas_call x1, Pallas kernels, on_device(): pl.pallas_call(local_kernel, in_specs=[HBM, HBM] + [VMEM] * 7, out_specs=...  1.4 us
  transfers between devices with their start and end apart: 12, of which 3 were waited for; matrix products, arithmetic and copies ran while one was open for 0% of the time, Pallas kernels for 14%

profile of v7, /device:TPU:0, one launch (start us, length us, event | category | flops | bytes accessed | tf_op | source)
XLA Modules:
  0.0 22.4 jit_solution(10683713770256840804)
XLA Ops:
  0.0 2.1 %send.1 = (f32[64,128]{1,0:T(8,128)S(1)}, f32[64,128]{1,0:T(8,128)S(1)}, f32[64,128]{1,0:T(8,128)S(1)}, f32[64,128]{1,0:T(8,128)S(1)}, bf16[144,1536]{1,0:T(8,12...) custom-call(f32[512,256]{1,0:T(8,128)} %nodal_hbm.3, ...), custom_call_target="tpu_custom_call" | custom-call | tf_op jit(solution)/shard_map/send/pallas_call | solution.py:592
  2.2 0.5 %collective-permute-start.2 = (f32[64,128]{1,0:T(8,128)S(1)}, f32[64,128]{1,0:T(8,128)S(1)}, u32[]{:S(2)}, u32[]{:S(2)}) collective-permute-start(f32[64,128]{1,0:T(8,128)S(1)} %get-tuple-element.57), channel_id=1, source_target_pairs={{0,1},{1,0},{2,3},{3,2},{4,5},{5,4},{6,7},{7,6},{8,9},{9,8},{10,11... | collective-permute-start | bytes 98312 | tf_op jit(solution)/shard_map/ppermute | solution.py:557
  2.7 2.6 %collective-permute-start = (f32[64,128]{1,0:T(8,128)S(1)}, f32[64,128]{1,0:T(8,128)S(1)}, u32[]{:S(2)}, u32[]{:S(2)}) collective-permute-start(f32[64,128]{1,0:T(8,128)S(1)} %get-tuple-element.45), channel_id=1, source_target_pairs={{0,8},{8,0},{16,24},{24,16},{1,9},{9,1},{17,25},{25,17},{2,10},{10... | collective-permute-start | bytes 98312 | tf_op jit(solution)/shard_map/ppermute | solution.py:551
  5.3 2.5 %collective-permute-start.1 = (f32[64,128]{1,0:T(8,128)S(1)}, f32[64,128]{1,0:T(8,128)S(1)}, u32[]{:S(2)}, u32[]{:S(2)}) collective-permute-start(f32[64,128]{1,0:T(8,128)S(1)} %get-tuple-element.46), channel_id=1, source_target_pairs={{0,24},{8,16},{16,8},{24,0},{1,25},{9,17},{17,9},{25,1},{2,26},{10... | collective-permute-start | bytes 98312 | tf_op jit(solution)/shard_map/ppermute | solution.py:551
  7.8 0.0 collective-permute-done.2.cross_ref
  7.8 2.0 %collective-permute-start.3 = (f32[32,128]{1,0:T(8,128)S(1)}, f32[32,128]{1,0:T(8,128)S(1)}, u32[]{:S(2)}, u32[]{:S(2)}) collective-permute-start(f32[32,128]{1,0:T(8,128)S(1)} %get-tuple-element.59), channel_id=1, source_target_pairs={{0,7},{1,6},{2,5},{3,4},{4,3},{5,2},{6,1},{7,0},{8,15},{9,14},{10,... | collective-permute-start | bytes 49160 | tf_op jit(solution)/shard_map/ppermute | solution.py:567
  9.8 0.7 %collective-permute-start.4 = (f32[32,128]{1,0:T(8,128)S(1)}, f32[32,128]{1,0:T(8,128)S(1)}, u32[]{:S(2)}, u32[]{:S(2)}) collective-permute-start(f32[32,128]{1,0:T(8,128)S(1)} %get-tuple-element.60), channel_id=1, source_target_pairs={{0,5},{1,4},{2,7},{3,6},{4,1},{5,0},{6,3},{7,2},{8,13},{9,12},{10,... | collective-permute-start | bytes 49160 | tf_op jit(solution)/shard_map/ppermute | solution.py:567
  10.5 0.1 collective-permute-start.5
  10.7 1.4 %local.1 = (f32[64,512]{1,0:T(8,128)S(1)}, f32[64,384]{1,0:T(8,128)S(1)}, bf16[384,384]{1,0:T(8,128)(2,1)S(1)}, bf16[256,192]{1,0:T(8,128)(2,1)S(1)}, bf16[128,1...) custom-call(f32[512,256]{1,0:T(8,128)} %nodal_hbm.3, ...), custom_call_target="tpu_custom_call" | custom-call | flops 1500000000 | bytes 6000000 | tf_op jit(solution)/shard_map/local/pallas_call | solution.py:625
  12.1 0.0 collective-permute-done.near_in_ref
  12.1 0.0 collective-permute-done.1.far_in_ref
  12.1 0.9 %collective-permute-done.4.refs_2_ = f32[32,128]{1,0:T(8,128)S(1)} collective-permute-done((f32[32,128]{1,0:T(8,128)S(1)}, f32[32,128]{1,0:T(8,128)S(1)}, u32[]{:S(2)}, u32[]{:S(2)}) %collective-permute-start.4) | collective-permute-done | bytes 16416 | tf_op jit(solution)/shard_map/ppermute | solution.py:567
  13.0 0.8 %collective-permute-done.5.refs_3_ = f32[32,128]{1,0:T(8,128)S(1)} collective-permute-done((f32[32,128]{1,0:T(8,128)S(1)}, f32[32,128]{1,0:T(8,128)S(1)}, u32[]{:S(2)}, u32[]{:S(2)}) %collective-permute-start.5) | collective-permute-done | bytes 16416 | tf_op jit(solution)/shard_map/ppermute | solution.py:567
  13.8 0.4 %answer.1 = (f32[72,128]{1,0:T(8,128)S(1)}, f32[72,128]{1,0:T(8,128)S(1)}, f32[64,128]{1,0:T(8,128)S(1)}, f32[64,128]{1,0:T(8,128)S(1)}, f32[64,384]{1,0:T(8,128)S(1)}, /*index=5*/f32[16,128]{1,0:T(8,128)S(1)}) custom-call(f32[64,128]{1,0:T(8,128)S(1)} %collective-permute-done.near_in_ref, f32[64,128]{1,0:T(8,128)S(1)} %collective-permute-done.1.far_in_ref, ...), custom_call_target="tpu_custom_call" | custom-call | tf_op jit(solution)/shard_map/answer/pallas_call | solution.py:645
  14.2 0.2 collective-permute-start.8
  14.4 0.7 %collective-permute-start.6 = (f32[72,128]{1,0:T(8,128)S(1)}, f32[72,128]{1,0:T(8,128)S(1)}, u32[]{:S(2)}, u32[]{:S(2)}) collective-permute-start(f32[72,128]{1,0:T(8,128)S(1)} %get-tuple-element.62), channel_id=1, source_target_pairs={{0,8},{8,0},{16,24},{24,16},{1,9},{9,1},{17,25},{25,17},{2,10},{10... | collective-permute-start | bytes 110600 | tf_op jit(solution)/shard_map/ppermute | solution.py:551
  15.1 0.8 %collective-permute-start.7 = (f32[72,128]{1,0:T(8,128)S(1)}, f32[72,128]{1,0:T(8,128)S(1)}, u32[]{:S(2)}, u32[]{:S(2)}) collective-permute-start(f32[72,128]{1,0:T(8,128)S(1)} %get-tuple-element.63), channel_id=1, source_target_pairs={{0,24},{8,16},{16,8},{24,0},{1,25},{9,17},{17,9},{25,1},{2,26},{10... | collective-permute-start | bytes 110600 | tf_op jit(solution)/shard_map/ppermute | solution.py:551
  15.9 1.1 %collective-permute-start.9 = (f32[32,128]{1,0:T(8,128)S(1)}, f32[32,128]{1,0:T(8,128)S(1)}, u32[]{:S(2)}, u32[]{:S(2)}) collective-permute-start(f32[32,128]{1,0:T(8,128)S(1)} %get-tuple-element.82), channel_id=1, source_target_pairs={{0,7},{1,6},{2,5},{3,4},{4,3},{5,2},{6,1},{7,0},{8,15},{9,14},{10,... | collective-permute-start | bytes 49160 | tf_op jit(solution)/shard_map/ppermute | solution.py:567
  17.0 0.7 %collective-permute-start.10 = (f32[32,128]{1,0:T(8,128)S(1)}, f32[32,128]{1,0:T(8,128)S(1)}, u32[]{:S(2)}, u32[]{:S(2)}) collective-permute-start(f32[32,128]{1,0:T(8,128)S(1)} %get-tuple-element.83), channel_id=1, source_target_pairs={{0,5},{1,4},{2,7},{3,6},{4,1},{5,0},{6,3},{7,2},{8,13},{9,12},{10,... | collective-permute-start | bytes 49160 | tf_op jit(solution)/shard_map/ppermute | solution.py:567
  17.7 1.0 %collective-permute-start.11 = (f32[32,128]{1,0:T(8,128)S(1)}, f32[32,128]{1,0:T(8,128)S(1)}, u32[]{:S(2)}, u32[]{:S(2)}) collective-permute-start(f32[32,128]{1,0:T(8,128)S(1)} %get-tuple-element.84), channel_id=1, source_target_pairs={{0,3},{1,2},{2,1},{3,0},{4,7},{5,6},{6,5},{7,4},{8,11},{9,10},{10,... | collective-permute-start | bytes 49160 | tf_op jit(solution)/shard_map/ppermute | solution.py:567
  18.7 1.8 %gather.1 = (f32[2,512,128]{2,1,0:T(8,128)S(1)}, bf16[384,1536]{1,0:T(8,128)(2,1)S(1)}, bf16[128,2048]{1,0:T(8,128)(2,1)S(1)}, s32[8,256]{1,0:T(8,128)S(1)}) custom-call(f32[2,512,128]{2,1,0:T(8,128)S(1)} %get-tuple-element.66.nodal_ref, bf16[3,512,256]{2,1,0:T(8,128)(2,1)S(1)} %get-tuple-element.67.metric_ref, f32[64,512]{1,0:T(8,128)S(1)} %get-tuple-element.68.mortar_ref, ...), custom_call_target="tpu_custom_call" | custom-call | flops 1500000000 | bytes 6000000 | tf_op jit(solution)/shard_map/gather/pallas_call | solution.py:665
  20.6 0.3 %collective-permute-done.7.far_in_ref = f32[72,128]{1,0:T(8,128)S(1)} collective-permute-done((f32[72,128]{1,0:T(8,128)S(1)}, f32[72,128]{1,0:T(8,128)S(1)}, u32[]{:S(2)}, u32[]{:S(2)}) %collective-permute-start.7) | collective-permute-done | bytes 36896 | tf_op jit(solution)/shard_map/ppermute | solution.py:551
  20.9 0.0 collective-permute-done.11.refs_3_
  20.9 1.5 %final.1 = f32[512,256]{1,0:T(8,128)} custom-call(f32[72,128]{1,0:T(8,128)S(1)} %collective-permute-done.6.near_in_ref, f32[72,128]{1,0:T(8,128)S(1)} %collective-permute-done.7.far_in_ref, f32[8,384]{1,0:T(8,128)S(1)} %get-tuple-element.64.slot_level_ref, bf16[256,192]{1,0:T(8,128)(2,1)S(1)} %get-tuple-element.65.back_maps_ref.maps_ref, ...), custom_call_target="tpu_custom_call" | custom-call | tf_op jit(solution)/shard_map/final/pallas_call | solution.py:687
  (7 shorter events, 0.0 us)
Async XLA Ops:
  2.2 5.7 %collective-permute-start.2 = (f32[64,128]{1,0:T(8,128)S(1)}, f32[64,128]{1,0:T(8,128)S(1)}, u32[]{:S(2)}, u32[]{:S(2)}) collective-permute-start(f32[64,128]{1,0:T(8,128)S(1)} %get-tuple-element.57), channel_id=1, source_target_pairs={{0,1},{1,0},{2,3},{3,2},{4,5},{5,4},{6,7},{7,6},{8,9},{9,8},{10,11... | collective-permute-start | bytes 98312 | tf_op jit(solution)/shard_map/ppermute | solution.py:557
  2.7 9.4 %collective-permute-start = (f32[64,128]{1,0:T(8,128)S(1)}, f32[64,128]{1,0:T(8,128)S(1)}, u32[]{:S(2)}, u32[]{:S(2)}) collective-permute-start(f32[64,128]{1,0:T(8,128)S(1)} %get-tuple-element.45), channel_id=1, source_target_pairs={{0,8},{8,0},{16,24},{24,16},{1,9},{9,1},{17,25},{25,17},{2,10},{10... | collective-permute-start | bytes 98312 | tf_op jit(solution)/shard_map/ppermute | solution.py:551
  5.3 6.8 %collective-permute-start.1 = (f32[64,128]{1,0:T(8,128)S(1)}, f32[64,128]{1,0:T(8,128)S(1)}, u32[]{:S(2)}, u32[]{:S(2)}) collective-permute-start(f32[64,128]{1,0:T(8,128)S(1)} %get-tuple-element.46), channel_id=1, source_target_pairs={{0,24},{8,16},{16,8},{24,0},{1,25},{9,17},{17,9},{25,1},{2,26},{10... | collective-permute-start | bytes 98312 | tf_op jit(solution)/shard_map/ppermute | solution.py:551
  7.8 4.3 %collective-permute-start.3 = (f32[32,128]{1,0:T(8,128)S(1)}, f32[32,128]{1,0:T(8,128)S(1)}, u32[]{:S(2)}, u32[]{:S(2)}) collective-permute-start(f32[32,128]{1,0:T(8,128)S(1)} %get-tuple-element.59), channel_id=1, source_target_pairs={{0,7},{1,6},{2,5},{3,4},{4,3},{5,2},{6,1},{7,0},{8,15},{9,14},{10,... | collective-permute-start | bytes 49160 | tf_op jit(solution)/shard_map/ppermute | solution.py:567
  9.8 3.2 %collective-permute-start.4 = (f32[32,128]{1,0:T(8,128)S(1)}, f32[32,128]{1,0:T(8,128)S(1)}, u32[]{:S(2)}, u32[]{:S(2)}) collective-permute-start(f32[32,128]{1,0:T(8,128)S(1)} %get-tuple-element.60), channel_id=1, source_target_pairs={{0,5},{1,4},{2,7},{3,6},{4,1},{5,0},{6,3},{7,2},{8,13},{9,12},{10,... | collective-permute-start | bytes 49160 | tf_op jit(solution)/shard_map/ppermute | solution.py:567
  10.5 3.3 %collective-permute-start.5 = (f32[32,128]{1,0:T(8,128)S(1)}, f32[32,128]{1,0:T(8,128)S(1)}, u32[]{:S(2)}, u32[]{:S(2)}) collective-permute-start(f32[32,128]{1,0:T(8,128)S(1)} %get-tuple-element.61), channel_id=1, source_target_pairs={{0,3},{1,2},{2,1},{3,0},{4,7},{5,6},{6,5},{7,4},{8,11},{9,10},{10,... | collective-permute-start | bytes 49160 | tf_op jit(solution)/shard_map/ppermute | solution.py:567
  14.2 1.7 %collective-permute-start.8 = (f32[64,128]{1,0:T(8,128)S(1)}, f32[64,128]{1,0:T(8,128)S(1)}, u32[]{:S(2)}, u32[]{:S(2)}) collective-permute-start(f32[64,128]{1,0:T(8,128)S(1)} %get-tuple-element.80), channel_id=1, source_target_pairs={{0,1},{1,0},{2,3},{3,2},{4,5},{5,4},{6,7},{7,6},{8,9},{9,8},{10,11... | collective-permute-start | bytes 98312 | tf_op jit(solution)/shard_map/ppermute | solution.py:557
  14.4 6.2 %collective-permute-start.6 = (f32[72,128]{1,0:T(8,128)S(1)}, f32[72,128]{1,0:T(8,128)S(1)}, u32[]{:S(2)}, u32[]{:S(2)}) collective-permute-start(f32[72,128]{1,0:T(8,128)S(1)} %get-tuple-element.62), channel_id=1, source_target_pairs={{0,8},{8,0},{16,24},{24,16},{1,9},{9,1},{17,25},{25,17},{2,10},{10... | collective-permute-start | bytes 110600 | tf_op jit(solution)/shard_map/ppermute | solution.py:551
  15.1 5.8 %collective-permute-start.7 = (f32[72,128]{1,0:T(8,128)S(1)}, f32[72,128]{1,0:T(8,128)S(1)}, u32[]{:S(2)}, u32[]{:S(2)}) collective-permute-start(f32[72,128]{1,0:T(8,128)S(1)} %get-tuple-element.63), channel_id=1, source_target_pairs={{0,24},{8,16},{16,8},{24,0},{1,25},{9,17},{17,9},{25,1},{2,26},{10... | collective-permute-start | bytes 110600 | tf_op jit(solution)/shard_map/ppermute | solution.py:551
  15.9 4.9 %collective-permute-start.9 = (f32[32,128]{1,0:T(8,128)S(1)}, f32[32,128]{1,0:T(8,128)S(1)}, u32[]{:S(2)}, u32[]{:S(2)}) collective-permute-start(f32[32,128]{1,0:T(8,128)S(1)} %get-tuple-element.82), channel_id=1, source_target_pairs={{0,7},{1,6},{2,5},{3,4},{4,3},{5,2},{6,1},{7,0},{8,15},{9,14},{10,... | collective-permute-start | bytes 49160 | tf_op jit(solution)/shard_map/ppermute | solution.py:567
  17.0 3.8 %collective-permute-start.10 = (f32[32,128]{1,0:T(8,128)S(1)}, f32[32,128]{1,0:T(8,128)S(1)}, u32[]{:S(2)}, u32[]{:S(2)}) collective-permute-start(f32[32,128]{1,0:T(8,128)S(1)} %get-tuple-element.83), channel_id=1, source_target_pairs={{0,5},{1,4},{2,7},{3,6},{4,1},{5,0},{6,3},{7,2},{8,13},{9,12},{10,... | collective-permute-start | bytes 49160 | tf_op jit(solution)/shard_map/ppermute | solution.py:567
  17.7 3.2 %collective-permute-start.11 = (f32[32,128]{1,0:T(8,128)S(1)}, f32[32,128]{1,0:T(8,128)S(1)}, u32[]{:S(2)}, u32[]{:S(2)}) collective-permute-start(f32[32,128]{1,0:T(8,128)S(1)} %get-tuple-element.84), channel_id=1, source_target_pairs={{0,3},{1,2},{2,1},{3,0},{4,7},{5,6},{6,5},{7,4},{8,11},{9,10},{10,... | collective-permute-start | bytes 49160 | tf_op jit(solution)/shard_map/ppermute | solution.py:567

commit v8 on v7

--- a/solution.py
+++ b/solution.py
@@ -166,7 +166,7 @@
 
 
 def chip_masks(chips):
-    return [0] + list(range(chips - 1, 0, -1))
+    return [0, chips - 1] + list(range(1, chips - 1))
 
 
 def part_group(group_ref, keep_ref, cross_ref):

time: 22.5 us -> 22.5 us (level)
  no operation moved by 1% of the time
where the time goes in v8:
time: 22.5 us; the launch traced here: 22.4 us
  starting transfers between devices  13 us (58%)
  Pallas kernels  7.21 us (32%)
  waiting for transfers between devices  2.03 us (9%)
    ppermute x6, starting transfers between devices, group_swap(): lax.ppermute(messages[mask], 'clus', [(i, i ^ 2 * mask + 1) for i in rang...  5.69 us
    ppermute x2, starting transfers between devices, curve_swap(): lax.ppermute(near, 'elem', near_pairs)  3.33 us
    ppermute x2, starting transfers between devices, curve_swap(): lax.ppermute(far, 'elem', far_pairs)  3.32 us
    pallas_call x1, Pallas kernels, on_device(): pl.pallas_call(functools.partial(send_kernel, total_vertices, paired), in...  2.14 us
    pallas_call x1, Pallas kernels, on_device(): pl.pallas_call(functools.partial(gather_kernel, total_vertices), in_specs...  1.8 us
    ppermute x6, waiting for transfers between devices, group_swap(): lax.ppermute(messages[mask], 'clus', [(i, i ^ 2 * mask + 1) for i in rang...  1.76 us
    pallas_call x1, Pallas kernels, on_device(): pl.pallas_call(functools.partial(final_kernel, paired), in_specs=[VMEM] *...  1.47 us
    pallas_call x1, Pallas kernels, on_device(): pl.pallas_call(local_kernel, in_specs=[HBM, HBM] + [VMEM] * 7, out_specs=...  1.4 us
  transfers between devices with their start and end apart: 12, of which 3 were waited for; matrix products, arithmetic and copies ran while one was open for 0% of the time, Pallas kernels for 14%

profile of v8, /device:TPU:0, one launch (start us, length us, event | category | flops | bytes accessed | tf_op | source)
XLA Modules:
  0.0 22.4 jit_solution(978561597028230722)
XLA Ops:
  0.0 2.1 %send.1 = (f32[64,128]{1,0:T(8,128)S(1)}, f32[64,128]{1,0:T(8,128)S(1)}, f32[64,128]{1,0:T(8,128)S(1)}, f32[64,128]{1,0:T(8,128)S(1)}, bf16[144,1536]{1,0:T(8,12...) custom-call(f32[512,256]{1,0:T(8,128)} %nodal_hbm.3, ...), custom_call_target="tpu_custom_call" | custom-call | tf_op jit(solution)/shard_map/send/pallas_call | solution.py:592
  2.2 0.5 %collective-permute-start.2 = (f32[64,128]{1,0:T(8,128)S(1)}, f32[64,128]{1,0:T(8,128)S(1)}, u32[]{:S(2)}, u32[]{:S(2)}) collective-permute-start(f32[64,128]{1,0:T(8,128)S(1)} %get-tuple-element.57), channel_id=1, source_target_pairs={{0,1},{1,0},{2,3},{3,2},{4,5},{5,4},{6,7},{7,6},{8,9},{9,8},{10,11... | collective-permute-start | bytes 98312 | tf_op jit(solution)/shard_map/ppermute | solution.py:557
  2.7 2.6 %collective-permute-start = (f32[64,128]{1,0:T(8,128)S(1)}, f32[64,128]{1,0:T(8,128)S(1)}, u32[]{:S(2)}, u32[]{:S(2)}) collective-permute-start(f32[64,128]{1,0:T(8,128)S(1)} %get-tuple-element.45), channel_id=1, source_target_pairs={{0,8},{8,0},{16,24},{24,16},{1,9},{9,1},{17,25},{25,17},{2,10},{10... | collective-permute-start | bytes 98312 | tf_op jit(solution)/shard_map/ppermute | solution.py:551
  5.3 2.5 %collective-permute-start.1 = (f32[64,128]{1,0:T(8,128)S(1)}, f32[64,128]{1,0:T(8,128)S(1)}, u32[]{:S(2)}, u32[]{:S(2)}) collective-permute-start(f32[64,128]{1,0:T(8,128)S(1)} %get-tuple-element.46), channel_id=1, source_target_pairs={{0,24},{8,16},{16,8},{24,0},{1,25},{9,17},{17,9},{25,1},{2,26},{10... | collective-permute-start | bytes 98312 | tf_op jit(solution)/shard_map/ppermute | solution.py:551
  7.8 0.0 collective-permute-done.2.cross_ref
  7.8 2.0 %collective-permute-start.3 = (f32[32,128]{1,0:T(8,128)S(1)}, f32[32,128]{1,0:T(8,128)S(1)}, u32[]{:S(2)}, u32[]{:S(2)}) collective-permute-start(f32[32,128]{1,0:T(8,128)S(1)} %get-tuple-element.59), channel_id=1, source_target_pairs={{0,7},{1,6},{2,5},{3,4},{4,3},{5,2},{6,1},{7,0},{8,15},{9,14},{10,... | collective-permute-start | bytes 49160 | tf_op jit(solution)/shard_map/ppermute | solution.py:567
  9.8 0.8 %collective-permute-start.4 = (f32[32,128]{1,0:T(8,128)S(1)}, f32[32,128]{1,0:T(8,128)S(1)}, u32[]{:S(2)}, u32[]{:S(2)}) collective-permute-start(f32[32,128]{1,0:T(8,128)S(1)} %get-tuple-element.60), channel_id=1, source_target_pairs={{0,3},{1,2},{2,1},{3,0},{4,7},{5,6},{6,5},{7,4},{8,11},{9,10},{10,... | collective-permute-start | bytes 49160 | tf_op jit(solution)/shard_map/ppermute | solution.py:567
  10.6 0.1 collective-permute-start.5
  10.7 1.4 %local.1 = (f32[64,512]{1,0:T(8,128)S(1)}, f32[64,384]{1,0:T(8,128)S(1)}, bf16[384,384]{1,0:T(8,128)(2,1)S(1)}, bf16[256,192]{1,0:T(8,128)(2,1)S(1)}, bf16[128,1...) custom-call(f32[512,256]{1,0:T(8,128)} %nodal_hbm.3, ...), custom_call_target="tpu_custom_call" | custom-call | flops 1500000000 | bytes 6000000 | tf_op jit(solution)/shard_map/local/pallas_call | solution.py:625
  12.1 0.0 collective-permute-done.near_in_ref
  12.1 0.9 %collective-permute-done.4.refs_2_ = f32[32,128]{1,0:T(8,128)S(1)} collective-permute-done((f32[32,128]{1,0:T(8,128)S(1)}, f32[32,128]{1,0:T(8,128)S(1)}, u32[]{:S(2)}, u32[]{:S(2)}) %collective-permute-start.4) | collective-permute-done | bytes 16416 | tf_op jit(solution)/shard_map/ppermute | solution.py:567
  13.0 0.9 %collective-permute-done.5.refs_3_ = f32[32,128]{1,0:T(8,128)S(1)} collective-permute-done((f32[32,128]{1,0:T(8,128)S(1)}, f32[32,128]{1,0:T(8,128)S(1)}, u32[]{:S(2)}, u32[]{:S(2)}) %collective-permute-start.5) | collective-permute-done | bytes 16416 | tf_op jit(solution)/shard_map/ppermute | solution.py:567
  13.9 0.4 %answer.1 = (f32[72,128]{1,0:T(8,128)S(1)}, f32[72,128]{1,0:T(8,128)S(1)}, f32[64,128]{1,0:T(8,128)S(1)}, f32[64,128]{1,0:T(8,128)S(1)}, f32[64,384]{1,0:T(8,128)S(1)}, /*index=5*/f32[16,128]{1,0:T(8,128)S(1)}) custom-call(f32[64,128]{1,0:T(8,128)S(1)} %collective-permute-done.near_in_ref, f32[64,128]{1,0:T(8,128)S(1)} %collective-permute-done.1.far_in_ref, ...), custom_call_target="tpu_custom_call" | custom-call | tf_op jit(solution)/shard_map/answer/pallas_call | solution.py:645
  14.2 0.2 collective-permute-start.8
  14.4 0.7 %collective-permute-start.6 = (f32[72,128]{1,0:T(8,128)S(1)}, f32[72,128]{1,0:T(8,128)S(1)}, u32[]{:S(2)}, u32[]{:S(2)}) collective-permute-start(f32[72,128]{1,0:T(8,128)S(1)} %get-tuple-element.62), channel_id=1, source_target_pairs={{0,8},{8,0},{16,24},{24,16},{1,9},{9,1},{17,25},{25,17},{2,10},{10... | collective-permute-start | bytes 110600 | tf_op jit(solution)/shard_map/ppermute | solution.py:551
  15.1 0.8 %collective-permute-start.7 = (f32[72,128]{1,0:T(8,128)S(1)}, f32[72,128]{1,0:T(8,128)S(1)}, u32[]{:S(2)}, u32[]{:S(2)}) collective-permute-start(f32[72,128]{1,0:T(8,128)S(1)} %get-tuple-element.63), channel_id=1, source_target_pairs={{0,24},{8,16},{16,8},{24,0},{1,25},{9,17},{17,9},{25,1},{2,26},{10... | collective-permute-start | bytes 110600 | tf_op jit(solution)/shard_map/ppermute | solution.py:551
  15.9 0.0 collective-permute-done.8.cross_ref
  16.0 1.0 %collective-permute-start.9 = (f32[32,128]{1,0:T(8,128)S(1)}, f32[32,128]{1,0:T(8,128)S(1)}, u32[]{:S(2)}, u32[]{:S(2)}) collective-permute-start(f32[32,128]{1,0:T(8,128)S(1)} %get-tuple-element.82), channel_id=1, source_target_pairs={{0,7},{1,6},{2,5},{3,4},{4,3},{5,2},{6,1},{7,0},{8,15},{9,14},{10,... | collective-permute-start | bytes 49160 | tf_op jit(solution)/shard_map/ppermute | solution.py:567
  17.0 0.7 %collective-permute-start.10 = (f32[32,128]{1,0:T(8,128)S(1)}, f32[32,128]{1,0:T(8,128)S(1)}, u32[]{:S(2)}, u32[]{:S(2)}) collective-permute-start(f32[32,128]{1,0:T(8,128)S(1)} %get-tuple-element.83), channel_id=1, source_target_pairs={{0,3},{1,2},{2,1},{3,0},{4,7},{5,6},{6,5},{7,4},{8,11},{9,10},{10,... | collective-permute-start | bytes 49160 | tf_op jit(solution)/shard_map/ppermute | solution.py:567
  17.7 1.1 %collective-permute-start.11 = (f32[32,128]{1,0:T(8,128)S(1)}, f32[32,128]{1,0:T(8,128)S(1)}, u32[]{:S(2)}, u32[]{:S(2)}) collective-permute-start(f32[32,128]{1,0:T(8,128)S(1)} %get-tuple-element.84), channel_id=1, source_target_pairs={{0,5},{1,4},{2,7},{3,6},{4,1},{5,0},{6,3},{7,2},{8,13},{9,12},{10,... | collective-permute-start | bytes 49160 | tf_op jit(solution)/shard_map/ppermute | solution.py:567
  18.8 1.8 %gather.1 = (f32[2,512,128]{2,1,0:T(8,128)S(1)}, bf16[384,1536]{1,0:T(8,128)(2,1)S(1)}, bf16[128,2048]{1,0:T(8,128)(2,1)S(1)}, s32[8,256]{1,0:T(8,128)S(1)}) custom-call(f32[2,512,128]{2,1,0:T(8,128)S(1)} %get-tuple-element.66.nodal_ref, bf16[3,512,256]{2,1,0:T(8,128)(2,1)S(1)} %get-tuple-element.67.metric_ref, f32[64,512]{1,0:T(8,128)S(1)} %get-tuple-element.68.mortar_ref, ...), custom_call_target="tpu_custom_call" | custom-call | flops 1500000000 | bytes 6000000 | tf_op jit(solution)/shard_map/gather/pallas_call | solution.py:665
  20.6 0.3 %collective-permute-done.7.far_in_ref = f32[72,128]{1,0:T(8,128)S(1)} collective-permute-done((f32[72,128]{1,0:T(8,128)S(1)}, f32[72,128]{1,0:T(8,128)S(1)}, u32[]{:S(2)}, u32[]{:S(2)}) %collective-permute-start.7) | collective-permute-done | bytes 36896 | tf_op jit(solution)/shard_map/ppermute | solution.py:551
  20.9 0.0 collective-permute-done.11.refs_3_
  20.9 1.5 %final.1 = f32[512,256]{1,0:T(8,128)} custom-call(f32[72,128]{1,0:T(8,128)S(1)} %collective-permute-done.6.near_in_ref, f32[72,128]{1,0:T(8,128)S(1)} %collective-permute-done.7.far_in_ref, f32[8,384]{1,0:T(8,128)S(1)} %get-tuple-element.64.slot_level_ref, bf16[256,192]{1,0:T(8,128)(2,1)S(1)} %get-tuple-element.65.back_maps_ref.maps_ref, ...), custom_call_target="tpu_custom_call" | custom-call | tf_op jit(solution)/shard_map/final/pallas_call | solution.py:687
  (7 shorter events, 0.0 us)
Async XLA Ops:
  2.2 5.7 %collective-permute-start.2 = (f32[64,128]{1,0:T(8,128)S(1)}, f32[64,128]{1,0:T(8,128)S(1)}, u32[]{:S(2)}, u32[]{:S(2)}) collective-permute-start(f32[64,128]{1,0:T(8,128)S(1)} %get-tuple-element.57), channel_id=1, source_target_pairs={{0,1},{1,0},{2,3},{3,2},{4,5},{5,4},{6,7},{7,6},{8,9},{9,8},{10,11... | collective-permute-start | bytes 98312 | tf_op jit(solution)/shard_map/ppermute | solution.py:557
  2.7 9.4 %collective-permute-start = (f32[64,128]{1,0:T(8,128)S(1)}, f32[64,128]{1,0:T(8,128)S(1)}, u32[]{:S(2)}, u32[]{:S(2)}) collective-permute-start(f32[64,128]{1,0:T(8,128)S(1)} %get-tuple-element.45), channel_id=1, source_target_pairs={{0,8},{8,0},{16,24},{24,16},{1,9},{9,1},{17,25},{25,17},{2,10},{10... | collective-permute-start | bytes 98312 | tf_op jit(solution)/shard_map/ppermute | solution.py:551
  5.3 6.8 %collective-permute-start.1 = (f32[64,128]{1,0:T(8,128)S(1)}, f32[64,128]{1,0:T(8,128)S(1)}, u32[]{:S(2)}, u32[]{:S(2)}) collective-permute-start(f32[64,128]{1,0:T(8,128)S(1)} %get-tuple-element.46), channel_id=1, source_target_pairs={{0,24},{8,16},{16,8},{24,0},{1,25},{9,17},{17,9},{25,1},{2,26},{10... | collective-permute-start | bytes 98312 | tf_op jit(solution)/shard_map/ppermute | solution.py:551
  7.8 4.3 %collective-permute-start.3 = (f32[32,128]{1,0:T(8,128)S(1)}, f32[32,128]{1,0:T(8,128)S(1)}, u32[]{:S(2)}, u32[]{:S(2)}) collective-permute-start(f32[32,128]{1,0:T(8,128)S(1)} %get-tuple-element.59), channel_id=1, source_target_pairs={{0,7},{1,6},{2,5},{3,4},{4,3},{5,2},{6,1},{7,0},{8,15},{9,14},{10,... | collective-permute-start | bytes 49160 | tf_op jit(solution)/shard_map/ppermute | solution.py:567
  9.8 3.2 %collective-permute-start.4 = (f32[32,128]{1,0:T(8,128)S(1)}, f32[32,128]{1,0:T(8,128)S(1)}, u32[]{:S(2)}, u32[]{:S(2)}) collective-permute-start(f32[32,128]{1,0:T(8,128)S(1)} %get-tuple-element.60), channel_id=1, source_target_pairs={{0,3},{1,2},{2,1},{3,0},{4,7},{5,6},{6,5},{7,4},{8,11},{9,10},{10,... | collective-permute-start | bytes 49160 | tf_op jit(solution)/shard_map/ppermute | solution.py:567
  10.6 3.3 %collective-permute-start.5 = (f32[32,128]{1,0:T(8,128)S(1)}, f32[32,128]{1,0:T(8,128)S(1)}, u32[]{:S(2)}, u32[]{:S(2)}) collective-permute-start(f32[32,128]{1,0:T(8,128)S(1)} %get-tuple-element.61), channel_id=1, source_target_pairs={{0,5},{1,4},{2,7},{3,6},{4,1},{5,0},{6,3},{7,2},{8,13},{9,12},{10,... | collective-permute-start | bytes 49160 | tf_op jit(solution)/shard_map/ppermute | solution.py:567
  14.2 1.7 %collective-permute-start.8 = (f32[64,128]{1,0:T(8,128)S(1)}, f32[64,128]{1,0:T(8,128)S(1)}, u32[]{:S(2)}, u32[]{:S(2)}) collective-permute-start(f32[64,128]{1,0:T(8,128)S(1)} %get-tuple-element.80), channel_id=1, source_target_pairs={{0,1},{1,0},{2,3},{3,2},{4,5},{5,4},{6,7},{7,6},{8,9},{9,8},{10,11... | collective-permute-start | bytes 98312 | tf_op jit(solution)/shard_map/ppermute | solution.py:557
  14.4 6.2 %collective-permute-start.6 = (f32[72,128]{1,0:T(8,128)S(1)}, f32[72,128]{1,0:T(8,128)S(1)}, u32[]{:S(2)}, u32[]{:S(2)}) collective-permute-start(f32[72,128]{1,0:T(8,128)S(1)} %get-tuple-element.62), channel_id=1, source_target_pairs={{0,8},{8,0},{16,24},{24,16},{1,9},{9,1},{17,25},{25,17},{2,10},{10... | collective-permute-start | bytes 110600 | tf_op jit(solution)/shard_map/ppermute | solution.py:551
  15.1 5.8 %collective-permute-start.7 = (f32[72,128]{1,0:T(8,128)S(1)}, f32[72,128]{1,0:T(8,128)S(1)}, u32[]{:S(2)}, u32[]{:S(2)}) collective-permute-start(f32[72,128]{1,0:T(8,128)S(1)} %get-tuple-element.63), channel_id=1, source_target_pairs={{0,24},{8,16},{16,8},{24,0},{1,25},{9,17},{17,9},{25,1},{2,26},{10... | collective-permute-start | bytes 110600 | tf_op jit(solution)/shard_map/ppermute | solution.py:551
  16.0 4.9 %collective-permute-start.9 = (f32[32,128]{1,0:T(8,128)S(1)}, f32[32,128]{1,0:T(8,128)S(1)}, u32[]{:S(2)}, u32[]{:S(2)}) collective-permute-start(f32[32,128]{1,0:T(8,128)S(1)} %get-tuple-element.82), channel_id=1, source_target_pairs={{0,7},{1,6},{2,5},{3,4},{4,3},{5,2},{6,1},{7,0},{8,15},{9,14},{10,... | collective-permute-start | bytes 49160 | tf_op jit(solution)/shard_map/ppermute | solution.py:567
  17.0 3.9 %collective-permute-start.10 = (f32[32,128]{1,0:T(8,128)S(1)}, f32[32,128]{1,0:T(8,128)S(1)}, u32[]{:S(2)}, u32[]{:S(2)}) collective-permute-start(f32[32,128]{1,0:T(8,128)S(1)} %get-tuple-element.83), channel_id=1, source_target_pairs={{0,3},{1,2},{2,1},{3,0},{4,7},{5,6},{6,5},{7,4},{8,11},{9,10},{10,... | collective-permute-start | bytes 49160 | tf_op jit(solution)/shard_map/ppermute | solution.py:567
  17.7 3.2 %collective-permute-start.11 = (f32[32,128]{1,0:T(8,128)S(1)}, f32[32,128]{1,0:T(8,128)S(1)}, u32[]{:S(2)}, u32[]{:S(2)}) collective-permute-start(f32[32,128]{1,0:T(8,128)S(1)} %get-tuple-element.84), channel_id=1, source_target_pairs={{0,5},{1,4},{2,7},{3,6},{4,1},{5,0},{6,3},{7,2},{8,13},{9,12},{10,... | collective-permute-start | bytes 49160 | tf_op jit(solution)/shard_map/ppermute | solution.py:567
